TPU v7x, 32 devices: a whole 2x2x4 slice. The times are simulated.
32 devices in a mesh: blk: 8 (over y, x, core), tp: 4 (over z).
Axes of the slice: x: 2, y: 2, z: 4, core: 2. Of those that a mesh axis runs over, the one named last changes fastest.
Arguments:
- patches: float32 [2048, 768], P('blk'), may hold values from -6 to 6
- window_ids: int32 [2048], replicated, may hold values from 0 to 31, as said below
- lead_index: int32 [2048], P('blk'), may hold values from 0 to 15
- lead_table: bfloat16 [16, 768], replicated, may hold values from -4 to 4
- attention_gain: float32 [768], replicated, may hold values from 0.5 to 1.5
- attention_bias: float32 [768], replicated, may hold values from -2 to 2
- query_key_value: bfloat16 [3, 768, 768], P(None, None, 'tp'), may hold values from -0.21875 to 0.21875
- out_weight: bfloat16 [768, 768], P('tp'), may hold values from -1.25 to 1.25
- feedforward_gain: float32 [768], replicated, may hold values from 0.5 to 1.5
- feedforward_bias: float32 [768], replicated, may hold values from -2 to 2
- up_weight: bfloat16 [768, 3072], P(None, 'tp'), may hold values from -0.21875 to 0.21875
- down_weight: bfloat16 [3072, 768], P('tp'), may hold values from -0.109375 to 0.109375
- gate_head: bfloat16 [3, 16, 768], P(None, 'tp'), may hold values from -0.109375 to 0.109375
- pixel_mask: int32 [16, 2048], P('tp', 'blk'), may hold values from 0 to 1
- cotangent: float32 [2048, 768], P('blk'), may hold values from -6 to 6
Outputs:
- block_out: float32 [2048, 768], P('blk')
- penalty: float32 [], replicated
- grad_patches: float32 [2048, 768], P('blk')
- grad_lead_table: float32 [16, 768], replicated
- grad_attention_gain: float32 [768], replicated
- grad_attention_bias: float32 [768], replicated
- grad_query_key_value: float32 [3, 768, 768], P(None, None, 'tp')
- grad_out_weight: float32 [768, 768], P('tp')
- grad_feedforward_gain: float32 [768], replicated
- grad_feedforward_bias: float32 [768], replicated
- grad_up_weight: float32 [768, 3072], P(None, 'tp')
- grad_down_weight: float32 [3072, 768], P('tp')
- grad_gate_head: float32 [3, 16, 768], P(None, 'tp')
Inputs may be any that keep to these rules, and one draw needn't show every extreme that they name: `window_ids`: equal values mark the patches of one regional window; patch t lies in band t // 256; one window in every draw has patches in every band.
All inputs are finite; a program needn't handle non-finite values.
Results may differ from a plain program's by a relative error of at most 0.018.
Values may be sent and summed in bfloat16 or wider, within the bound.
A program may use at most 192 MiB of HBM per device.

v0:
```python
from functools import partial
import math

import jax
import jax.numpy as jnp
from jax import lax
from jax.sharding import PartitionSpec as P

HEAD_DIM = 64
PIX = 16


EPS = 1e-05
MASKED = -1e30


def norm_forward(values, gain_vector, bias_vector):
    row_mean = jnp.mean(values, axis=-1, keepdims=True)
    centered = values - row_mean
    inverse = lax.rsqrt(jnp.mean(centered * centered, axis=-1, keepdims=True) + EPS)
    unit_rows = centered * inverse
    return (unit_rows * gain_vector + bias_vector, unit_rows, inverse)


def norm_backward(incoming, unit_rows, inverse, gain_vector):
    scaled = incoming * gain_vector
    return inverse * (
        scaled
        - jnp.mean(scaled, axis=-1, keepdims=True)
        - unit_rows * jnp.mean(scaled * unit_rows, axis=-1, keepdims=True)
    )


def split_blocks(array_in, block_count, block_width):
    return array_in.reshape((block_count, block_width) + array_in.shape[1:])


def forward_fold(queries, query_ids, window_ids, score_scale):

    def absorb_keys(carried, pieces, offset):
        key_piece, value_piece = pieces
        piece_rows = key_piece.shape[0]
        block_width = math.gcd(piece_rows, 2048)
        block_count = piece_rows // block_width

        def absorb_block(state_now, blocks):
            highest, totals, running_sum = state_now
            key_part, value_part, id_part = blocks
            products = jnp.einsum(
                "qhd,khd->hqk", queries, key_part, preferred_element_type=jnp.float32
            )
            allowed = (query_ids[:, None] == id_part[None, :])[None]
            scores = jnp.where(allowed, products * score_scale, MASKED)
            new_high = jnp.maximum(highest, jnp.max(scores, axis=-1))
            weights = jnp.where(allowed, jnp.exp(scores - new_high[..., None]), 0.0)
            factor = jnp.exp(highest - new_high)
            totals = totals * factor + jnp.sum(weights, axis=-1)
            running_sum = running_sum * factor[..., None] + jnp.einsum(
                "hqk,khd->hqd",
                weights.astype(jnp.bfloat16),
                value_part,
                preferred_element_type=jnp.float32,
            )
            return ((new_high, totals, running_sum), None)

        result, unused = lax.scan(
            absorb_block,
            carried,
            (
                split_blocks(key_piece, block_count, block_width),
                split_blocks(value_piece, block_count, block_width),
                split_blocks(window_ids, block_count, block_width),
            ),
        )
        return result

    return absorb_keys


def score_grads(
    query_part,
    key_part,
    value_part,
    grad_part,
    query_id_part,
    key_id_part,
    total_part,
    delta_part,
    score_scale,
):
    products = jnp.einsum("qhd,khd->hqk", query_part, key_part, preferred_element_type=jnp.float32)
    allowed = (query_id_part[:, None] == key_id_part[None, :])[None]
    probabilities = jnp.where(allowed, jnp.exp(products * score_scale - total_part[..., None]), 0.0)
    value_dots = jnp.einsum(
        "qhd,khd->hqk", grad_part, value_part, preferred_element_type=jnp.float32
    )
    score_low = (probabilities * (value_dots - delta_part[..., None]) * score_scale).astype(
        jnp.bfloat16
    )
    return (probabilities.astype(jnp.bfloat16), score_low)


def local(
    patches,
    window_ids,
    lead_index,
    lead_table,
    attention_gain,
    attention_bias,
    query_key_value,
    out_weight,
    feedforward_gain,
    feedforward_bias,
    up_weight,
    down_weight,
    gate_head,
    pixel_mask,
    cotangent,
):
    local_tokens = patches.shape[0]
    local_width = out_weight.shape[0]
    local_heads = local_width // HEAD_DIM
    all_tokens = local_tokens * lax.axis_size("blk")
    score_scale = HEAD_DIM ** (-0.5)
    first_row = lax.axis_index("blk") * local_tokens
    query_ids = lax.dynamic_slice_in_dim(window_ids, first_row, local_tokens)
    selector = lead_index[:, None] == jnp.arange(lead_table.shape[0], dtype=jnp.int32)[None, :]
    lead_rows = jnp.dot(
        selector.astype(jnp.bfloat16), lead_table, preferred_element_type=jnp.float32
    )
    hidden = patches + lead_rows
    normed, unit_first, inverse_first = norm_forward(hidden, attention_gain, attention_bias)
    normed_low = normed.astype(jnp.bfloat16)
    projected = jnp.einsum(
        "td,cde->cte", normed_low, query_key_value, preferred_element_type=jnp.float32
    ).astype(jnp.bfloat16)
    head_shape = (local_tokens, local_heads, HEAD_DIM)
    queries = projected[0].reshape(head_shape)
    key_block = projected[1].reshape(head_shape)
    value_block = projected[2].reshape(head_shape)
    start_state = (
        jnp.full((local_heads, local_tokens), MASKED, jnp.float32),
        jnp.zeros((local_heads, local_tokens), jnp.float32),
        jnp.zeros((local_heads, local_tokens, HEAD_DIM), jnp.float32),
    )
    absorb = forward_fold(queries, query_ids, window_ids, score_scale)
    highest, totals, running_sum = absorb(
        start_state,
        (
            lax.all_gather(key_block, "blk", axis=0, tiled=True),
            lax.all_gather(value_block, "blk", axis=0, tiled=True),
        ),
        jnp.int32(0),
    )
    attended = running_sum / totals[..., None]
    log_totals = highest + jnp.log(totals)
    attended_low = (
        jnp.transpose(attended, (1, 0, 2)).reshape(local_tokens, local_width).astype(jnp.bfloat16)
    )
    branch = lax.psum(
        jnp.dot(attended_low, out_weight, preferred_element_type=jnp.float32).astype(jnp.bfloat16),
        "tp",
    ).astype(jnp.float32)
    middle = hidden + branch
    normed_two, unit_second, inverse_second = norm_forward(
        middle, feedforward_gain, feedforward_bias
    )
    normed_two_low = normed_two.astype(jnp.bfloat16)
    upward = jnp.dot(normed_two_low, up_weight, preferred_element_type=jnp.float32)
    activated, gelu_pull = jax.vjp(partial(jax.nn.gelu, approximate=False), upward)
    activated_low = activated.astype(jnp.bfloat16)
    feedforward = lax.psum(
        jnp.dot(activated_low, down_weight, preferred_element_type=jnp.float32).astype(
            jnp.bfloat16
        ),
        "tp",
    ).astype(jnp.float32)
    block_out = middle + feedforward
    block_low = block_out.astype(jnp.bfloat16)
    logits = jnp.einsum("epd,td->ept", gate_head, block_low, preferred_element_type=jnp.float32)
    log_probs = jax.nn.log_softmax(logits, axis=0)
    probabilities = jnp.exp(log_probs)
    entropy = -jnp.sum(probabilities * log_probs, axis=0)
    mask_float = pixel_mask.astype(jnp.float32)
    entropy_sum, pixel_count = lax.psum(
        (jnp.sum(mask_float * entropy), jnp.sum(mask_float)), ("blk", "tp")
    )
    penalty = entropy_sum / pixel_count
    pixels_all = all_tokens * PIX
    entropy_grad = mask_float * (pixels_all / pixel_count)
    logit_grad = (-probabilities * (log_probs + entropy[None]) * entropy_grad[None]).astype(
        jnp.bfloat16
    )
    gate_grad = jnp.einsum("ept,td->epd", logit_grad, block_low, preferred_element_type=jnp.float32)
    gater_term = jnp.einsum(
        "ept,epd->td", logit_grad, gate_head, preferred_element_type=jnp.float32
    )
    out_grad = cotangent + lax.psum(gater_term.astype(jnp.bfloat16), "tp").astype(jnp.float32)
    out_grad_low = out_grad.astype(jnp.bfloat16)
    down_grad = jnp.einsum(
        "tf,td->fd", activated_low, out_grad_low, preferred_element_type=jnp.float32
    )
    activated_grad = jnp.einsum(
        "td,fd->tf", out_grad_low, down_weight, preferred_element_type=jnp.float32
    )
    upward_grad = gelu_pull(activated_grad)[0].astype(jnp.bfloat16)
    up_grad = jnp.einsum(
        "td,tf->df", normed_two_low, upward_grad, preferred_element_type=jnp.float32
    )
    normed_two_term = jnp.einsum(
        "tf,df->td", upward_grad, up_weight, preferred_element_type=jnp.float32
    )
    normed_two_grad = lax.psum(normed_two_term.astype(jnp.bfloat16), "tp").astype(jnp.float32)
    second_gain_grad = jnp.sum(normed_two_grad * unit_second, axis=0)
    second_bias_grad = jnp.sum(normed_two_grad, axis=0)
    middle_grad = out_grad + norm_backward(
        normed_two_grad, unit_second, inverse_second, feedforward_gain
    )
    middle_low = middle_grad.astype(jnp.bfloat16)
    out_weight_grad = jnp.einsum(
        "te,td->ed", attended_low, middle_low, preferred_element_type=jnp.float32
    )
    attended_grad = jnp.einsum(
        "td,ed->te", middle_low, out_weight, preferred_element_type=jnp.float32
    )
    attended_grad_low = attended_grad.astype(jnp.bfloat16).reshape(head_shape)
    row_delta = jnp.sum(
        jnp.transpose(attended_grad_low.astype(jnp.float32), (1, 0, 2)) * attended, axis=-1
    )
    query_grad = jnp.zeros(head_shape, jnp.float32)
    key_piece = lax.all_gather(key_block, "blk", axis=0, tiled=True)
    value_piece = lax.all_gather(value_block, "blk", axis=0, tiled=True)
    piece_rows = key_piece.shape[0]
    block_width = math.gcd(piece_rows, 2048)
    block_count = piece_rows // block_width

    def visit_block(query_grad, blocks):
        key_part, value_part, id_part = blocks
        probs_low, score_low = score_grads(
            queries,
            key_part,
            value_part,
            attended_grad_low,
            query_ids,
            id_part,
            log_totals,
            row_delta,
            score_scale,
        )
        query_grad = query_grad + jnp.einsum(
            "hqk,khd->qhd", score_low, key_part, preferred_element_type=jnp.float32
        )
        key_grad = jnp.einsum(
            "hqk,qhd->khd", score_low, queries, preferred_element_type=jnp.float32
        )
        value_grad = jnp.einsum(
            "hqk,qhd->khd", probs_low, attended_grad_low, preferred_element_type=jnp.float32
        )
        return (query_grad, jnp.stack((key_grad, value_grad), axis=1))

    query_grad, block_grads = lax.scan(
        visit_block,
        query_grad,
        (
            split_blocks(key_piece, block_count, block_width),
            split_blocks(value_piece, block_count, block_width),
            split_blocks(window_ids, block_count, block_width),
        ),
    )
    block_grads = block_grads.reshape(piece_rows, 2, local_heads, HEAD_DIM)
    gathered_grads = block_grads
    query_grad, gathered_grads = (query_grad, gathered_grads)
    key_value_grad = lax.psum_scatter(gathered_grads, "blk", scatter_dimension=0, tiled=True)
    key_grad = key_value_grad[:, 0]
    value_grad = key_value_grad[:, 1]
    projected_grad = (
        jnp.stack((query_grad, key_grad, value_grad), axis=0)
        .reshape(3, local_tokens, local_width)
        .astype(jnp.bfloat16)
    )
    qkv_grad = jnp.einsum(
        "td,cte->cde", normed_low, projected_grad, preferred_element_type=jnp.float32
    )
    normed_term = jnp.einsum(
        "cte,cde->td", projected_grad, query_key_value, preferred_element_type=jnp.float32
    )
    normed_grad = lax.psum(normed_term.astype(jnp.bfloat16), "tp").astype(jnp.float32)
    first_gain_grad = jnp.sum(normed_grad * unit_first, axis=0)
    first_bias_grad = jnp.sum(normed_grad, axis=0)
    hidden_grad = middle_grad + norm_backward(
        normed_grad, unit_first, inverse_first, attention_gain
    )
    lead_grad_rows = jnp.dot(
        jnp.transpose(selector.astype(jnp.float32)), hidden_grad, precision=lax.Precision.HIGHEST
    )
    summed = lax.psum(
        (
            qkv_grad,
            out_weight_grad,
            up_grad,
            down_grad,
            gate_grad,
            first_gain_grad,
            first_bias_grad,
            second_gain_grad,
            second_bias_grad,
            lead_grad_rows,
        ),
        "blk",
    )
    return (
        block_out,
        penalty,
        hidden_grad,
        summed[9],
        summed[5],
        summed[6],
        summed[0],
        summed[1],
        summed[7],
        summed[8],
        summed[2],
        summed[3],
        summed[4],
    )


def solution(mesh):
    in_specs = (
        P("blk", None),
        P(),
        P("blk"),
        P(),
        P(),
        P(),
        P(None, None, "tp"),
        P("tp", None),
        P(),
        P(),
        P(None, "tp"),
        P("tp", None),
        P(None, "tp", None),
        P("tp", "blk"),
        P("blk", None),
    )
    out_specs = (
        P("blk", None),
        P(),
        P("blk", None),
        P(),
        P(),
        P(),
        P(None, None, "tp"),
        P("tp", None),
        P(),
        P(),
        P(None, "tp"),
        P("tp", None),
        P(None, "tp", None),
    )
    return jax.shard_map(local, mesh=mesh, in_specs=in_specs, out_specs=out_specs, check_vma=False)
```

profile of v0, /device:TPU:1, one launch (start us, length us, event | category | flops | bytes accessed | tf_op | source)
XLA Modules:
  0.0 559.5 jit_solution(1406694017892618199)
XLA Ops:
  8.1 1.1 broadcast_compare_fusion
  9.2 1.7 fusion.78
  11.2 1.7 fusion.71
  13.0 14.5 %all_gather.8 = bf16[2048,3,64]{0,2,1:T(8,128)(2,1)S(1)} all-gather(bf16[256,3,64]{0,2,1:T(8,128)(2,1)S(1)} %bitcast.106), channel_id=1, replica_groups=mesh['blk'=8,'tp'=4] {'blk'}, dimensions={0}, use_global_device_ids=true | all-gather | bytes 884736 | tf_op jit(solution)/shard_map/all_gather | solution.py:150
  27.5 1.5 select_reduce_fusion
  29.0 2.0 fusion.1
  31.6 12.3 %all_gather.9 = bf16[2048,3,64]{0,2,1:T(8,128)(2,1)S(1)} all-gather(bf16[256,3,64]{0,2,1:T(8,128)(2,1)S(1)} %bitcast.105), channel_id=1, replica_groups=mesh['blk'=8,'tp'=4] {'blk'}, dimensions={0}, use_global_device_ids=true | all-gather | bytes 884736 | tf_op jit(solution)/shard_map/all_gather | solution.py:151
  44.0 2.6 fusion.43
  48.3 35.5 %all-reduce.11.cloned.1.call-done = bf16[256,768]{1,0:T(8,128)(2,1)} async-done(((bf16[256,768]{1,0:T(8,128)(2,1)}), bf16[256,768]{1,0:T(8,128)(2,1)}) %all-reduce.11.cloned.1.call-update) | async-done | bytes 393232 | tf_op jit(solution)/shard_map/psum | solution.py:160
  83.8 1.2 fusion.75
  85.2 3.1 multiply_convert_fusion.1
  89.1 1.2 convolution_convert_fusion.1
  90.4 36.8 %all-reduce.13.cloned.1.call-done = bf16[256,768]{1,0:T(8,128)(2,1)} async-done(((bf16[256,768]{1,0:T(8,128)(2,1)}), bf16[256,768]{1,0:T(8,128)(2,1)}) %all-reduce.13.cloned.1.call-update) | async-done | bytes 393232 | tf_op jit(solution)/shard_map/psum | solution.py:172
  127.2 1.1 convert_add_fusion.1
  130.8 1.9 convert_reduce_fusion.2
  132.6 41.2 %all-reduce = (f32[]{:T(128)}, f32[]{:T(128)}) all-reduce(f32[]{:T(128)} %get-tuple-element.82, f32[]{:T(128)} %get-tuple-element.81), channel_id=1, replica_groups=mesh['blk'=8,'tp'=4] {'blk','tp'}, use_global_device_ids=true, to_apply=%region_12.13 | all-reduce | flops 2 | bytes 16 | tf_op jit(solution)/shard_map/psum | solution.py:185
  176.5 1.8 fusion.12
  178.6 35.7 %all-reduce.15.cloned.1.call-done = bf16[256,768]{1,0:T(8,128)(2,1)} async-done(((bf16[256,768]{1,0:T(8,128)(2,1)}), bf16[256,768]{1,0:T(8,128)(2,1)}) %all-reduce.15.cloned.1.call-update) | async-done | bytes 393232 | tf_op jit(solution)/shard_map/psum | solution.py:198
  214.3 2.5 add_convert_fusion
  217.5 1.3 convolution_convert_fusion
  218.9 36.8 %all-reduce.17.cloned.1.call-done = bf16[256,768]{1,0:T(8,128)(2,1)} async-done(((bf16[256,768]{1,0:T(8,128)(2,1)}), bf16[256,768]{1,0:T(8,128)(2,1)}) %all-reduce.17.cloned.1.call-update) | async-done | bytes 393232 | tf_op jit(solution)/shard_map/psum | solution.py:213
  255.7 2.0 fusion.29
  257.7 1.8 fusion.26
  259.5 1.3 convolution_convert_fusion.4
  260.9 4.5 fusion.9
  265.5 2.9 multiply_convert_fusion
  268.5 1.7 copy-done.2
  270.8 1.8 pad_maximum_fusion
  273.4 2.1 fusion.38
  275.5 3.3 fusion.65
  278.7 1.7 convolution_convert_fusion.3
  280.5 39.8 %reduce-scatter.2.cloned.1.call-done = f32[256,2,3,64]{0,3,2,1:T(8,128)} async-done(((f32[2048,2,3,64]{0,3,2,1:T(8,128)}), f32[256,2,3,64]{0,3,2,1:T(8,128)}) %reduce-scatter.2.cloned.1.call-update) | async-done | bytes 393232 | tf_op jit(solution)/shard_map/reduce_scatter | solution.py:273
  322.0 2.5 fusion.13
  324.6 3.1 fusion.72
  327.7 1.1 fusion.44
  328.8 31.4 %all-reduce.19.cloned.1.call-done = bf16[256,768]{1,0:T(8,128)(2,1)} async-done(((bf16[256,768]{1,0:T(8,128)(2,1)}), bf16[256,768]{1,0:T(8,128)(2,1)}) %all-reduce.19.cloned.1.call-update) | async-done | bytes 393232 | tf_op jit(solution)/shard_map/psum | solution.py:287
  360.2 2.0 fusion.30
  362.2 1.3 fusion.22
  363.5 1.7 fusion.49
  365.3 2.7 convolution_bitcast_fusion.1
  369.4 51.1 %all-reduce.21.cloned.1.call-done = (f32[16,768]{1,0:T(8,128)}, f32[768]{0:T(1024)}, f32[768]{0:T(1024)}, f32[768]{0:T(1024)}, f32[768]{0:T(1024)}, /*index=5*/f32[3,4,768]{2,1,0:T(4,128)}) async-done(((f32[16,768]{1,0:T(8,128)}, f32[768]{0:T(1024)}, f32[768]{0:T(1024)}, f32[768]{0:T(1024)}, f32[768]{0:T(1024)}, /*index=5*/f32[3,4,768]{2,1,0:T(4,128)}), (f32[16,768]{1,0:T(8,128)}, f32[768]{0:T(1024)}, ...) | async-done | bytes 98320 | tf_op jit(solution)/shard_map/psum | solution.py:296
  420.5 118.7 %all-reduce.23.cloned.1.call-done = (f32[3,768,192]{1,2,0:T(8,128)}, f32[192,768]{1,0:T(8,128)}, f32[768,768]{1,0:T(8,128)}, f32[768,768]{1,0:T(8,128)}) async-done(((f32[3,768,192]{1,2,0:T(8,128)}, f32[192,768]{1,0:T(8,128)}, f32[768,768]{1,0:T(8,128)}, f32[768,768]{1,0:T(8,128)}), (f32[3,768,192]{1,2,0:T(8,128)}, f32[192,768]{1,0:T(8,128)}, f32[768,768]{1,0:T(8,128)}, ...) | async-done | bytes 7077904 | tf_op jit(solution)/shard_map/psum | solution.py:296
  539.2 1.6 copy.43
  540.8 1.3 copy.44
  542.0 1.3 copy.45
  543.3 2.8 copy.46
  548.1 1.4 copy.50
  549.5 1.4 copy.51
  (148 shorter events, 16.1 us)
Async XLA Ops:
  7.2 78.0 %copy-start = (bf16[768,768]{1,0:T(8,128)(2,1)S(1)}, bf16[768,768]{1,0:T(8,128)(2,1)}, u32[]{:S(2)}) copy-start(bf16[768,768]{1,0:T(8,128)(2,1)} %param.25) | copy-start | bytes 3538948
  7.2 76.6 %all-reduce.11.cloned.1.call-start = ((), (), s32[]{:S(2)}) async-start(), calls=%async_computation.1 | async-start | bytes 786432 | tf_op jit(solution)/shard_map/psum | solution.py:160
  9.2 34.8 %copy-start.7 = (pred[256,2048]{1,0:T(8,128)(4,1)}, pred[256,2048]{1,0:T(8,128)(4,1)S(1)}, u32[]{:S(2)}) copy-start(pred[256,2048]{1,0:T(8,128)(4,1)S(1)} %broadcast_compare_fusion) | copy-start | bytes 1572868
  10.9 16.6 %copy-start.28 = (f32[256]{0:T(256)}, f32[256]{0:T(256)S(1)}, u32[]{:S(2)}) copy-start(f32[256]{0:T(256)S(1)} %broadcast_multiply_fusion.5) | copy-start | bytes 3076
  11.2 16.3 %copy-start.34 = (f32[256]{0:T(256)}, f32[256]{0:T(256)S(1)}, u32[]{:S(2)}) copy-start(f32[256]{0:T(256)S(1)} %add_rsqrt_fusion.1) | copy-start | bytes 3076
  13.0 16.0 %copy-start.17 = (bf16[1,256,192]{1,2,0:T(8,128)(2,1)}, bf16[1,256,192]{1,2,0:T(8,128)(2,1)S(1)}, u32[]{:S(2)}) copy-start(bf16[1,256,192]{1,2,0:T(8,128)(2,1)S(1)} %get-tuple-element.101) | copy-start | bytes 294916
  29.0 15.0 %copy-start.1 = (f32[3,256,2048]{2,1,0:T(8,128)}, f32[3,256,2048]{2,1,0:T(8,128)S(1)}, u32[]{:S(2)}) copy-start(f32[3,256,2048]{2,1,0:T(8,128)S(1)} %get-tuple-element.114) | copy-start | bytes 18874372
  43.9 2.6 copy-start.19
  44.0 3.2 copy-start.15
  46.5 38.7 %copy-start.30 = (f32[768]{0:T(1024)S(1)}, f32[768]{0:T(1024)}, u32[]{:S(2)}) copy-start(f32[768]{0:T(1024)} %param.23) | copy-start | bytes 9220
  46.5 38.7 %copy-start.45 = (f32[768]{0:T(1024)S(1)}, f32[768]{0:T(1024)}, u32[]{:S(2)}) copy-start(f32[768]{0:T(1024)} %param.24) | copy-start | bytes 9220
  48.3 78.9 %all-reduce.13.cloned.1.call-start = ((), (), s32[]{:S(2)}) async-start(), calls=%async_computation.2 | async-start | bytes 786432 | tf_op jit(solution)/shard_map/psum | solution.py:172
  84.9 3.4 copy-start.36
  85.2 3.1 copy-start.40
  85.2 3.8 copy-start.16
  89.1 125.2 %copy-start.10 = (f32[256,768]{1,0:T(8,128)S(1)}, f32[256,768]{1,0:T(8,128)}, u32[]{:S(2)}) copy-start(f32[256,768]{1,0:T(8,128)} %param.29) | copy-start | bytes 2359300
  90.3 124.0 %all-reduce.15.cloned.1.call-start = ((), (), s32[]{:S(2)}) async-start(), calls=%async_computation.3 | async-start | bytes 786432 | tf_op jit(solution)/shard_map/psum | solution.py:198
  178.4 77.3 %all-reduce.17.cloned.1.call-start = ((), (), s32[]{:S(2)}) async-start(), calls=%async_computation.4 | async-start | bytes 786432 | tf_op jit(solution)/shard_map/psum | solution.py:213
  214.3 41.4 %copy-start.31 = (f32[768]{0:T(1024)S(1)}, f32[768]{0:T(1024)}, u32[]{:S(2)}) copy-start(f32[768]{0:T(1024)} %param.23) | copy-start | bytes 9220
  214.3 41.4 %copy-start.37 = (f32[256]{0:T(256)S(1)}, f32[256]{0:T(256)}, u32[]{:S(2)}) copy-start(f32[256]{0:T(256)} %copy-done.36) | copy-start | bytes 3076
  214.3 41.4 %copy-start.41 = (f32[256]{0:T(256)S(1)}, f32[256]{0:T(256)}, u32[]{:S(2)}) copy-start(f32[256]{0:T(256)} %copy-done.40) | copy-start | bytes 3076
  218.8 42.0 %copy-start.48 = (f32[3,256]{1,0:T(4,128)S(1)}, f32[3,256]{1,0:T(4,128)}, u32[]{:S(2)}) copy-start(f32[3,256]{1,0:T(4,128)} %get-tuple-element.108) | copy-start | bytes 9220
  218.8 101.5 %reduce-scatter.2.cloned.1.call-start = ((), (), s32[]{:S(2)}) async-start(), calls=%async_computation.5 | async-start | bytes 3538944 | tf_op jit(solution)/shard_map/reduce_scatter | solution.py:273
  257.7 7.8 %slice-start = ((s8[6291456]{0:T(1024)(128)(4,1)}), s8[4194304]{0:T(1024)(128)(4,1)S(1)}, s32[]{:S(2)}) async-start(s8[6291456]{0:T(1024)(128)(4,1)} %bitcast.91), calls=%async_computation.9 | async-start | bytes 8388608
  260.8 4.6 copy-start.26
  260.8 4.6 copy-start.42
  260.8 4.6 copy-start.43
  260.8 4.7 slice-start.1
  260.8 4.7 copy-start.8
  260.8 4.7 copy-start.20
  265.5 4.7 copy-start.18
  268.5 1.7 copy-start.2
  272.7 87.5 %all-reduce.19.cloned.1.call-start = ((), (), s32[]{:S(2)}) async-start(), calls=%async_computation.6 | async-start | bytes 786432 | tf_op jit(solution)/shard_map/psum | solution.py:287
  273.4 5.4 copy-start.3
  273.4 5.4 copy-start.6
  324.5 35.7 %copy-start.27 = (f32[768]{0:T(1024)S(1)}, f32[768]{0:T(1024)}, u32[]{:S(2)}) copy-start(f32[768]{0:T(1024)} %param.19) | copy-start | bytes 9220
  324.5 35.7 %copy-start.29 = (f32[256]{0:T(256)S(1)}, f32[256]{0:T(256)}, u32[]{:S(2)}) copy-start(f32[256]{0:T(256)} %copy-done.28) | copy-start | bytes 3076
  324.5 35.7 %copy-start.35 = (f32[256]{0:T(256)S(1)}, f32[256]{0:T(256)}, u32[]{:S(2)}) copy-start(f32[256]{0:T(256)} %copy-done.34) | copy-start | bytes 3076
  324.5 96.0 %all-reduce.21.cloned.1.call-start = ((), (), s32[]{:S(2)}) async-start(), calls=%async_computation.7 | async-start | bytes 204800 | tf_op jit(solution)/shard_map/psum | solution.py:296
  324.6 3.1 copy-start.25
  327.7 37.6 %copy-start.44 = (f32[768]{0:T(1024)S(1)}, f32[768]{0:T(1024)}, u32[]{:S(2)}) copy-start(f32[768]{0:T(1024)} %param.20) | copy-start | bytes 9220
  363.5 4.6 copy-start.9
  365.3 173.9 %all-reduce.23.cloned.1.call-start = ((), (), s32[]{:S(2)}) async-start(), calls=%async_computation.8 | async-start | bytes 14155776 | tf_op jit(solution)/shard_map/psum | solution.py:296
  420.5 126.4 %copy-start.47 = (f32[768]{0:T(1024)S(1)}, f32[768]{0:T(1024)}, u32[]{:S(2)}) copy-start(f32[768]{0:T(1024)} %get-tuple-element.130) | copy-start | bytes 9220
  420.5 127.0 %copy-start.46 = (f32[768]{0:T(1024)S(1)}, f32[768]{0:T(1024)}, u32[]{:S(2)}) copy-start(f32[768]{0:T(1024)} %get-tuple-element.131) | copy-start | bytes 9220
  539.2 6.9 %copy-start.21 = (f32[192,768]{1,0:T(8,128)S(1)}, f32[192,768]{1,0:T(8,128)}, u32[]{:S(2)}) copy-start(f32[192,768]{1,0:T(8,128)} %get-tuple-element.129) | copy-start | bytes 1769476
  539.2 8.9 %copy-start.12 = (f32[768,768]{1,0:T(8,128)S(1)}, f32[768,768]{1,0:T(8,128)}, u32[]{:S(2)}) copy-start(f32[768,768]{1,0:T(8,128)} %get-tuple-element.132) | copy-start | bytes 7077892
  546.1 3.4 copy-start.11
  (11 other events, 9.1 us)
Sparse Core Ops, SparseCore 0:
  48.4 35.3 all-reduce.10
  90.5 36.6 all-reduce.12
  178.5 35.7 all-reduce.14
  218.9 36.6 all-reduce.16
  272.8 47.4 reduce-scatter.1
  324.7 35.4 all-reduce.18
  365.4 55.0 all-reduce.20
  425.8 113.3 all-reduce.22
where the time goes:
time: 561 us; the launch traced here: 560 us
  waiting for transfers between devices  386 us (69%)
  blocking collectives  68 us (12%)
  matrix products  46.9 us (8%)
  local copies, waits for them, and re-layouts  20.6 us (4%)
  other arithmetic  19.8 us (4%)
  between operations  17.9 us (3%)
    psum x2, waiting for transfers between devices, local(): lax.psum((qkv_grad, out_weight_grad, up_grad, down_grad, gate_grad, first...  170 us
    psum x1, blocking collectives, local(): lax.psum((jnp.sum(mask_float * entropy), jnp.sum(mask_float)), ('blk', 't...  41.2 us
    reduce_scatter x1, waiting for transfers between devices, local(): lax.psum_scatter(gathered_grads, 'blk', scatter_dimension=0, tiled=True)  39.8 us
    psum x1, waiting for transfers between devices, local(): lax.psum(normed_two_term.astype(jnp.bfloat16), 'tp').astype(jnp.float32)  36.8 us
    psum x1, waiting for transfers between devices, local(): lax.psum(jnp.dot(activated_low, down_weight, preferred_element_type=jnp.f...  36.8 us
    psum x1, waiting for transfers between devices, local(): lax.psum(gater_term.astype(jnp.bfloat16), 'tp').astype(jnp.float32)  35.7 us
    psum x1, waiting for transfers between devices, local(): lax.psum(jnp.dot(attended_low, out_weight, preferred_element_type=jnp.flo...  35.5 us
    psum x1, waiting for transfers between devices, local(): lax.psum(normed_term.astype(jnp.bfloat16), 'tp').astype(jnp.float32)  31.4 us
  transfers between devices with their start and end apart: 8, of which 8 were waited for; matrix products, arithmetic and copies ran while one was open for 3% of the time, Pallas kernels for 0%

commit v1 on v0

v1 whole, which is shorter than its diff:
```python
from functools import partial
from types import SimpleNamespace

import jax
import jax.numpy as jnp
from jax import lax
from jax.experimental import pallas as pl
from jax.experimental.pallas import tpu as pltpu
from jax.sharding import PartitionSpec as P

HEAD_DIM = 64
EPS = 1e-05
MASKED = -1e30
SCALE = HEAD_DIM ** (-0.5)
GROUP = 8
F32 = jnp.float32
BF16 = jnp.bfloat16
MESH = pl.DeviceIdType.MESH
VMEM_LIMIT = 61 * 2**20
INV_SQRT2 = 0.7071067811865476
INV_SQRT_2PI = 0.3989422804014327


def dot(a, b, ca, cb):
    return lax.dot_general(a, b, (((ca,), (cb,)), ((), ())), preferred_element_type=F32)


def mm_nn(a, b):
    return dot(a, b, 1, 0)


def mm_nt(a, b):
    return dot(a, b, 1, 1)


def mm_tn(a, b):
    return dot(a, b, 0, 0)


def norm_stats(values):
    mean = jnp.mean(values, axis=-1, keepdims=True)
    centered = values - mean
    inverse = lax.rsqrt(jnp.mean(centered * centered, axis=-1, keepdims=True) + EPS)
    return centered * inverse, inverse


def norm_backward(incoming, unit_rows, inverse, gain):
    scaled = incoming * gain
    return inverse * (
        scaled
        - jnp.mean(scaled, axis=-1, keepdims=True)
        - unit_rows * jnp.mean(scaled * unit_rows, axis=-1, keepdims=True)
    )


def total(x):
    return jnp.sum(jnp.sum(x, axis=0, keepdims=True), axis=1, keepdims=True)


def dims_of(nb, nt, tokens, width, local_width, hidden, leads, pixels):
    s = SimpleNamespace(nb=nb, nt=nt, L=tokens, D=width, W=local_width, F=hidden, leads=leads)
    s.H = local_width // HEAD_DIM
    s.S = tokens // nt
    s.half = nb // 2
    s.groups = nb // GROUP
    s.pixels = pixels
    s.sizes = (hidden + width, local_width * 4)
    s.bases = (0, s.sizes[0])
    s.rows = sum(s.sizes)
    s.tail = (leads + 4 + 15) // 16 * 16
    return s


def scratch_of(s):
    L, D, W, F, nb, nt, S = s.L, s.D, s.W, s.F, s.nb, s.nt, s.S
    v = pltpu.VMEM
    out = {
        "patches": v((L, D), F32),
        "qkv": v((3, D, W), BF16),
        "ow": v((nt, W, D), BF16),
        "up": v((D, F), BF16),
        "down": v((F, D), BF16),
        "cot": v((L, D), F32),
        "gate": v((nt * 32, D), BF16),
        "mask": v((nt, 8, L), F32),
        "cnt": v((nb, 8, 128), F32),
        "u1": v((L, D), F32),
        "r1": v((L, 1), F32),
        "normed": v((L, D), BF16),
        "kv": v((nb, 2 * W, L), BF16),
        "qd": v((nb, 2 * W, L), BF16),
        "st": v((nb, 8, L), F32),
        "m": v((8, L), F32),
        "l": v((8, L), F32),
        "acc": v((W, L), F32),
        "att": v((nt, W, L), BF16),
        "mid": v((L, D), F32),
        "u2": v((L, D), F32),
        "r2": v((L, 1), F32),
        "n2low": v((L, D), BF16),
        "upw": v((L, F), F32),
        "actlow": v((L, F), BF16),
        "ffp": v((L, D), BF16),
        "ffr": v((nt - 1, S, D), BF16),
        "blow": v((L, D), BF16),
        "oglow": v((L, D), BF16),
        "n2p": v((L, D), BF16),
        "n2r": v((nt - 1, S, D), BF16),
        "n2g": v((L, D), BF16),
        "mglow": v((L, D), BF16),
        "dq": v((W, L), F32),
        "dk": v((W, L), F32),
        "dv": v((W, L), F32),
        "dp": v((3, W, L), BF16),
        "ngp": v((L, D), BF16),
        "ngr": v((nt - 1, S, D), BF16),
        "ngg": v((L, D), BF16),
        "va": v((GROUP, 32, D), BF16),
        "vb": v((GROUP, s.tail, D), BF16),
        "ent": v((nb, 8, 128), F32),
        "va_sum": v((32, D), F32),
        "vb_sum": v((s.tail, D), F32),
        "gsrc": v((s.rows, D), BF16),
        "gout": v((s.rows, D), BF16),
    }
    dma = pltpu.SemaphoreType.DMA
    out["loads"] = dma((8,))
    for name in ("zmask", "zgate", "zow", "zowr", "zatt", "zff", "zblk", "zn2", "zn2g", "zng", "zngg"):
        out[name + "_s"] = dma((nt - 1,))
        out[name + "_r"] = dma((nt - 1,))
    for name in ("kv", "q", "da", "st"):
        for part in ("_s", "_r", "_rs", "_rr"):
            out[name + part] = dma((s.half,))
    for name, count in (("cnt", nb), ("ent", nb), ("va", GROUP), ("vb", GROUP)):
        out[name + "_s"] = dma((count - 1,))
        out[name + "_r"] = dma((count - 1,))
    if s.groups > 1:
        for name, rows in (("va2", 32), ("vb2", s.tail)):
            out[name] = v((s.groups, rows, D), BF16)
            out[name + "_s"] = dma((s.groups - 1,))
            out[name + "_r"] = dma((s.groups - 1,))
    for i, rows in enumerate(s.sizes):
        hr = rows // 2
        qr = hr // 4
        out["core%d" % i] = v((hr, D), BF16)
        out["quart%d" % i] = v((3, qr, D), BF16)
        if s.groups > 1:
            out["sup%d" % i] = v((s.groups, qr, D), BF16)
            out["sup%d_s" % i] = dma((s.groups - 1,))
            out["sup%d_r" % i] = dma((s.groups - 1,))
        for part in ("c1", "c2"):
            out["%s%d_s" % (part, i)] = dma((1,))
            out["%s%d_r" % (part, i)] = dma((1,))
        for part in ("rs", "ag"):
            out["%s%d_s" % (part, i)] = dma((3,))
            out["%s%d_r" % (part, i)] = dma((3,))
    return out


def main_kernel(s, names, *refs):
    (
        patches,
        windows,
        leads_in,
        table,
        gain1,
        bias1,
        qkv,
        out_weight,
        gain2,
        bias2,
        up,
        down,
        gate,
        pixel_mask,
        cotangent,
        o_block,
        o_hidden,
        o_grads,
        o_va,
        o_vb,
    ) = refs[:20]
    k = SimpleNamespace(**dict(zip(names, refs[20:])))
    sem = vars(k)
    L, D, W, F, H, S, nb, nt = s.L, s.D, s.W, s.F, s.H, s.S, s.nb, s.nt
    b = lax.axis_index("blk")
    t = lax.axis_index("tp")
    core = lax.rem(b, 2)
    pair = b // 2
    sib = b + 1 - 2 * core
    mine = pl.ds(pl.multiple_of(t * S, S), S)

    def z_peer(j):
        return lax.rem(t + j, nt)

    def remote(src, dst, send, recv, device):
        return pltpu.make_async_remote_copy(
            src, dst, send, recv, device_id=device, device_id_type=MESH
        )

    def z_copy(name, j, src, dst):
        return remote(src, dst, sem[name + "_s"].at[j - 1], sem[name + "_r"].at[j - 1], (b, z_peer(j)))

    def z_from(j):
        return lax.rem(t + nt - j, nt)

    def rows_of(tt):
        return pl.ds(pl.multiple_of(tt * S, S), S)

    def ag_copy(name, at, i, dst_band):
        return remote(at(b), at(b), sem[name + "_s"].at[i], sem[name + "_r"].at[i], (dst_band, t))

    def relay_copy(name, at, i, band):
        return remote(at(band), at(band), sem[name + "_rs"].at[i], sem[name + "_rr"].at[i], (sib, t))

    def band_same(i):
        return lax.rem(b + nb - 2 * i, nb)

    def band_sib(i):
        return lax.rem(sib + nb - 2 * i, nb)

    def ag_start(name, at):
        @pl.loop(1, s.half)
        def _(i):
            ag_copy(name, at, i, lax.rem(b + 2 * i, nb)).start()

        relay_copy(name, at, 0, b).start()

    def ag_relay(name, at, i):
        band = band_same(i)
        remote(at(band), at(band), sem[name + "_s"].at[i], sem[name + "_r"].at[i], (sib, t)).wait_recv()
        relay_copy(name, at, i, band).start()

    def ag_wait_relay(name, at, i):
        relay_copy(name, at, i, band_sib(i)).wait_recv()

    def ag_finish(name, at):
        @pl.loop(1, s.half)
        def _(i):
            ag_copy(name, at, i, sib).wait_send()

        @pl.loop(0, s.half)
        def _(i):
            relay_copy(name, at, i, b).wait_send()

    every = (nb, b, lambda i: i)
    near = (GROUP, lax.rem(b, GROUP), lambda i: b // GROUP * GROUP + i)
    far = (s.groups, b // GROUP, lambda i: i * GROUP + lax.rem(b, GROUP))

    def swap_copy(name, members, i, slot, to):
        ref = sem[name]
        return remote(
            ref.at[slot],
            ref.at[slot],
            sem[name + "_s"].at[i - 1],
            sem[name + "_r"].at[i - 1],
            (members[2](to), t),
        )

    def swap_start(name, members):
        count, me, _ = members

        @pl.loop(1, count)
        def _(i):
            swap_copy(name, members, i, me, lax.rem(me + i, count)).start()

    def swap_wait(name, members):
        count, me, _ = members

        @pl.loop(1, count)
        def _(i):
            peer = lax.rem(me + count - i, count)
            swap_copy(name, members, i, peer, peer).wait_recv()

    def swap_finish(name, members):
        count, me, _ = members

        @pl.loop(1, count)
        def _(i):
            swap_copy(name, members, i, me, lax.rem(me + i, count)).wait_send()

    def swap_sum(name):
        swap_wait(name, near)
        out = slots_sum(sem[name], GROUP)
        if s.groups > 1:
            sem[name + "2"][far[1]] = out.astype(BF16)
            swap_start(name + "2", far)
            swap_wait(name + "2", far)
            out = slots_sum(sem[name + "2"], s.groups)
            swap_finish(name + "2", far)
        swap_finish(name, near)
        return out

    def slots_sum(ref, count):
        return lax.fori_loop(
            1, count, lambda i, acc: acc + ref[i].astype(F32), ref[0].astype(F32)
        )

    def rs_start(name, part, recv):
        for j in range(1, nt):
            z_copy(name, j, part.at[rows_of(z_peer(j))], recv.at[j - 1]).start()

    def rs_sum(name, part, recv):
        acc = part[mine, :].astype(F32)
        for j in range(1, nt):
            z_copy(name, j, part.at[rows_of(z_from(j))], recv.at[j - 1]).wait_recv()
            acc = acc + recv[j - 1].astype(F32)
        return acc

    def rs_finish(name, part, recv):
        for j in range(1, nt):
            z_copy(name, j, part.at[rows_of(z_peer(j))], recv.at[j - 1]).wait_send()

    def gather_start(name, ref):
        for j in range(1, nt):
            z_copy(name, j, ref.at[mine], ref.at[mine]).start()

    def gather_wait(name, ref):
        for j in range(1, nt):
            rows = rows_of(z_from(j))
            z_copy(name, j, ref.at[rows], ref.at[rows]).wait_recv()

    def gather_finish(name, ref):
        for j in range(1, nt):
            z_copy(name, j, ref.at[mine], ref.at[mine]).wait_send()

    quarter = lax.rem(pair, 4)
    first_pair = pair - quarter
    group = pair // 4

    def g_rows(i, half, q):
        hr = s.sizes[i] // 2
        qr = hr // 4
        return pl.ds(pl.multiple_of(s.bases[i] + half * hr + q * qr, 16), qr)

    def g_half(i, half):
        hr = s.sizes[i] // 2
        return pl.ds(pl.multiple_of(s.bases[i] + half * hr, 16), hr)

    def q_peer(j):
        return lax.rem(quarter + j, 4)

    def q_dev(j):
        return ((first_pair + q_peer(j)) * 2 + core, t)

    def c1_copy(i):
        return remote(
            k.gsrc.at[g_half(i, 1 - core)], sem["core%d" % i], sem["c1%d_s" % i].at[0], sem["c1%d_r" % i].at[0], (sib, t)
        )

    def rs_copy(i, j):
        qr = s.sizes[i] // 8
        src = sem["core%d" % i].at[pl.ds(pl.multiple_of(q_peer(j) * qr, 16), qr)]
        return remote(
            src, sem["quart%d" % i].at[j - 1], sem["rs%d_s" % i].at[j - 1], sem["rs%d_r" % i].at[j - 1], q_dev(j)
        )

    def ag_copy_g(i, j, q):
        rows = g_rows(i, core, q)
        return remote(
            k.gout.at[rows], k.gout.at[rows], sem["ag%d_s" % i].at[j - 1], sem["ag%d_r" % i].at[j - 1], q_dev(j)
        )

    def c2_copy(i, half):
        rows = g_half(i, half)
        return remote(
            k.gout.at[rows], k.gout.at[rows], sem["c2%d_s" % i].at[0], sem["c2%d_r" % i].at[0], (sib, t)
        )

    def sup_copy(i, j):
        ref = sem["sup%d" % i]
        dev = ((lax.rem(group + j, s.groups) * 4 + quarter) * 2 + core, t)
        return remote(ref.at[group], ref.at[group], sem["sup%d_s" % i].at[j - 1], sem["sup%d_r" % i].at[j - 1], dev)

    def grads_step1(i):
        c1_copy(i).start()

    def grads_step2(i):
        c1_copy(i).wait()
        hs = sem["core%d" % i]
        hs[...] = (k.gsrc[g_half(i, core), :].astype(F32) + hs[...].astype(F32)).astype(BF16)
        for j in range(1, 4):
            rs_copy(i, j).start()

    def grads_step3(i):
        qr = s.sizes[i] // 8
        acc = sem["core%d" % i][pl.ds(pl.multiple_of(quarter * qr, 16), qr), :].astype(F32)
        for j in range(1, 4):
            rs_copy(i, j).wait()
            acc = acc + sem["quart%d" % i][j - 1].astype(F32)
        if s.groups > 1:
            ref = sem["sup%d" % i]
            ref[group] = acc.astype(BF16)
            for j in range(1, s.groups):
                sup_copy(i, j).start()
            for j in range(1, s.groups):
                sup_copy(i, j).wait()
            acc = ref[0].astype(F32)
            for g in range(1, s.groups):
                acc = acc + ref[g].astype(F32)
        k.gout[g_rows(i, core, quarter), :] = acc.astype(BF16)
        for j in range(1, 4):
            ag_copy_g(i, j, quarter).start()

    def grads_step4(i):
        for j in range(1, 4):
            ag_copy_g(i, j, quarter).wait_send()
            ag_copy_g(i, j, lax.rem(quarter + 4 - j, 4)).wait_recv()
        c2_copy(i, core).start()

    def grads_step5(i):
        c2_copy(i, core).wait_send()
        c2_copy(i, 1 - core).wait_recv()

    loads = [
        pltpu.make_async_copy(patches, k.patches, k.loads.at[0]),
        pltpu.make_async_copy(qkv, k.qkv, k.loads.at[1]),
        pltpu.make_async_copy(out_weight, k.ow.at[t], k.loads.at[2]),
        pltpu.make_async_copy(up, k.up, k.loads.at[3]),
        pltpu.make_async_copy(down, k.down, k.loads.at[4]),
        pltpu.make_async_copy(cotangent, k.cot, k.loads.at[5]),
    ]
    for copy in loads:
        copy.start()
    barrier = pltpu.get_barrier_semaphore()

    @pl.loop(1, nb)
    def _(i):
        pl.semaphore_signal(barrier, inc=1, device_id=(lax.rem(b + i, nb), t), device_id_type=MESH)

    for j in range(1, nt):
        pl.semaphore_signal(barrier, inc=1, device_id=(b, z_peer(j)), device_id_type=MESH)

    lead_hot = (lax.broadcasted_iota(jnp.int32, (s.leads, L), 0) == leads_in[...]).astype(F32)
    loads[0].wait()
    hidden = k.patches[...] + mm_tn(lead_hot.astype(BF16), table[...])
    unit1, inverse1 = norm_stats(hidden)
    k.u1[...] = unit1
    k.r1[...] = inverse1
    k.mid[...] = hidden
    k.normed[...] = (unit1 * gain1[...] + bias1[...]).astype(BF16)
    loads[1].wait()

    def project(c):
        return jnp.transpose(mm_nn(k.normed[...], k.qkv[c]))

    k.kv[b, 0:W, :] = project(1).astype(BF16)
    k.kv[b, W : 2 * W, :] = project(2).astype(BF16)
    gate_pad = jnp.zeros((4, D), F32)
    gate_rows = []
    for e in range(3):
        gate_rows += [gate[e].astype(F32), gate_pad]
    gate_rows += [gate_pad, gate_pad]
    my_gate = pl.ds(pl.multiple_of(t * 32, 32), 32)
    k.gate[my_gate, :] = jnp.concatenate(gate_rows, axis=0).astype(BF16)
    k.mask[t] = jnp.concatenate([pixel_mask[...].astype(F32), jnp.zeros((4, L), F32)], axis=0)
    pl.semaphore_wait(barrier, nb - 1 + nt - 1)

    def kv_at(band):
        return k.kv.at[band]

    ag_start("kv", kv_at)
    for j in range(1, nt):
        z_copy("zmask", j, k.mask.at[t], k.mask.at[t]).start()
        z_copy("zgate", j, k.gate.at[my_gate], k.gate.at[my_gate]).start()
    hw = W // 2
    loads[2].wait()

    def ow_half(tt, c):
        return k.ow.at[tt, pl.ds(pl.multiple_of(c * hw, hw), hw)]

    for j in range(1, nt):
        z_copy("zow", j, ow_half(t, core), ow_half(t, core)).start()
    k.qd[b, 0:W, :] = (project(0).astype(BF16).astype(F32) * SCALE).astype(BF16)

    for j in range(1, nt):
        z_copy("zmask", j, k.mask.at[t], k.mask.at[z_from(j)]).wait_recv()
    k.cnt[b] = jnp.broadcast_to(total(jnp.sum(k.mask[...], axis=0)), (8, 128))
    swap_start("cnt", every)

    def id_row(band):
        return windows[pl.ds(band, 1), :].astype(F32)

    def id_column(band):
        return jnp.transpose(jnp.broadcast_to(id_row(band), (128, L)))[:, 0:1]

    def head(h):
        return pl.ds(h * HEAD_DIM, HEAD_DIM)

    def value_head(h):
        return pl.ds(W + h * HEAD_DIM, HEAD_DIM)

    k.m[...] = jnp.full((8, L), MASKED, F32)
    k.l[...] = jnp.zeros((8, L), F32)
    k.acc[...] = jnp.zeros((W, L), F32)

    def forward_band(band):
        allowed = id_column(band) == id_row(b)
        for h in range(H):
            scores = mm_tn(k.kv[band, head(h), :], k.qd[b, head(h), :])
            scores = jnp.where(allowed, scores, MASKED)
            high = k.m[h : h + 1, :]
            new_high = jnp.maximum(high, jnp.max(scores, axis=0, keepdims=True))
            weights = jnp.exp(scores - new_high)
            factor = jnp.exp(high - new_high)
            k.m[h : h + 1, :] = new_high
            k.l[h : h + 1, :] = k.l[h : h + 1, :] * factor + jnp.sum(weights, axis=0, keepdims=True)
            k.acc[head(h), :] = k.acc[head(h), :] * factor + mm_nn(
                k.kv[band, value_head(h), :], weights.astype(BF16)
            )

    @pl.loop(0, s.half)
    def _(i):
        @pl.when(i > 0)
        def _():
            ag_relay("kv", kv_at, i)

        forward_band(band_same(i))
        ag_wait_relay("kv", kv_at, i)
        forward_band(band_sib(i))

    for h in range(H):
        att = k.acc[head(h), :] / k.l[h : h + 1, :]
        k.acc[head(h), :] = att
        k.att[t, head(h), :] = att.astype(BF16)
        k.st[b, h : h + 1, :] = k.m[h : h + 1, :] + jnp.log(k.l[h : h + 1, :])
    for j in range(1, nt):
        z_copy("zatt", j, k.att.at[t], k.att.at[t]).start()

    def q_at(band):
        return k.qd.at[band, pl.ds(0, W)]

    def da_at(band):
        return k.qd.at[band, pl.ds(W, W)]

    def st_at(band):
        return k.st.at[band]

    ag_start("q", q_at)
    for j in range(1, nt):
        src = z_from(j)
        z_copy("zow", j, ow_half(src, core), ow_half(src, core)).wait_recv()
        remote(
            ow_half(src, core), ow_half(src, core), k.zowr_s.at[j - 1], k.zowr_r.at[j - 1], (sib, t)
        ).start()
    for j in range(1, nt):
        src = z_from(j)
        remote(
            ow_half(src, 1 - core), ow_half(src, 1 - core), k.zowr_s.at[j - 1], k.zowr_r.at[j - 1], (sib, t)
        ).wait_recv()
    for j in range(1, nt):
        z_copy("zatt", j, k.att.at[t], k.att.at[z_from(j)]).wait_recv()
        z_copy("zgate", j, k.gate.at[my_gate], k.gate.at[my_gate]).wait_recv()

    middle = k.mid[...] + mm_tn(
        k.att[...].reshape(nt * W, L), k.ow[...].reshape(nt * W, D)
    )
    k.mid[...] = middle
    unit2, inverse2 = norm_stats(middle)
    k.u2[...] = unit2
    k.r2[...] = inverse2
    k.n2low[...] = (unit2 * gain2[...] + bias2[...]).astype(BF16)
    loads[3].wait()
    loads[4].wait()
    upward = mm_nn(k.n2low[...], k.up[...])
    k.upw[...] = upward
    k.actlow[...] = (0.5 * upward * (1.0 + lax.erf(upward * INV_SQRT2))).astype(BF16)
    k.ffp[...] = mm_nn(k.actlow[...], k.down[...]).astype(BF16)
    rs_start("zff", k.ffp, k.ffr)
    upward = k.upw[...]
    k.upw[...] = 0.5 * (1.0 + lax.erf(upward * INV_SQRT2)) + upward * (
        jnp.exp(-0.5 * upward * upward) * INV_SQRT_2PI
    )

    @pl.loop(1, s.half)
    def _(i):
        ag_relay("q", q_at, i)

    swap_wait("cnt", every)
    block_slice = k.mid[mine, :] + rs_sum("zff", k.ffp, k.ffr)
    k.blow[mine, :] = block_slice.astype(BF16)
    gather_start("zblk", k.blow)
    loads[5].wait()
    pixel_count = jnp.sum(k.cnt[...], axis=0)[0:1, 0:1]
    gather_wait("zblk", k.blow)

    block_copy = pltpu.make_async_copy(k.blow, o_block, k.loads.at[6])
    block_copy.start()
    logits = mm_nt(k.gate[...], k.blow[...]).reshape(nt, 4, 8, L)
    parts = [logits[:, e] for e in range(3)]
    high = jnp.maximum(jnp.maximum(parts[0], parts[1]), parts[2])
    logs = jnp.log(sum(jnp.exp(x - high) for x in parts))
    log_probs = [x - high - logs for x in parts]
    probs = [jnp.exp(x) for x in log_probs]
    entropy = -sum(p * x for p, x in zip(probs, log_probs))
    mask = k.mask[...]
    entropy_sum = total(jnp.sum(mask * entropy, axis=0))
    weight = mask * (float(s.pixels) / pixel_count)[None]
    grads = [-p * (x + entropy) * weight for p, x in zip(probs, log_probs)]
    grads.append(jnp.zeros((nt, 8, L), F32))
    logit_grad = jnp.stack(grads, axis=1).reshape(nt * 32, L).astype(BF16)
    out_grad = k.cot[...] + mm_tn(logit_grad, k.gate[...])
    k.cot[...] = out_grad
    k.oglow[...] = out_grad.astype(BF16)

    upward_grad = (mm_nt(k.oglow[...], k.down[...]) * k.upw[...]).astype(BF16)
    k.n2p[...] = mm_nt(upward_grad, k.up[...]).astype(BF16)
    rs_start("zn2", k.n2p, k.n2r)
    k.gsrc[0:F, :] = mm_tn(k.actlow[...], k.oglow[...]).astype(BF16)
    k.gsrc[F : F + D, :] = mm_tn(k.n2low[...], upward_grad).astype(BF16)
    grads_step1(0)
    lg_rows = jnp.stack(grads, axis=1).reshape(nt, 32, L)
    pick = lax.broadcasted_iota(jnp.int32, (nt, 1, 1), 0) == t
    own_lg = jnp.sum(jnp.where(pick, lg_rows, 0.0), axis=0).astype(BF16)
    k.va[near[1]] = mm_nn(own_lg, k.blow[...]).astype(BF16)
    k.ent[b] = jnp.broadcast_to(entropy_sum / pixel_count, (8, 128))
    swap_start("va", near)
    swap_start("ent", every)
    grads_step2(0)
    k.n2g[mine, :] = rs_sum("zn2", k.n2p, k.n2r).astype(BF16)
    gather_start("zn2g", k.n2g)
    gather_wait("zn2g", k.n2g)
    n2_grad = k.n2g[...].astype(F32)
    gain2_grad = jnp.sum(n2_grad * k.u2[...], axis=0, keepdims=True)
    bias2_grad = jnp.sum(n2_grad, axis=0, keepdims=True)
    middle_grad = k.cot[...] + norm_backward(n2_grad, k.u2[...], k.r2[...], gain2[...])
    k.cot[...] = middle_grad
    k.mglow[...] = middle_grad.astype(BF16)

    att_grad = mm_nt(k.ow[t], k.mglow[...]).astype(BF16)
    k.qd[b, W : 2 * W, :] = att_grad
    weighted = att_grad.astype(F32) * k.acc[...]
    for h in range(H):
        k.st[b, H + h : H + h + 1, :] = jnp.sum(
            weighted[h * HEAD_DIM : (h + 1) * HEAD_DIM], axis=0, keepdims=True
        )
    ag_start("st", st_at)
    ag_start("da", da_at)
    k.gsrc[s.bases[1] : s.bases[1] + W, :] = mm_nn(k.att[t], k.mglow[...]).astype(BF16)
    k.dq[...] = jnp.zeros((W, L), F32)
    k.dk[...] = jnp.zeros((W, L), F32)
    k.dv[...] = jnp.zeros((W, L), F32)

    @pl.loop(0, nb)
    def _(band):
        allowed = id_column(band) == id_row(b)
        for h in range(H):
            keys = k.kv[band, head(h), :]
            scores = jnp.where(allowed, mm_tn(keys, k.qd[b, head(h), :]), MASKED)
            prob = jnp.exp(scores - k.st[b, h : h + 1, :])
            dots = mm_tn(k.kv[band, value_head(h), :], k.qd[b, value_head(h), :])
            grad = (prob * (dots - k.st[b, H + h : H + h + 1, :])).astype(BF16)
            k.dq[head(h), :] += mm_nn(keys, grad)

    @pl.loop(1, s.half)
    def _(i):
        ag_wait_relay("q", q_at, i)

    ag_wait_relay("q", q_at, 0)
    my_column = id_column(b)

    def backward_band(band):
        allowed = my_column == id_row(band)
        for h in range(H):
            queries = k.qd[band, head(h), :]
            att_grads = k.qd[band, value_head(h), :]
            scores = jnp.where(allowed, mm_tn(k.kv[b, head(h), :], queries), MASKED)
            prob = jnp.exp(scores - k.st[band, h : h + 1, :])
            dots = mm_tn(k.kv[b, value_head(h), :], att_grads)
            grad = (prob * (dots - k.st[band, H + h : H + h + 1, :])).astype(BF16)
            k.dk[head(h), :] += mm_nt(queries, grad)
            k.dv[head(h), :] += mm_nt(att_grads, prob.astype(BF16))

    @pl.loop(0, s.half)
    def _(i):
        @pl.when(i > 0)
        def _():
            ag_relay("st", st_at, i)
            ag_relay("da", da_at, i)

        backward_band(band_same(i))
        ag_wait_relay("st", st_at, i)
        ag_wait_relay("da", da_at, i)
        backward_band(band_sib(i))

    grads_step3(0)
    k.dp[0] = (k.dq[...] * SCALE).astype(BF16)
    k.dp[1] = k.dk[...].astype(BF16)
    k.dp[2] = k.dv[...].astype(BF16)
    n1_part = mm_nt(jnp.transpose(k.dp[0].astype(F32)).astype(BF16), k.qkv[0])
    n1_part += mm_nt(jnp.transpose(k.dp[1].astype(F32)).astype(BF16), k.qkv[1])
    n1_part += mm_nt(jnp.transpose(k.dp[2].astype(F32)).astype(BF16), k.qkv[2])
    k.ngp[...] = n1_part.astype(BF16)
    rs_start("zng", k.ngp, k.ngr)
    base = s.bases[1] + W
    k.gsrc[base : base + 3 * W, :] = mm_nn(k.dp[...].reshape(3 * W, L), k.normed[...]).astype(BF16)
    grads_step1(1)
    grads_step2(1)
    k.ngg[mine, :] = rs_sum("zng", k.ngp, k.ngr).astype(BF16)
    gather_start("zngg", k.ngg)
    grads_step4(0)
    grads_step3(1)
    grads_step5(0)
    gather_wait("zngg", k.ngg)
    n1_grad = k.ngg[...].astype(F32)
    unit1 = k.u1[...]
    gain1_grad = jnp.sum(n1_grad * unit1, axis=0, keepdims=True)
    bias1_grad = jnp.sum(n1_grad, axis=0, keepdims=True)
    hidden_grad = k.cot[...] + norm_backward(n1_grad, unit1, k.r1[...], gain1[...])
    k.patches[...] = hidden_grad
    hidden_copy = pltpu.make_async_copy(k.patches, o_hidden, k.loads.at[7])
    hidden_copy.start()
    hot = lead_hot.astype(BF16)
    coarse = hidden_grad.astype(BF16)
    fine = (hidden_grad - coarse.astype(F32)).astype(BF16)
    tail = [mm_nn(hot, coarse) + mm_nn(hot, fine), gain1_grad, bias1_grad, gain2_grad, bias2_grad]
    tail.append(jnp.zeros((s.tail - s.leads - 4, D), F32))
    k.vb[near[1]] = jnp.concatenate(tail, axis=0).astype(BF16)
    swap_start("vb", near)
    grads_step4(1)
    swap_wait("ent", every)
    k.va_sum[...] = swap_sum("va")
    k.va_sum[24:32, 0:128] = jnp.sum(k.ent[...], axis=0)
    k.vb_sum[...] = swap_sum("vb")
    grads_step5(1)

    outs = [
        pltpu.make_async_copy(k.gout, o_grads, k.loads.at[0]),
        pltpu.make_async_copy(k.va_sum, o_va, k.loads.at[1]),
        pltpu.make_async_copy(k.vb_sum, o_vb, k.loads.at[2]),
    ]
    for copy in outs:
        copy.start()

    for j in range(1, nt):
        z_copy("zmask", j, k.mask.at[t], k.mask.at[t]).wait_send()
        z_copy("zgate", j, k.gate.at[my_gate], k.gate.at[my_gate]).wait_send()
        z_copy("zow", j, ow_half(t, core), ow_half(t, core)).wait_send()
        remote(
            ow_half(t, core), ow_half(t, core), k.zowr_s.at[j - 1], k.zowr_r.at[j - 1], (sib, t)
        ).wait_send()
        z_copy("zatt", j, k.att.at[t], k.att.at[t]).wait_send()
    rs_finish("zff", k.ffp, k.ffr)
    gather_finish("zblk", k.blow)
    rs_finish("zn2", k.n2p, k.n2r)
    gather_finish("zn2g", k.n2g)
    rs_finish("zng", k.ngp, k.ngr)
    gather_finish("zngg", k.ngg)
    ag_finish("kv", kv_at)
    ag_finish("q", q_at)
    ag_finish("da", da_at)
    ag_finish("st", st_at)
    swap_finish("cnt", every)
    swap_finish("ent", every)
    block_copy.wait()
    hidden_copy.wait()
    for copy in outs:
        copy.wait()


def last_kernel(
    s, block, hidden, grads, va, vb,
    o_block, o_pen, o_hidden, o_lead, o_g1, o_b1, o_qkv, o_out, o_g2, o_b2, o_up, o_down, o_gate,
):
    o_block[...] = block[...].astype(F32)
    o_hidden[...] = hidden[...]
    o_down[...] = grads[0 : s.F, :].astype(F32)
    o_up[...] = grads[s.F : s.F + s.D, :].astype(F32)
    base = s.bases[1]
    o_out[...] = grads[base : base + s.W, :].astype(F32)
    for c in range(3):
        rows = grads[base + (c + 1) * s.W : base + (c + 2) * s.W, :]
        o_qkv[c] = jnp.transpose(rows.astype(F32))
    small = va[...]
    for e in range(3):
        o_gate[e] = small[8 * e : 8 * e + 4]
    o_pen[...] = small[24:25, 0:1]
    tail = vb[...]
    o_lead[...] = tail[0 : s.leads]
    o_g1[...] = tail[s.leads : s.leads + 1]
    o_b1[...] = tail[s.leads + 1 : s.leads + 2]
    o_g2[...] = tail[s.leads + 2 : s.leads + 3]
    o_b2[...] = tail[s.leads + 3 : s.leads + 4]


def local(
    nb,
    nt,
    patches,
    window_ids,
    lead_index,
    lead_table,
    attention_gain,
    attention_bias,
    query_key_value,
    out_weight,
    feedforward_gain,
    feedforward_bias,
    up_weight,
    down_weight,
    gate_head,
    pixel_mask,
    cotangent,
):
    L, D = patches.shape
    leads = lead_table.shape[0]
    W = out_weight.shape[0]
    F = up_weight.shape[1]
    s = dims_of(nb, nt, L, D, W, F, leads, L * nb * pixel_mask.shape[0] * nt)
    scratch = scratch_of(s)
    vm = pl.BlockSpec(memory_space=pltpu.VMEM)
    hbm = pl.BlockSpec(memory_space=pl.ANY)
    row = (1, D)
    block, hidden, grads, va, vb = pl.pallas_call(
        partial(main_kernel, s, tuple(scratch)),
        out_shape=(
            jax.ShapeDtypeStruct((L, D), BF16),
            jax.ShapeDtypeStruct((L, D), F32),
            jax.ShapeDtypeStruct((s.rows, D), BF16),
            jax.ShapeDtypeStruct((32, D), F32),
            jax.ShapeDtypeStruct((s.tail, D), F32),
        ),
        in_specs=[hbm, vm, vm, vm, vm, vm, hbm, hbm, vm, vm, hbm, hbm, vm, vm, hbm],
        out_specs=(hbm,) * 5,
        scratch_shapes=list(scratch.values()),
        compiler_params=pltpu.CompilerParams(
            collective_id=0, has_side_effects=True, vmem_limit_bytes=VMEM_LIMIT
        ),
        name="block_step",
    )(
        patches,
        window_ids.reshape(nb, L),
        lead_index.reshape(1, L),
        lead_table,
        attention_gain.reshape(row),
        attention_bias.reshape(row),
        query_key_value,
        out_weight,
        feedforward_gain.reshape(row),
        feedforward_bias.reshape(row),
        up_weight,
        down_weight,
        gate_head,
        pixel_mask,
        cotangent,
    )
    vec = jax.ShapeDtypeStruct(row, F32)
    outs = pl.pallas_call(
        partial(last_kernel, s),
        out_shape=(
            jax.ShapeDtypeStruct((L, D), F32),
            jax.ShapeDtypeStruct((1, 1), F32),
            jax.ShapeDtypeStruct((L, D), F32),
            jax.ShapeDtypeStruct((leads, D), F32),
            vec,
            vec,
            jax.ShapeDtypeStruct((3, D, W), F32),
            jax.ShapeDtypeStruct((W, D), F32),
            vec,
            vec,
            jax.ShapeDtypeStruct((D, F), F32),
            jax.ShapeDtypeStruct((F, D), F32),
            jax.ShapeDtypeStruct(gate_head.shape, F32),
        ),
        in_specs=[vm] * 5,
        out_specs=(vm,) * 13,
        compiler_params=pltpu.CompilerParams(vmem_limit_bytes=VMEM_LIMIT),
        name="write_out",
    )(block, hidden, grads, va, vb)
    outs = list(outs)
    outs[1] = outs[1].reshape(())
    for i in (4, 5, 8, 9):
        outs[i] = outs[i].reshape((D,))
    return tuple(outs)


def solution(mesh):
    in_specs = (
        P("blk", None),
        P(),
        P("blk"),
        P(),
        P(),
        P(),
        P(None, None, "tp"),
        P("tp", None),
        P(),
        P(),
        P(None, "tp"),
        P("tp", None),
        P(None, "tp", None),
        P("tp", "blk"),
        P("blk", None),
    )
    out_specs = (
        P("blk", None),
        P(),
        P("blk", None),
        P(),
        P(),
        P(),
        P(None, None, "tp"),
        P("tp", None),
        P(),
        P(),
        P(None, "tp"),
        P("tp", None),
        P(None, "tp", None),
    )
    return jax.shard_map(
        partial(local, mesh.shape["blk"], mesh.shape["tp"]),
        mesh=mesh,
        in_specs=in_specs,
        out_specs=out_specs,
        check_vma=False,
    )
```

time: 561 us -> 149 us (0.27)
  waiting for transfers between devices: 386 us -> 0 us
  Pallas kernels: 0 us -> 131 us
  blocking collectives: 68 us -> 0 us
  matrix products: 46.9 us -> 0 us
  between operations: 17.9 us -> 0.66 us
  other arithmetic: 19.8 us -> 5.14 us
  local copies, waits for them, and re-layouts: 20.6 us -> 11.6 us
    psum x7 -> x0, waiting for transfers between devices: 346 us -> none  [the longest x2 170 us: local(): lax.psum((qkv_grad, out_weight_grad, up_grad, down_grad, gate_grad, first...]
    pallas_call x0 -> x2, Pallas kernels: none -> 131 us  [the longest x1 124 us: local(): pl.pallas_call(partial(main_kernel, s, tuple(scratch)), out_shape=(jax.Sh...]
    dot_general x22 -> x0, matrix products: 45.2 us -> none  [the longest x1 4.53 us: visit_block(): jnp.einsum('hqk,qhd->khd', probs_low, attended_grad_low, preferred_elemen...]
    psum x1 -> x0, blocking collectives: 41.2 us -> none  [local(): lax.psum((jnp.sum(mask_float * entropy), jnp.sum(mask_float)), ('blk', 't...]
    reduce_scatter x1 -> x0, waiting for transfers between devices: 39.8 us -> none  [local(): lax.psum_scatter(gathered_grads, 'blk', scatter_dimension=0, tiled=True)]
    all_gather x2 -> x0, blocking collectives: 26.8 us -> none  [the longest x1 14.5 us: local(): lax.all_gather(key_block, 'blk', axis=0, tiled=True)]
    unnamed x112 -> x2, local copies, waits for them, and re-layouts: 19.7 us -> 5.23 us
    reduce_sum x10 -> x0, other arithmetic: 9.62 us -> none  [the longest x1 2.02 us: absorb_block(): totals = totals * factor + jnp.sum(weights, axis=-1)]
  transfers between devices with their start and end apart: 8 -> 0, of which waited for: 8 -> 0; matrix products, arithmetic and copies ran while one was open for 3% -> 0% of each run, Pallas kernels for 0% -> 0%
where the time goes in v1:
time: 149 us; the launch traced here: 148 us
  Pallas kernels  131 us (88%)
  local copies, waits for them, and re-layouts  11.6 us (8%)
  other arithmetic  5.14 us (3%)
    pallas_call x1, Pallas kernels, local(): pl.pallas_call(partial(main_kernel, s, tuple(scratch)), out_shape=(jax.Sh...  124 us
    pallas_call x1, Pallas kernels, local(): pl.pallas_call(partial(last_kernel, s), out_shape=(jax.ShapeDtypeStruct((...  6.44 us
    unnamed x2, local copies, waits for them, and re-layouts  5.23 us
    pallas_call x4, other arithmetic, local(): pl.pallas_call(partial(last_kernel, s), out_shape=(jax.ShapeDtypeStruct((...  5.14 us

profile of v1, /device:TPU:1, one launch (start us, length us, event | category | flops | bytes accessed | tf_op | source)
XLA Modules:
  0.0 147.9 jit_solution(17005699586013330332)
XLA Ops:
  0.6 1.3 reshape.61.refs_4_
  1.9 1.3 reshape.62.refs_5_
  3.2 1.3 reshape.63.refs_8_
  4.4 1.3 reshape.64.refs_9_
  5.7 1.3 reshape.59.refs_1_
  7.0 2.3 %copy.28.refs_6_ = bf16[3,768,192]{2,1,0:T(8,128)(2,1)} copy(bf16[3,768,192]{1,2,0:T(8,128)(2,1)} %param.21) | data formatting | bytes 1769472 | tf_op args[6]
  9.3 124.1 %block_step.1 = (bf16[256,768]{1,0:T(8,128)(2,1)}, f32[256,768]{1,0:T(8,128)}, bf16[2304,768]{1,0:T(8,128)(2,1)}, f32[32,768]{1,0:T(8,128)}, f32[32,768]{1,0:T(8,128)}) custom-call(f32[256,768]{1,0:T(8,128)} %refs_0_.1, s32[8,256]{1,0:T(8,128)} %reshape.59.refs_1_, s32[1,256]{1,0:T(1,128)} %bitcast.2, bf16[16,768]{1,0:T(8,128)(2,1)} %refs_3_.1, ...), custom_call_target="tpu_custom_call" | custom-call | tf_op jit(solution)/shard_map/block_step/pallas_call | solution.py:814
  133.4 6.4 %write_out.1 = (f32[256,768]{1,0:T(8,128)}, f32[1,1]{1,0:T(1,128)}, f32[256,768]{1,0:T(8,128)}, f32[16,768]{1,0:T(8,128)}, f32[1,768]{1,0:T(1,128)}, /*index=5*/...) custom-call(bf16[256,768]{1,0:T(8,128)(2,1)} %get-tuple-element.31.b, ...), custom_call_target="tpu_custom_call" | custom-call | tf_op jit(solution)/shard_map/write_out/pallas_call | solution.py:848
  139.9 1.3 reduce
  141.2 1.3 reduce.1
  142.4 1.3 reduce.2
  143.7 1.3 reduce.3
  145.0 2.9 %copy.29 = f32[3,768,192]{1,2,0:T(8,128)} copy(f32[3,768,192]{2,1,0:T(8,128)} %get-tuple-element.55) | data formatting | bytes 3538944

commit v2 on v1

--- a/solution.py
+++ b/solution.py
@@ -51,6 +51,10 @@
         - jnp.mean(scaled, axis=-1, keepdims=True)
         - unit_rows * jnp.mean(scaled * unit_rows, axis=-1, keepdims=True)
     )
+
+
+def row_of(ref):
+    return ref[...].reshape(1, ref.shape[0])
 
 
 def total(x):
@@ -76,7 +80,8 @@
     v = pltpu.VMEM
     out = {
         "patches": v((L, D), F32),
-        "qkv": v((3, D, W), BF16),
+        "ids": v((nb, L), F32),
+        "qkv": v((3, W, D), BF16),
         "ow": v((nt, W, D), BF16),
         "up": v((D, F), BF16),
         "down": v((F, D), BF16),
@@ -160,7 +165,7 @@
 def main_kernel(s, names, *refs):
     (
         patches,
-        windows,
+        windows_in,
         leads_in,
         table,
         gain1,
@@ -431,18 +436,18 @@
     for j in range(1, nt):
         pl.semaphore_signal(barrier, inc=1, device_id=(b, z_peer(j)), device_id_type=MESH)
 
-    lead_hot = (lax.broadcasted_iota(jnp.int32, (s.leads, L), 0) == leads_in[...]).astype(F32)
+    lead_hot = (lax.broadcasted_iota(jnp.int32, (s.leads, L), 0) == row_of(leads_in)).astype(F32)
     loads[0].wait()
     hidden = k.patches[...] + mm_tn(lead_hot.astype(BF16), table[...])
     unit1, inverse1 = norm_stats(hidden)
     k.u1[...] = unit1
     k.r1[...] = inverse1
     k.mid[...] = hidden
-    k.normed[...] = (unit1 * gain1[...] + bias1[...]).astype(BF16)
+    k.normed[...] = (unit1 * row_of(gain1) + row_of(bias1)).astype(BF16)
     loads[1].wait()
 
     def project(c):
-        return jnp.transpose(mm_nn(k.normed[...], k.qkv[c]))
+        return mm_nt(k.qkv[c], k.normed[...])
 
     k.kv[b, 0:W, :] = project(1).astype(BF16)
     k.kv[b, W : 2 * W, :] = project(2).astype(BF16)
@@ -478,8 +483,10 @@
     k.cnt[b] = jnp.broadcast_to(total(jnp.sum(k.mask[...], axis=0)), (8, 128))
     swap_start("cnt", every)
 
+    k.ids[...] = windows_in[...].reshape(nb, L).astype(F32)
+
     def id_row(band):
-        return windows[pl.ds(band, 1), :].astype(F32)
+        return k.ids[pl.ds(band, 1), :]
 
     def id_column(band):
         return jnp.transpose(jnp.broadcast_to(id_row(band), (128, L)))[:, 0:1]
@@ -559,7 +566,7 @@
     unit2, inverse2 = norm_stats(middle)
     k.u2[...] = unit2
     k.r2[...] = inverse2
-    k.n2low[...] = (unit2 * gain2[...] + bias2[...]).astype(BF16)
+    k.n2low[...] = (unit2 * row_of(gain2) + row_of(bias2)).astype(BF16)
     loads[3].wait()
     loads[4].wait()
     upward = mm_nn(k.n2low[...], k.up[...])
@@ -623,7 +630,7 @@
     n2_grad = k.n2g[...].astype(F32)
     gain2_grad = jnp.sum(n2_grad * k.u2[...], axis=0, keepdims=True)
     bias2_grad = jnp.sum(n2_grad, axis=0, keepdims=True)
-    middle_grad = k.cot[...] + norm_backward(n2_grad, k.u2[...], k.r2[...], gain2[...])
+    middle_grad = k.cot[...] + norm_backward(n2_grad, k.u2[...], k.r2[...], row_of(gain2))
     k.cot[...] = middle_grad
     k.mglow[...] = middle_grad.astype(BF16)
 
@@ -687,9 +694,7 @@
     k.dp[0] = (k.dq[...] * SCALE).astype(BF16)
     k.dp[1] = k.dk[...].astype(BF16)
     k.dp[2] = k.dv[...].astype(BF16)
-    n1_part = mm_nt(jnp.transpose(k.dp[0].astype(F32)).astype(BF16), k.qkv[0])
-    n1_part += mm_nt(jnp.transpose(k.dp[1].astype(F32)).astype(BF16), k.qkv[1])
-    n1_part += mm_nt(jnp.transpose(k.dp[2].astype(F32)).astype(BF16), k.qkv[2])
+    n1_part = mm_tn(k.dp[...].reshape(3 * W, L), k.qkv[...].reshape(3 * W, D))
     k.ngp[...] = n1_part.astype(BF16)
     rs_start("zng", k.ngp, k.ngr)
     base = s.bases[1] + W
@@ -706,7 +711,7 @@
     unit1 = k.u1[...]
     gain1_grad = jnp.sum(n1_grad * unit1, axis=0, keepdims=True)
     bias1_grad = jnp.sum(n1_grad, axis=0, keepdims=True)
-    hidden_grad = k.cot[...] + norm_backward(n1_grad, unit1, k.r1[...], gain1[...])
+    hidden_grad = k.cot[...] + norm_backward(n1_grad, unit1, k.r1[...], row_of(gain1))
     k.patches[...] = hidden_grad
     hidden_copy = pltpu.make_async_copy(k.patches, o_hidden, k.loads.at[7])
     hidden_copy.start()
@@ -770,17 +775,17 @@
     o_out[...] = grads[base : base + s.W, :].astype(F32)
     for c in range(3):
         rows = grads[base + (c + 1) * s.W : base + (c + 2) * s.W, :]
-        o_qkv[c] = jnp.transpose(rows.astype(F32))
+        o_qkv[c] = rows.astype(F32)
     small = va[...]
     for e in range(3):
         o_gate[e] = small[8 * e : 8 * e + 4]
     o_pen[...] = small[24:25, 0:1]
     tail = vb[...]
     o_lead[...] = tail[0 : s.leads]
-    o_g1[...] = tail[s.leads : s.leads + 1]
-    o_b1[...] = tail[s.leads + 1 : s.leads + 2]
-    o_g2[...] = tail[s.leads + 2 : s.leads + 3]
-    o_b2[...] = tail[s.leads + 3 : s.leads + 4]
+    o_g1[...] = tail[s.leads + 0].reshape(s.D)
+    o_b1[...] = tail[s.leads + 1].reshape(s.D)
+    o_g2[...] = tail[s.leads + 2].reshape(s.D)
+    o_b2[...] = tail[s.leads + 3].reshape(s.D)
 
 
 def local(
@@ -810,7 +815,6 @@
     scratch = scratch_of(s)
     vm = pl.BlockSpec(memory_space=pltpu.VMEM)
     hbm = pl.BlockSpec(memory_space=pl.ANY)
-    row = (1, D)
     block, hidden, grads, va, vb = pl.pallas_call(
         partial(main_kernel, s, tuple(scratch)),
         out_shape=(
@@ -829,22 +833,22 @@
         name="block_step",
     )(
         patches,
-        window_ids.reshape(nb, L),
-        lead_index.reshape(1, L),
+        window_ids,
+        lead_index,
         lead_table,
-        attention_gain.reshape(row),
-        attention_bias.reshape(row),
-        query_key_value,
+        attention_gain,
+        attention_bias,
+        jnp.transpose(query_key_value, (0, 2, 1)),
         out_weight,
-        feedforward_gain.reshape(row),
-        feedforward_bias.reshape(row),
+        feedforward_gain,
+        feedforward_bias,
         up_weight,
         down_weight,
         gate_head,
         pixel_mask,
         cotangent,
     )
-    vec = jax.ShapeDtypeStruct(row, F32)
+    vec = jax.ShapeDtypeStruct((D,), F32)
     outs = pl.pallas_call(
         partial(last_kernel, s),
         out_shape=(
@@ -854,7 +858,7 @@
             jax.ShapeDtypeStruct((leads, D), F32),
             vec,
             vec,
-            jax.ShapeDtypeStruct((3, D, W), F32),
+            jax.ShapeDtypeStruct((3, W, D), F32),
             jax.ShapeDtypeStruct((W, D), F32),
             vec,
             vec,
@@ -869,8 +873,7 @@
     )(block, hidden, grads, va, vb)
     outs = list(outs)
     outs[1] = outs[1].reshape(())
-    for i in (4, 5, 8, 9):
-        outs[i] = outs[i].reshape((D,))
+    outs[6] = jnp.transpose(outs[6], (0, 2, 1))
     return tuple(outs)
 
 

time: 149 us -> 131 us (0.88)
  local copies, waits for them, and re-layouts: 11.6 us -> 0 us
  other arithmetic: 5.14 us -> 0 us
    reshape x5 -> x0, local copies, waits for them, and re-layouts: 6.36 us -> none  [the longest x1 1.3 us: local(): window_ids.reshape(nb, L)]
    unnamed x2 -> x0, local copies, waits for them, and re-layouts: 5.23 us -> none
    pallas_call x4 -> x0, other arithmetic: 5.14 us -> none  [local(): pl.pallas_call(partial(last_kernel, s), out_shape=(jax.ShapeDtypeStruct((...]
where the time goes in v2:
time: 131 us
  Pallas kernels  130 us (99%)
    pallas_call x1, Pallas kernels, local(): pl.pallas_call(partial(main_kernel, s, tuple(scratch)), out_shape=(jax.Sh...  124 us
    pallas_call x1, Pallas kernels, local(): pl.pallas_call(partial(last_kernel, s), out_shape=(jax.ShapeDtypeStruct((...  6.04 us

profile of v2, /device:TPU:1, one launch (start us, length us, event | category | flops | bytes accessed | tf_op | source)
XLA Modules:
  0.0 131.1 jit_solution(14134099751864751689)
XLA Ops:
  0.7 124.4 %block_step.1 = (bf16[256,768]{1,0:T(8,128)(2,1)}, f32[256,768]{1,0:T(8,128)}, bf16[2304,768]{1,0:T(8,128)(2,1)}, f32[32,768]{1,0:T(8,128)}, f32[32,768]{1,0:T(8,128)}) custom-call(f32[256,768]{1,0:T(8,128)} %refs_0_.1, s32[2048]{0:T(1024)} %refs_1_.1, s32[256]{0:T(256)} %refs_2_.1, bf16[16,768]{1,0:T(8,128)(2,1)} %refs_3_.1, f32[768]{0:T(1024)} %refs_4_.1, ...), custom_call_target="tpu_custom_call" | custom-call | tf_op jit(solution)/shard_map/block_step/pallas_call | solution.py:818
  125.1 6.0 %write_out.1 = (f32[256,768]{1,0:T(8,128)}, f32[1,1]{1,0:T(1,128)}, f32[256,768]{1,0:T(8,128)}, f32[16,768]{1,0:T(8,128)}, f32[768]{0:T(1024)}, /*index=5*/f32[7...) custom-call(bf16[256,768]{1,0:T(8,128)(2,1)} %get-tuple-element.31.b, ...), custom_call_target="tpu_custom_call" | custom-call | tf_op jit(solution)/shard_map/write_out/pallas_call | solution.py:852

commit v3 on v2

--- a/solution.py
+++ b/solution.py
@@ -68,8 +68,8 @@
     s.half = nb // 2
     s.groups = nb // GROUP
     s.pixels = pixels
-    s.sizes = (hidden + width, local_width * 4)
-    s.bases = (0, s.sizes[0])
+    s.sizes = (hidden + width, local_width * 2, local_width * 2)
+    s.bases = (0, hidden + width, hidden + width + 2 * local_width)
     s.rows = sum(s.sizes)
     s.tail = (leads + 4 + 15) // 16 * 16
     return s
@@ -112,7 +112,8 @@
         "n2p": v((L, D), BF16),
         "n2r": v((nt - 1, S, D), BF16),
         "n2g": v((L, D), BF16),
-        "mglow": v((L, D), BF16),
+        "dasrc": v((nt, S, W), BF16),
+        "datok": v((nt, S, W), BF16),
         "dq": v((W, L), F32),
         "dk": v((W, L), F32),
         "dv": v((W, L), F32),
@@ -130,7 +131,7 @@
     }
     dma = pltpu.SemaphoreType.DMA
     out["loads"] = dma((8,))
-    for name in ("zmask", "zgate", "zow", "zowr", "zatt", "zff", "zblk", "zn2", "zn2g", "zng", "zngg"):
+    for name in ("zmask", "zgate", "zow", "zowr", "zatt", "zff", "zblk", "zn2", "zn2g", "zda", "zng", "zngg"):
         out[name + "_s"] = dma((nt - 1,))
         out[name + "_r"] = dma((nt - 1,))
     for name in ("kv", "q", "da", "st"):
@@ -444,13 +445,6 @@
     k.r1[...] = inverse1
     k.mid[...] = hidden
     k.normed[...] = (unit1 * row_of(gain1) + row_of(bias1)).astype(BF16)
-    loads[1].wait()
-
-    def project(c):
-        return mm_nt(k.qkv[c], k.normed[...])
-
-    k.kv[b, 0:W, :] = project(1).astype(BF16)
-    k.kv[b, W : 2 * W, :] = project(2).astype(BF16)
     gate_pad = jnp.zeros((4, D), F32)
     gate_rows = []
     for e in range(3):
@@ -459,23 +453,29 @@
     my_gate = pl.ds(pl.multiple_of(t * 32, 32), 32)
     k.gate[my_gate, :] = jnp.concatenate(gate_rows, axis=0).astype(BF16)
     k.mask[t] = jnp.concatenate([pixel_mask[...].astype(F32), jnp.zeros((4, L), F32)], axis=0)
+    hw = W // 2
+
+    def ow_half(tt, c):
+        return k.ow.at[tt, pl.ds(pl.multiple_of(c * hw, hw), hw)]
+
+    loads[2].wait()
     pl.semaphore_wait(barrier, nb - 1 + nt - 1)
+    for j in range(1, nt):
+        z_copy("zmask", j, k.mask.at[t], k.mask.at[t]).start()
+        z_copy("zow", j, ow_half(t, core), ow_half(t, core)).start()
+        z_copy("zgate", j, k.gate.at[my_gate], k.gate.at[my_gate]).start()
+    loads[1].wait()
+
+    def project(c):
+        return mm_nt(k.qkv[c], k.normed[...])
+
+    k.kv[b, 0:W, :] = project(1).astype(BF16)
+    k.kv[b, W : 2 * W, :] = project(2).astype(BF16)
 
     def kv_at(band):
         return k.kv.at[band]
 
     ag_start("kv", kv_at)
-    for j in range(1, nt):
-        z_copy("zmask", j, k.mask.at[t], k.mask.at[t]).start()
-        z_copy("zgate", j, k.gate.at[my_gate], k.gate.at[my_gate]).start()
-    hw = W // 2
-    loads[2].wait()
-
-    def ow_half(tt, c):
-        return k.ow.at[tt, pl.ds(pl.multiple_of(c * hw, hw), hw)]
-
-    for j in range(1, nt):
-        z_copy("zow", j, ow_half(t, core), ow_half(t, core)).start()
     k.qd[b, 0:W, :] = (project(0).astype(BF16).astype(F32) * SCALE).astype(BF16)
 
     for j in range(1, nt):
@@ -501,20 +501,32 @@
     k.l[...] = jnp.zeros((8, L), F32)
     k.acc[...] = jnp.zeros((W, L), F32)
 
-    def forward_band(band):
-        allowed = id_column(band) == id_row(b)
+    def forward_bands(bands):
+        tiles = [(h, i) for h in range(H) for i in range(len(bands))]
+        allowed = [id_column(band) == id_row(b) for band in bands]
+        scores = {
+            (h, i): jnp.where(
+                allowed[i], mm_tn(k.kv[bands[i], head(h), :], k.qd[b, head(h), :]), MASKED
+            )
+            for h, i in tiles
+        }
+        old_high = [k.m[h : h + 1, :] for h in range(H)]
+        sums = [k.l[h : h + 1, :] for h in range(H)]
+        outs = [k.acc[head(h), :] for h in range(H)]
+        high = list(old_high)
+        for h, i in tiles:
+            high[h] = jnp.maximum(high[h], jnp.max(scores[h, i], axis=0, keepdims=True))
+        weights = {(h, i): jnp.exp(scores[h, i] - high[h]) for h, i in tiles}
+        factor = [jnp.exp(x - y) for x, y in zip(old_high, high)]
+        outs = [x * f for x, f in zip(outs, factor)]
+        sums = [x * f for x, f in zip(sums, factor)]
+        for h, i in tiles:
+            outs[h] += mm_nn(k.kv[bands[i], value_head(h), :], weights[h, i].astype(BF16))
+            sums[h] += jnp.sum(weights[h, i], axis=0, keepdims=True)
         for h in range(H):
-            scores = mm_tn(k.kv[band, head(h), :], k.qd[b, head(h), :])
-            scores = jnp.where(allowed, scores, MASKED)
-            high = k.m[h : h + 1, :]
-            new_high = jnp.maximum(high, jnp.max(scores, axis=0, keepdims=True))
-            weights = jnp.exp(scores - new_high)
-            factor = jnp.exp(high - new_high)
-            k.m[h : h + 1, :] = new_high
-            k.l[h : h + 1, :] = k.l[h : h + 1, :] * factor + jnp.sum(weights, axis=0, keepdims=True)
-            k.acc[head(h), :] = k.acc[head(h), :] * factor + mm_nn(
-                k.kv[band, value_head(h), :], weights.astype(BF16)
-            )
+            k.m[h : h + 1, :] = high[h]
+            k.l[h : h + 1, :] = sums[h]
+            k.acc[head(h), :] = outs[h]
 
     @pl.loop(0, s.half)
     def _(i):
@@ -522,9 +534,8 @@
         def _():
             ag_relay("kv", kv_at, i)
 
-        forward_band(band_same(i))
         ag_wait_relay("kv", kv_at, i)
-        forward_band(band_sib(i))
+        forward_bands([band_same(i), band_sib(i)])
 
     for h in range(H):
         att = k.acc[head(h), :] / k.l[h : h + 1, :]
@@ -624,17 +635,22 @@
     swap_start("va", near)
     swap_start("ent", every)
     grads_step2(0)
-    k.n2g[mine, :] = rs_sum("zn2", k.n2p, k.n2r).astype(BF16)
+    n2_low = rs_sum("zn2", k.n2p, k.n2r).astype(BF16)
+    k.n2g[mine, :] = n2_low
+
+    def middle_backward(n2_grad, rows):
+        return k.cot[rows, :] + norm_backward(n2_grad, k.u2[rows, :], k.r2[rows, :], row_of(gain2))
+
+    low_slice = middle_backward(n2_low.astype(F32), mine).astype(BF16)
+    for tt in range(nt):
+        k.dasrc[tt] = mm_nt(low_slice, k.ow[tt]).astype(BF16)
+    for j in range(1, nt):
+        z_copy("zda", j, k.dasrc.at[z_peer(j)], k.datok.at[t]).start()
     gather_start("zn2g", k.n2g)
-    gather_wait("zn2g", k.n2g)
-    n2_grad = k.n2g[...].astype(F32)
-    gain2_grad = jnp.sum(n2_grad * k.u2[...], axis=0, keepdims=True)
-    bias2_grad = jnp.sum(n2_grad, axis=0, keepdims=True)
-    middle_grad = k.cot[...] + norm_backward(n2_grad, k.u2[...], k.r2[...], row_of(gain2))
-    k.cot[...] = middle_grad
-    k.mglow[...] = middle_grad.astype(BF16)
-
-    att_grad = mm_nt(k.ow[t], k.mglow[...]).astype(BF16)
+    k.datok[t] = k.dasrc[t]
+    for j in range(1, nt):
+        z_copy("zda", j, k.dasrc.at[z_peer(j)], k.datok.at[z_from(j)]).wait_recv()
+    att_grad = jnp.transpose(k.datok[...].reshape(L, W).astype(F32)).astype(BF16)
     k.qd[b, W : 2 * W, :] = att_grad
     weighted = att_grad.astype(F32) * k.acc[...]
     for h in range(H):
@@ -643,40 +659,73 @@
         )
     ag_start("st", st_at)
     ag_start("da", da_at)
-    k.gsrc[s.bases[1] : s.bases[1] + W, :] = mm_nn(k.att[t], k.mglow[...]).astype(BF16)
     k.dq[...] = jnp.zeros((W, L), F32)
     k.dk[...] = jnp.zeros((W, L), F32)
     k.dv[...] = jnp.zeros((W, L), F32)
-
-    @pl.loop(0, nb)
-    def _(band):
-        allowed = id_column(band) == id_row(b)
+    my_column = id_column(b)
+
+    def score_grads(allowed, scores, dots, stats):
+        probs = {
+            (h, i): jnp.exp(jnp.where(allowed[i], x, MASKED) - stats[i][h : h + 1])
+            for (h, i), x in scores.items()
+        }
+        grads = {
+            (h, i): (x * (dots[h, i] - stats[i][H + h : H + h + 1])).astype(BF16)
+            for (h, i), x in probs.items()
+        }
+        return probs, grads
+
+    @pl.loop(0, s.half)
+    def _(step):
+        bands = [2 * step, 2 * step + 1]
+        tiles = [(h, i) for h in range(H) for i in range(2)]
+        allowed = [id_column(band) == id_row(b) for band in bands]
+        scores = {(h, i): mm_tn(k.kv[bands[i], head(h), :], k.qd[b, head(h), :]) for h, i in tiles}
+        dots = {
+            (h, i): mm_tn(k.kv[bands[i], value_head(h), :], k.qd[b, value_head(h), :]) for h, i in tiles
+        }
+        outs = [k.dq[head(h), :] for h in range(H)]
+        _, grads = score_grads(allowed, scores, dots, [k.st[b]] * 2)
+        for h, i in tiles:
+            outs[h] += mm_nn(k.kv[bands[i], head(h), :], grads[h, i])
         for h in range(H):
-            keys = k.kv[band, head(h), :]
-            scores = jnp.where(allowed, mm_tn(keys, k.qd[b, head(h), :]), MASKED)
-            prob = jnp.exp(scores - k.st[b, h : h + 1, :])
-            dots = mm_tn(k.kv[band, value_head(h), :], k.qd[b, value_head(h), :])
-            grad = (prob * (dots - k.st[b, H + h : H + h + 1, :])).astype(BF16)
-            k.dq[head(h), :] += mm_nn(keys, grad)
+            k.dq[head(h), :] = outs[h]
+
+    k.dp[0] = (k.dq[...] * SCALE).astype(BF16)
+    base = s.bases[1]
+    gather_wait("zn2g", k.n2g)
+    n2_grad = k.n2g[...].astype(F32)
+    gain2_grad = jnp.sum(n2_grad * k.u2[...], axis=0, keepdims=True)
+    bias2_grad = jnp.sum(n2_grad, axis=0, keepdims=True)
+    middle_grad = middle_backward(n2_grad, pl.ds(0, L))
+    k.cot[...] = middle_grad
+    k.gsrc[base : base + W, :] = mm_nn(k.att[t], middle_grad.astype(BF16)).astype(BF16)
+    k.gsrc[base + W : base + 2 * W, :] = mm_nn(k.dp[0], k.normed[...]).astype(BF16)
+    grads_step1(1)
+    grads_step3(0)
 
     @pl.loop(1, s.half)
     def _(i):
         ag_wait_relay("q", q_at, i)
 
     ag_wait_relay("q", q_at, 0)
-    my_column = id_column(b)
-
-    def backward_band(band):
-        allowed = my_column == id_row(band)
+
+    def backward_bands(bands):
+        tiles = [(h, i) for h in range(H) for i in range(len(bands))]
+        allowed = [my_column == id_row(band) for band in bands]
+        scores = {(h, i): mm_tn(k.kv[b, head(h), :], k.qd[bands[i], head(h), :]) for h, i in tiles}
+        dots = {
+            (h, i): mm_tn(k.kv[b, value_head(h), :], k.qd[bands[i], value_head(h), :]) for h, i in tiles
+        }
+        key_outs = [k.dk[head(h), :] for h in range(H)]
+        value_outs = [k.dv[head(h), :] for h in range(H)]
+        probs, grads = score_grads(allowed, scores, dots, [k.st[band] for band in bands])
+        for h, i in tiles:
+            key_outs[h] += mm_nt(k.qd[bands[i], head(h), :], grads[h, i])
+            value_outs[h] += mm_nt(k.qd[bands[i], value_head(h), :], probs[h, i].astype(BF16))
         for h in range(H):
-            queries = k.qd[band, head(h), :]
-            att_grads = k.qd[band, value_head(h), :]
-            scores = jnp.where(allowed, mm_tn(k.kv[b, head(h), :], queries), MASKED)
-            prob = jnp.exp(scores - k.st[band, h : h + 1, :])
-            dots = mm_tn(k.kv[b, value_head(h), :], att_grads)
-            grad = (prob * (dots - k.st[band, H + h : H + h + 1, :])).astype(BF16)
-            k.dk[head(h), :] += mm_nt(queries, grad)
-            k.dv[head(h), :] += mm_nt(att_grads, prob.astype(BF16))
+            k.dk[head(h), :] = key_outs[h]
+            k.dv[head(h), :] = value_outs[h]
 
     @pl.loop(0, s.half)
     def _(i):
@@ -685,27 +734,26 @@
             ag_relay("st", st_at, i)
             ag_relay("da", da_at, i)
 
-        backward_band(band_same(i))
         ag_wait_relay("st", st_at, i)
         ag_wait_relay("da", da_at, i)
-        backward_band(band_sib(i))
-
-    grads_step3(0)
-    k.dp[0] = (k.dq[...] * SCALE).astype(BF16)
+        backward_bands([band_same(i), band_sib(i)])
+
+    grads_step2(1)
     k.dp[1] = k.dk[...].astype(BF16)
     k.dp[2] = k.dv[...].astype(BF16)
     n1_part = mm_tn(k.dp[...].reshape(3 * W, L), k.qkv[...].reshape(3 * W, D))
     k.ngp[...] = n1_part.astype(BF16)
     rs_start("zng", k.ngp, k.ngr)
-    base = s.bases[1] + W
-    k.gsrc[base : base + 3 * W, :] = mm_nn(k.dp[...].reshape(3 * W, L), k.normed[...]).astype(BF16)
-    grads_step1(1)
-    grads_step2(1)
+    base = s.bases[2]
+    k.gsrc[base : base + 2 * W, :] = mm_nn(k.dp[1:3].reshape(2 * W, L), k.normed[...]).astype(BF16)
+    grads_step1(2)
+    grads_step3(1)
+    grads_step2(2)
     k.ngg[mine, :] = rs_sum("zng", k.ngp, k.ngr).astype(BF16)
     gather_start("zngg", k.ngg)
     grads_step4(0)
-    grads_step3(1)
-    grads_step5(0)
+    grads_step4(1)
+    grads_step3(2)
     gather_wait("zngg", k.ngg)
     n1_grad = k.ngg[...].astype(F32)
     unit1 = k.u1[...]
@@ -722,12 +770,13 @@
     tail.append(jnp.zeros((s.tail - s.leads - 4, D), F32))
     k.vb[near[1]] = jnp.concatenate(tail, axis=0).astype(BF16)
     swap_start("vb", near)
-    grads_step4(1)
+    grads_step4(2)
     swap_wait("ent", every)
     k.va_sum[...] = swap_sum("va")
     k.va_sum[24:32, 0:128] = jnp.sum(k.ent[...], axis=0)
     k.vb_sum[...] = swap_sum("vb")
-    grads_step5(1)
+    for i in range(3):
+        grads_step5(i)
 
     outs = [
         pltpu.make_async_copy(k.gout, o_grads, k.loads.at[0]),
@@ -745,6 +794,7 @@
             ow_half(t, core), ow_half(t, core), k.zowr_s.at[j - 1], k.zowr_r.at[j - 1], (sib, t)
         ).wait_send()
         z_copy("zatt", j, k.att.at[t], k.att.at[t]).wait_send()
+        z_copy("zda", j, k.dasrc.at[z_peer(j)], k.datok.at[t]).wait_send()
     rs_finish("zff", k.ffp, k.ffr)
     gather_finish("zblk", k.blow)
     rs_finish("zn2", k.n2p, k.n2r)

time: 131 us -> 127 us (0.969)
  Pallas kernels: 130 us -> 126 us
    pallas_call x1, Pallas kernels: 124 us -> 120 us  [local(): pl.pallas_call(partial(main_kernel, s, tuple(scratch)), out_shape=(jax.Sh...]
where the time goes in v3:
time: 127 us; the launch traced here: 126 us
  Pallas kernels  126 us (99%)
    pallas_call x1, Pallas kernels, local(): pl.pallas_call(partial(main_kernel, s, tuple(scratch)), out_shape=(jax.Sh...  120 us
    pallas_call x1, Pallas kernels, local(): pl.pallas_call(partial(last_kernel, s), out_shape=(jax.ShapeDtypeStruct((...  6.04 us

profile of v3, /device:TPU:1, one launch (start us, length us, event | category | flops | bytes accessed | tf_op | source)
XLA Modules:
  0.0 126.4 jit_solution(17192988755310842540)
XLA Ops:
  0.7 119.7 %block_step.1 = (bf16[256,768]{1,0:T(8,128)(2,1)}, f32[256,768]{1,0:T(8,128)}, bf16[2304,768]{1,0:T(8,128)(2,1)}, f32[32,768]{1,0:T(8,128)}, f32[32,768]{1,0:T(8,128)}) custom-call(f32[256,768]{1,0:T(8,128)} %refs_0_.1, s32[2048]{0:T(1024)} %refs_1_.1, s32[256]{0:T(256)} %refs_2_.1, bf16[16,768]{1,0:T(8,128)(2,1)} %refs_3_.1, f32[768]{0:T(1024)} %refs_4_.1, ...), custom_call_target="tpu_custom_call" | custom-call | tf_op jit(solution)/shard_map/block_step/pallas_call | solution.py:868
  120.3 6.0 %write_out.1 = (f32[256,768]{1,0:T(8,128)}, f32[1,1]{1,0:T(1,128)}, f32[256,768]{1,0:T(8,128)}, f32[16,768]{1,0:T(8,128)}, f32[768]{0:T(1024)}, /*index=5*/f32[7...) custom-call(bf16[256,768]{1,0:T(8,128)(2,1)} %get-tuple-element.31.b, ...), custom_call_target="tpu_custom_call" | custom-call | tf_op jit(solution)/shard_map/write_out/pallas_call | solution.py:902

commit v4 on v3

v4 whole, which is shorter than its diff:
```python
from functools import partial
from types import SimpleNamespace

import jax
import jax.numpy as jnp
from jax import lax
from jax.experimental import pallas as pl
from jax.experimental.pallas import tpu as pltpu
from jax.sharding import PartitionSpec as P

HEAD_DIM = 64
EPS = 1e-05
MASKED = -1e30
SCALE = HEAD_DIM ** (-0.5)
GROUP = 8
F32 = jnp.float32
BF16 = jnp.bfloat16
MESH = pl.DeviceIdType.MESH
VMEM_LIMIT = 61 * 2**20
INV_SQRT2 = 0.7071067811865476
INV_SQRT_2PI = 0.3989422804014327


def dot(a, b, ca, cb):
    return lax.dot_general(a, b, (((ca,), (cb,)), ((), ())), preferred_element_type=F32)


def mm_nn(a, b):
    return dot(a, b, 1, 0)


def mm_nt(a, b):
    return dot(a, b, 1, 1)


def mm_tn(a, b):
    return dot(a, b, 0, 0)


def norm_stats(values):
    mean = jnp.mean(values, axis=-1, keepdims=True)
    centered = values - mean
    inverse = lax.rsqrt(jnp.mean(centered * centered, axis=-1, keepdims=True) + EPS)
    return centered * inverse, inverse


def norm_backward(incoming, unit_rows, inverse, gain):
    scaled = incoming * gain
    return inverse * (
        scaled
        - jnp.mean(scaled, axis=-1, keepdims=True)
        - unit_rows * jnp.mean(scaled * unit_rows, axis=-1, keepdims=True)
    )


def row_of(ref):
    return ref[...].reshape(1, ref.shape[0])


def total(x):
    return jnp.sum(jnp.sum(x, axis=0, keepdims=True), axis=1, keepdims=True)


def dims_of(nb, nt, tokens, width, local_width, hidden, leads, pixels):
    s = SimpleNamespace(nb=nb, nt=nt, L=tokens, D=width, W=local_width, F=hidden, leads=leads)
    s.H = local_width // HEAD_DIM
    s.T = tokens // 2
    s.R = s.T // nt
    s.half = nb // 2
    s.groups = nb // GROUP
    s.pixels = pixels
    s.sizes = (hidden, width, local_width * 2, local_width * 2)
    s.bases = tuple(sum(s.sizes[:i]) for i in range(4))
    s.rows = sum(s.sizes)
    s.tail = (leads + 4 + 15) // 16 * 16
    return s


def scratch_of(s):
    L, D, W, F, nb, nt, R = s.L, s.D, s.W, s.F, s.nb, s.nt, s.R
    v = pltpu.VMEM
    out = {
        "patches": v((L, D), F32),
        "windows": v((nb * L,), jnp.int32),
        "lead_index": v((L,), jnp.int32),
        "table": v((s.leads, D), BF16),
        "gain1": v((D,), F32),
        "bias1": v((D,), F32),
        "gain2": v((D,), F32),
        "bias2": v((D,), F32),
        "pix": v((4, L), jnp.int32),
        "head": v((3, 4, D), BF16),
        "ids": v((nb, L), F32),
        "qkv": v((3, W, D), BF16),
        "ow": v((nt, W, D), BF16),
        "up": v((D, F), BF16),
        "down": v((F, D), BF16),
        "cot": v((L, D), F32),
        "gatec": v((nt, 16, D), BF16),
        "gate": v((nt * 32, D), BF16),
        "mask": v((nt, 8, L), F32),
        "cnt": v((nb, 8, 128), F32),
        "u1": v((L, D), F32),
        "r1": v((L, 1), F32),
        "normed": v((L, D), BF16),
        "kv": v((nb, 2 * W, L), BF16),
        "qd": v((nb, 2 * W, L), BF16),
        "st": v((nb, 8, L), F32),
        "m": v((8, L), F32),
        "l": v((8, L), F32),
        "acc": v((W, L), F32),
        "att": v((nt, W, L), BF16),
        "mid": v((L, D), F32),
        "u2": v((L, D), F32),
        "r2": v((L, 1), F32),
        "n2low": v((L, D), BF16),
        "upw": v((L, F), F32),
        "actlow": v((L, F), BF16),
        "ffp": v((L, D), BF16),
        "ffr": v((2, nt - 1, R, D), BF16),
        "blow": v((L, D), BF16),
        "lg": v((nt * 32, L), BF16),
        "oglow": v((L, D), BF16),
        "ug": v((L, F), BF16),
        "n2p": v((L, D), BF16),
        "n2r": v((2, nt - 1, R, D), BF16),
        "n2g": v((L, D), BF16),
        "dasrc": v((2, nt, R, W), BF16),
        "datok": v((2, nt, R, W), BF16),
        "dq": v((W, L), F32),
        "dk": v((W, L), F32),
        "dv": v((W, L), F32),
        "dp": v((3, W, L), BF16),
        "ngp": v((L, D), BF16),
        "ngr": v((2, nt - 1, R, D), BF16),
        "ngg": v((L, D), BF16),
        "va": v((GROUP, 32, D), BF16),
        "vb": v((GROUP, s.tail, D), BF16),
        "ent": v((nb, 8, 128), F32),
        "va_sum": v((32, D), F32),
        "vb_sum": v((s.tail, D), F32),
        "gsrc": v((s.rows, D), BF16),
        "gout": v((s.rows, D), BF16),
    }
    dma = pltpu.SemaphoreType.DMA
    out["loads"] = dma((15,))
    out["stores"] = dma((8,))
    for name in ("zmask", "zgate", "zow", "zowr", "zatt", "zff", "zblk", "zn2", "zn2g", "zda", "zng", "zngg"):
        out[name + "_s"] = dma((2 * (nt - 1),))
        out[name + "_r"] = dma((2 * (nt - 1),))
    for name in ("kv", "q", "da0", "da1", "st"):
        for part in ("_s", "_r", "_rs", "_rr"):
            out[name + part] = dma((s.half,))
    for name, count in (("cnt", nb), ("ent", nb), ("va", GROUP), ("vb", GROUP)):
        out[name + "_s"] = dma((count - 1,))
        out[name + "_r"] = dma((count - 1,))
    if s.groups > 1:
        for name, rows in (("va2", 32), ("vb2", s.tail)):
            out[name] = v((s.groups, rows, D), BF16)
            out[name + "_s"] = dma((s.groups - 1,))
            out[name + "_r"] = dma((s.groups - 1,))
    for i, rows in enumerate(s.sizes):
        hr = rows // 2
        qr = hr // 4
        out["core%d" % i] = v((hr, D), BF16)
        out["quart%d" % i] = v((3, qr, D), BF16)
        if s.groups > 1:
            out["sup%d" % i] = v((s.groups, qr, D), BF16)
            out["sup%d_s" % i] = dma((s.groups - 1,))
            out["sup%d_r" % i] = dma((s.groups - 1,))
        out["gs%d" % i] = dma((8,))
        out["gr%d" % i] = dma((8,))
    return out


def main_kernel(s, names, *refs):
    (
        patches,
        windows_in,
        leads_in,
        table,
        gain1,
        bias1,
        qkv,
        out_weight,
        gain2,
        bias2,
        up,
        down,
        gate,
        pixel_mask,
        cotangent,
        o_block,
        o_hidden,
        o_grads,
        o_va,
        o_vb,
    ) = refs[:20]
    k = SimpleNamespace(**dict(zip(names, refs[20:])))
    sem = vars(k)
    L, D, W, F, H, T, R, nb, nt = s.L, s.D, s.W, s.F, s.H, s.T, s.R, s.nb, s.nt
    b = lax.axis_index("blk")
    t = lax.axis_index("tp")
    core = lax.rem(b, 2)
    pair = b // 2
    sib = b + 1 - 2 * core

    def z_peer(j):
        return lax.rem(t + j, nt)

    def z_from(j):
        return lax.rem(t + nt - j, nt)

    def remote(src, dst, send, recv, device):
        return pltpu.make_async_remote_copy(
            src, dst, send, recv, device_id=device, device_id_type=MESH
        )

    def z_copy(name, j, src, dst, h=0):
        i = h * (nt - 1) + j - 1
        return remote(src, dst, sem[name + "_s"].at[i], sem[name + "_r"].at[i], (b, z_peer(j)))

    def half(h):
        return pl.ds(h * T, T)

    def piece(h, tt):
        return pl.ds(pl.multiple_of(h * T + tt * R, R), R)

    def ag_copy(name, at, i, dst_band):
        return remote(at(b), at(b), sem[name + "_s"].at[i], sem[name + "_r"].at[i], (dst_band, t))

    def relay_copy(name, at, i, band):
        return remote(at(band), at(band), sem[name + "_rs"].at[i], sem[name + "_rr"].at[i], (sib, t))

    def band_same(i):
        return lax.rem(b + nb - 2 * i, nb)

    def band_sib(i):
        return lax.rem(sib + nb - 2 * i, nb)

    def ag_start(name, at):
        @pl.loop(1, s.half)
        def _(i):
            ag_copy(name, at, i, lax.rem(b + 2 * i, nb)).start()

        relay_copy(name, at, 0, b).start()

    def ag_relay(name, at, i):
        band = band_same(i)
        remote(at(band), at(band), sem[name + "_s"].at[i], sem[name + "_r"].at[i], (sib, t)).wait_recv()
        relay_copy(name, at, i, band).start()

    def ag_wait_relay(name, at, i):
        relay_copy(name, at, i, band_sib(i)).wait_recv()

    def ag_finish(name, at):
        @pl.loop(1, s.half)
        def _(i):
            ag_copy(name, at, i, sib).wait_send()

        @pl.loop(0, s.half)
        def _(i):
            relay_copy(name, at, i, b).wait_send()

    every = (nb, b, lambda i: i)
    near = (GROUP, lax.rem(b, GROUP), lambda i: b // GROUP * GROUP + i)
    far = (s.groups, b // GROUP, lambda i: i * GROUP + lax.rem(b, GROUP))

    def swap_copy(name, members, i, slot, to):
        ref = sem[name]
        return remote(
            ref.at[slot],
            ref.at[slot],
            sem[name + "_s"].at[i - 1],
            sem[name + "_r"].at[i - 1],
            (members[2](to), t),
        )

    def swap_start(name, members):
        count, me, _ = members

        @pl.loop(1, count)
        def _(i):
            swap_copy(name, members, i, me, lax.rem(me + i, count)).start()

    def swap_wait(name, members):
        count, me, _ = members

        @pl.loop(1, count)
        def _(i):
            peer = lax.rem(me + count - i, count)
            swap_copy(name, members, i, peer, peer).wait_recv()

    def swap_finish(name, members):
        count, me, _ = members

        @pl.loop(1, count)
        def _(i):
            swap_copy(name, members, i, me, lax.rem(me + i, count)).wait_send()

    def slots_sum(ref, count):
        return lax.fori_loop(
            1, count, lambda i, acc: acc + ref[i].astype(F32), ref[0].astype(F32)
        )

    def swap_sum(name):
        swap_wait(name, near)
        out = slots_sum(sem[name], GROUP)
        if s.groups > 1:
            sem[name + "2"][far[1]] = out.astype(BF16)
            swap_start(name + "2", far)
            swap_wait(name + "2", far)
            out = slots_sum(sem[name + "2"], s.groups)
            swap_finish(name + "2", far)
        swap_finish(name, near)
        return out

    def rs_start(name, h, part, recv):
        for j in range(1, nt):
            z_copy(name, j, part.at[piece(h, z_peer(j))], recv.at[h, j - 1], h).start()

    def rs_sum(name, h, part, recv):
        acc = part[piece(h, t), :].astype(F32)
        for j in range(1, nt):
            z_copy(name, j, part.at[piece(h, z_from(j))], recv.at[h, j - 1], h).wait_recv()
            acc = acc + recv[h, j - 1].astype(F32)
        return acc

    def rs_finish(name, part, recv):
        for h in range(2):
            for j in range(1, nt):
                z_copy(name, j, part.at[piece(h, z_peer(j))], recv.at[h, j - 1], h).wait_send()

    def gather_start(name, h, ref):
        for j in range(1, nt):
            z_copy(name, j, ref.at[piece(h, t)], ref.at[piece(h, t)], h).start()

    def gather_wait(name, h, ref):
        for j in range(1, nt):
            rows = piece(h, z_from(j))
            z_copy(name, j, ref.at[rows], ref.at[rows], h).wait_recv()

    def gather_finish(name, ref):
        for h in range(2):
            for j in range(1, nt):
                z_copy(name, j, ref.at[piece(h, t)], ref.at[piece(h, t)], h).wait_send()

    quarter = lax.rem(pair, 4)
    first_pair = pair - quarter
    group = pair // 4
    low_peer = quarter + 1 - 2 * lax.rem(quarter, 2)
    high_peer = lax.rem(quarter + 2, 4)
    first = low_peer * (1 - core) + high_peer * core
    second = low_peer * core + high_peer * (1 - core)
    across = lax.rem(low_peer + 2, 4)

    def g_rows(i, q):
        hr = s.sizes[i] // 2
        qr = hr // 4
        return pl.ds(pl.multiple_of(s.bases[i] + core * hr + q * qr, 16), qr)

    def g_half(i, c):
        hr = s.sizes[i] // 2
        return pl.ds(pl.multiple_of(s.bases[i] + c * hr, 16), hr)

    def q_rows(i, q):
        qr = s.sizes[i] // 8
        return pl.ds(pl.multiple_of(q * qr, 16), qr)

    def g_copy(i, slot, src, dst, q):
        dev = ((first_pair + q) * 2 + core, t)
        return remote(src, dst, sem["gs%d" % i].at[slot], sem["gr%d" % i].at[slot], dev)

    def sib_copy(i, slot, src, dst):
        return remote(src, dst, sem["gs%d" % i].at[slot], sem["gr%d" % i].at[slot], (sib, t))

    def c1_copy(i):
        return sib_copy(i, 0, k.gsrc.at[g_half(i, 1 - core)], sem["core%d" % i])

    def rs_copies(i):
        hs = sem["core%d" % i]
        land = sem["quart%d" % i]
        return (
            g_copy(i, 1, hs.at[q_rows(i, first)], land.at[0], first),
            g_copy(i, 2, hs.at[q_rows(i, across)], land.at[1], first),
        )

    def rs_copy_b(i):
        return g_copy(i, 3, sem["core%d" % i].at[q_rows(i, second)], sem["quart%d" % i].at[2], second)

    def out_copy(i, slot, q, to):
        rows = g_rows(i, q)
        return g_copy(i, slot, k.gout.at[rows], k.gout.at[rows], to)

    def c2_copy(i, c):
        rows = g_half(i, c)
        return sib_copy(i, 7, k.gout.at[rows], k.gout.at[rows])

    def sup_copy(i, j):
        ref = sem["sup%d" % i]
        dev = ((lax.rem(group + j, s.groups) * 4 + quarter) * 2 + core, t)
        return remote(ref.at[group], ref.at[group], sem["sup%d_s" % i].at[j - 1], sem["sup%d_r" % i].at[j - 1], dev)

    def grads1(i):
        c1_copy(i).start()

    def grads2(i):
        c1_copy(i).wait()
        hs = sem["core%d" % i]
        hs[...] = (k.gsrc[g_half(i, core), :].astype(F32) + hs[...].astype(F32)).astype(BF16)
        for copy in rs_copies(i):
            copy.start()

    def grads3(i):
        for copy in rs_copies(i):
            copy.wait()
        hs = sem["core%d" % i]
        rows = q_rows(i, second)
        hs[rows, :] = (hs[rows, :].astype(F32) + sem["quart%d" % i][1].astype(F32)).astype(BF16)
        rs_copy_b(i).start()

    def grads4(i):
        rs_copy_b(i).wait()
        land = sem["quart%d" % i]
        acc = sem["core%d" % i][q_rows(i, quarter), :].astype(F32)
        acc = acc + land[0].astype(F32) + land[2].astype(F32)
        if s.groups > 1:
            ref = sem["sup%d" % i]
            ref[group] = acc.astype(BF16)
            for j in range(1, s.groups):
                sup_copy(i, j).start()
            for j in range(1, s.groups):
                sup_copy(i, j).wait()
            acc = ref[0].astype(F32)
            for g in range(1, s.groups):
                acc = acc + ref[g].astype(F32)
        k.gout[g_rows(i, quarter), :] = acc.astype(BF16)
        out_copy(i, 4, quarter, second).start()

    def grads5(i):
        out_copy(i, 4, quarter, second).wait_send()
        out_copy(i, 4, second, second).wait_recv()
        out_copy(i, 5, quarter, first).start()
        out_copy(i, 6, second, first).start()

    def grads6(i):
        out_copy(i, 5, quarter, first).wait_send()
        out_copy(i, 6, second, first).wait_send()
        out_copy(i, 5, first, first).wait_recv()
        out_copy(i, 6, across, first).wait_recv()
        c2_copy(i, core).start()

    def grads_store(i):
        rows = pl.ds(s.bases[i], s.sizes[i])
        return pltpu.make_async_copy(k.gout.at[rows], o_grads.at[rows], k.stores.at[i])

    def grads7(i):
        c2_copy(i, core).wait_send()
        c2_copy(i, 1 - core).wait_recv()
        grads_store(i).start()

    def load(i, src, dst):
        return pltpu.make_async_copy(src, dst, k.loads.at[i])

    first_loads = [
        load(0, patches, k.patches),
        load(1, leads_in, k.lead_index),
        load(2, table, k.table),
        load(3, gain1, k.gain1),
        load(4, bias1, k.bias1),
    ]
    ow_load = load(5, out_weight, k.ow.at[t])
    small_loads = [
        load(6, pixel_mask, k.pix),
        load(7, gate, k.head),
        load(8, windows_in, k.windows),
    ]
    qkv_load = load(9, qkv, k.qkv)
    late_loads = [
        load(10, gain2, k.gain2),
        load(11, bias2, k.bias2),
        load(12, up, k.up),
        load(13, down, k.down),
        load(14, cotangent, k.cot),
    ]
    for copy in first_loads + small_loads + [qkv_load, ow_load]:
        copy.start()
    barrier = pltpu.get_barrier_semaphore()

    @pl.loop(1, nb)
    def _(i):
        pl.semaphore_signal(barrier, inc=1, device_id=(lax.rem(b + i, nb), t), device_id_type=MESH)

    for j in range(1, nt):
        pl.semaphore_signal(barrier, inc=1, device_id=(b, z_peer(j)), device_id_type=MESH)

    for copy in first_loads:
        copy.wait()
    lead_hot = lax.broadcasted_iota(jnp.int32, (s.leads, L), 0) == row_of(k.lead_index)
    lead_hot = lead_hot.astype(F32).astype(BF16)
    hidden = k.patches[...] + mm_tn(lead_hot, k.table[...])
    unit1, inverse1 = norm_stats(hidden)
    k.u1[...] = unit1
    k.r1[...] = inverse1
    k.mid[...] = hidden
    k.normed[...] = (unit1 * row_of(k.gain1) + row_of(k.bias1)).astype(BF16)
    for copy in small_loads:
        copy.wait()
    compact = [k.head[e].astype(F32) for e in range(3)] + [jnp.zeros((4, D), F32)]
    k.gatec[t] = jnp.concatenate(compact, axis=0).astype(BF16)
    k.mask[t] = jnp.concatenate([k.pix[...].astype(F32), jnp.zeros((4, L), F32)], axis=0)
    hw = W // 2

    def ow_half(tt, c):
        return k.ow.at[tt, pl.ds(pl.multiple_of(c * hw, hw), hw)]

    def ow_relay(j, tt, c):
        return remote(ow_half(tt, c), ow_half(tt, c), k.zowr_s.at[j - 1], k.zowr_r.at[j - 1], (sib, t))

    qkv_load.wait()

    def project(c):
        return mm_nt(k.qkv[c], k.normed[...])

    k.kv[b, 0:W, :] = project(1).astype(BF16)
    k.kv[b, W : 2 * W, :] = project(2).astype(BF16)
    ow_load.wait()
    pl.semaphore_wait(barrier, nb - 1 + nt - 1)

    def kv_at(band):
        return k.kv.at[band]

    ag_start("kv", kv_at)
    for j in range(1, nt):
        z_copy("zmask", j, k.mask.at[t], k.mask.at[t]).start()
        z_copy("zow", j, ow_half(t, core), ow_half(t, core)).start()
        z_copy("zgate", j, k.gatec.at[t], k.gatec.at[t]).start()
    for copy in late_loads:
        copy.start()
    k.qd[b, 0:W, :] = (project(0).astype(BF16).astype(F32) * SCALE).astype(BF16)

    k.ids[...] = k.windows[...].reshape(nb, L).astype(F32)

    def id_row(band):
        return k.ids[pl.ds(band, 1), :]

    def id_column(band):
        return jnp.transpose(jnp.broadcast_to(id_row(band), (128, L)))[:, 0:1]

    def head(h):
        return pl.ds(h * HEAD_DIM, HEAD_DIM)

    def value_head(h):
        return pl.ds(W + h * HEAD_DIM, HEAD_DIM)

    k.m[...] = jnp.full((8, L), MASKED, F32)
    k.l[...] = jnp.zeros((8, L), F32)
    k.acc[...] = jnp.zeros((W, L), F32)

    def forward_bands(bands):
        tiles = [(h, i) for h in range(H) for i in range(len(bands))]
        allowed = [id_column(band) == id_row(b) for band in bands]
        scores = {
            (h, i): jnp.where(
                allowed[i], mm_tn(k.kv[bands[i], head(h), :], k.qd[b, head(h), :]), MASKED
            )
            for h, i in tiles
        }
        old_high = [k.m[h : h + 1, :] for h in range(H)]
        sums = [k.l[h : h + 1, :] for h in range(H)]
        outs = [k.acc[head(h), :] for h in range(H)]
        high = list(old_high)
        for h, i in tiles:
            high[h] = jnp.maximum(high[h], jnp.max(scores[h, i], axis=0, keepdims=True))
        weights = {(h, i): jnp.exp(scores[h, i] - high[h]) for h, i in tiles}
        factor = [jnp.exp(x - y) for x, y in zip(old_high, high)]
        outs = [x * f for x, f in zip(outs, factor)]
        sums = [x * f for x, f in zip(sums, factor)]
        for h, i in tiles:
            outs[h] += mm_nn(k.kv[bands[i], value_head(h), :], weights[h, i].astype(BF16))
            sums[h] += jnp.sum(weights[h, i], axis=0, keepdims=True)
        for h in range(H):
            k.m[h : h + 1, :] = high[h]
            k.l[h : h + 1, :] = sums[h]
            k.acc[head(h), :] = outs[h]

    ag_wait_relay("kv", kv_at, 0)
    forward_bands([b, sib])
    for j in range(1, nt):
        z_copy("zmask", j, k.mask.at[t], k.mask.at[z_from(j)]).wait_recv()
    k.cnt[b] = jnp.broadcast_to(total(jnp.sum(k.mask[...], axis=0)), (8, 128))
    swap_start("cnt", every)

    @pl.loop(1, s.half)
    def _(i):
        ag_relay("kv", kv_at, i)
        ag_wait_relay("kv", kv_at, i)
        forward_bands([band_same(i), band_sib(i)])

    for h in range(H):
        att = k.acc[head(h), :] / k.l[h : h + 1, :]
        k.acc[head(h), :] = att
        k.att[t, head(h), :] = att.astype(BF16)
        k.st[b, h : h + 1, :] = k.m[h : h + 1, :] + jnp.log(k.l[h : h + 1, :])

    def att_half(tt, h):
        return k.att.at[tt, :, half(h)]

    for h in range(2):
        for j in range(1, nt):
            z_copy("zatt", j, att_half(t, h), att_half(t, h), h).start()

    def q_at(band):
        return k.qd.at[band, pl.ds(0, W)]

    def da_at(h):
        return lambda band: k.qd.at[band, pl.ds(W, W), half(h)]

    def st_at(band):
        return k.st.at[band]

    ag_start("q", q_at)
    for j in range(1, nt):
        src = z_from(j)
        z_copy("zow", j, ow_half(src, core), ow_half(src, core)).wait_recv()
        ow_relay(j, src, core).start()
    for copy in late_loads:
        copy.wait()
    for j in range(1, nt):
        ow_relay(j, z_from(j), 1 - core).wait_recv()

    for h in range(2):
        for j in range(1, nt):
            z_copy("zatt", j, att_half(z_from(j), h), att_half(z_from(j), h), h).wait_recv()
        rows = half(h)
        middle = k.mid[rows, :] + mm_tn(
            k.att[:, :, half(h)].reshape(nt * W, T), k.ow[...].reshape(nt * W, D)
        )
        k.mid[rows, :] = middle
        unit2, inverse2 = norm_stats(middle)
        k.u2[rows, :] = unit2
        k.r2[rows, :] = inverse2
        k.n2low[rows, :] = (unit2 * row_of(k.gain2) + row_of(k.bias2)).astype(BF16)
        upward = mm_nn(k.n2low[rows, :], k.up[...])
        k.upw[rows, :] = upward
        k.actlow[rows, :] = (0.5 * upward * (1.0 + lax.erf(upward * INV_SQRT2))).astype(BF16)
        k.ffp[rows, :] = mm_nn(k.actlow[rows, :], k.down[...]).astype(BF16)
        rs_start("zff", h, k.ffp, k.ffr)
    upward = k.upw[...]
    k.upw[...] = 0.5 * (1.0 + lax.erf(upward * INV_SQRT2)) + upward * (
        jnp.exp(-0.5 * upward * upward) * INV_SQRT_2PI
    )
    for j in range(1, nt):
        z_copy("zgate", j, k.gatec.at[t], k.gatec.at[z_from(j)]).wait_recv()
    for tt in range(nt):
        x = k.gatec[tt].astype(F32)
        pad = jnp.zeros((4, D), F32)
        parts = []
        for e in range(3):
            parts += [x[4 * e : 4 * e + 4], pad]
        k.gate[tt * 32 : (tt + 1) * 32, :] = jnp.concatenate(parts + [pad, pad], axis=0).astype(BF16)
    swap_wait("cnt", every)
    pixel_count = jnp.sum(k.cnt[...], axis=0)[0:1, 0:1]
    for h in range(2):
        block_piece = k.mid[piece(h, t), :] + rs_sum("zff", h, k.ffp, k.ffr)
        k.blow[piece(h, t), :] = block_piece.astype(BF16)
        gather_start("zblk", h, k.blow)

    @pl.loop(1, s.half)
    def _(i):
        ag_relay("q", q_at, i)

    entropy_sum = jnp.zeros((1, 1), F32)
    for h in range(2):
        rows = half(h)
        gather_wait("zblk", h, k.blow)
        logits = mm_nt(k.gate[...], k.blow[rows, :]).reshape(nt, 4, 8, T)
        parts = [logits[:, e] for e in range(3)]
        high = jnp.maximum(jnp.maximum(parts[0], parts[1]), parts[2])
        logs = jnp.log(sum(jnp.exp(x - high) for x in parts))
        log_probs = [x - high - logs for x in parts]
        probs = [jnp.exp(x) for x in log_probs]
        entropy = -sum(p * x for p, x in zip(probs, log_probs))
        mask = k.mask[:, :, half(h)]
        entropy_sum += total(jnp.sum(mask * entropy, axis=0))
        weight = mask * (float(s.pixels) / pixel_count)[None]
        grads = [-p * (x + entropy) * weight for p, x in zip(probs, log_probs)]
        grads.append(jnp.zeros((nt, 8, T), F32))
        k.lg[:, half(h)] = jnp.stack(grads, axis=1).reshape(nt * 32, T).astype(BF16)
        out_grad = k.cot[rows, :] + mm_tn(k.lg[:, half(h)], k.gate[...])
        k.cot[rows, :] = out_grad
        k.oglow[rows, :] = out_grad.astype(BF16)
        k.ug[rows, :] = (mm_nt(k.oglow[rows, :], k.down[...]) * k.upw[rows, :]).astype(BF16)
        k.n2p[rows, :] = mm_nt(k.ug[rows, :], k.up[...]).astype(BF16)
        rs_start("zn2", h, k.n2p, k.n2r)
    block_copy = pltpu.make_async_copy(k.blow, o_block, k.stores.at[4])
    block_copy.start()
    own_lg = k.lg[pl.ds(pl.multiple_of(t * 32, 32), 32), :]
    k.va[near[1]] = mm_nn(own_lg, k.blow[...]).astype(BF16)
    k.ent[b] = jnp.broadcast_to(entropy_sum / pixel_count, (8, 128))
    swap_start("va", near)
    swap_start("ent", every)
    k.gsrc[0:F, :] = mm_tn(k.actlow[...], k.oglow[...]).astype(BF16)
    grads1(0)
    k.gsrc[F : F + D, :] = mm_tn(k.n2low[...], k.ug[...]).astype(BF16)
    grads1(1)

    def middle_backward(n2_grad, rows):
        return k.cot[rows, :] + norm_backward(n2_grad, k.u2[rows, :], k.r2[rows, :], row_of(k.gain2))

    grads2(0)
    for h in range(2):
        rows = piece(h, t)
        n2_low = rs_sum("zn2", h, k.n2p, k.n2r).astype(BF16)
        k.n2g[rows, :] = n2_low
        low_piece = middle_backward(n2_low.astype(F32), rows).astype(BF16)
        for tt in range(nt):
            k.dasrc[h, tt] = mm_nt(low_piece, k.ow[tt]).astype(BF16)
        for j in range(1, nt):
            z_copy("zda", j, k.dasrc.at[h, z_peer(j)], k.datok.at[h, t], h).start()
        k.datok[h, t] = k.dasrc[h, t]
        if h == 0:
            grads2(1)
            grads3(0)
    for h in range(2):
        gather_start("zn2g", h, k.n2g)
    for h in range(2):
        for j in range(1, nt):
            z_copy("zda", j, k.dasrc.at[h, z_peer(j)], k.datok.at[h, z_from(j)], h).wait_recv()
        att_grad = jnp.transpose(k.datok[h].reshape(T, W).astype(F32)).astype(BF16)
        k.qd[b, W : 2 * W, half(h)] = att_grad
        ag_start("da%d" % h, da_at(h))
        weighted = att_grad.astype(F32) * k.acc[:, half(h)]
        for i in range(H):
            k.st[b, H + i : H + i + 1, half(h)] = jnp.sum(
                weighted[i * HEAD_DIM : (i + 1) * HEAD_DIM], axis=0, keepdims=True
            )
    ag_start("st", st_at)
    grads3(1)
    k.dq[...] = jnp.zeros((W, L), F32)
    k.dk[...] = jnp.zeros((W, L), F32)
    k.dv[...] = jnp.zeros((W, L), F32)
    my_column = id_column(b)

    def score_grads(allowed, scores, dots, stats):
        probs = {
            (h, i): jnp.exp(jnp.where(allowed[i], x, MASKED) - stats[i][h : h + 1])
            for (h, i), x in scores.items()
        }
        grads = {
            (h, i): (x * (dots[h, i] - stats[i][H + h : H + h + 1])).astype(BF16)
            for (h, i), x in probs.items()
        }
        return probs, grads

    @pl.loop(0, s.half)
    def _(step):
        bands = [2 * step, 2 * step + 1]
        tiles = [(h, i) for h in range(H) for i in range(2)]
        allowed = [id_column(band) == id_row(b) for band in bands]
        scores = {(h, i): mm_tn(k.kv[bands[i], head(h), :], k.qd[b, head(h), :]) for h, i in tiles}
        dots = {
            (h, i): mm_tn(k.kv[bands[i], value_head(h), :], k.qd[b, value_head(h), :]) for h, i in tiles
        }
        outs = [k.dq[head(h), :] for h in range(H)]
        _, grads = score_grads(allowed, scores, dots, [k.st[b]] * 2)
        for h, i in tiles:
            outs[h] += mm_nn(k.kv[bands[i], head(h), :], grads[h, i])
        for h in range(H):
            k.dq[head(h), :] = outs[h]

    grads4(0)
    k.dp[0] = (k.dq[...] * SCALE).astype(BF16)
    base = s.bases[2]
    for h in range(2):
        gather_wait("zn2g", h, k.n2g)
    n2_grad = k.n2g[...].astype(F32)
    gain2_grad = jnp.sum(n2_grad * k.u2[...], axis=0, keepdims=True)
    bias2_grad = jnp.sum(n2_grad, axis=0, keepdims=True)
    middle_grad = middle_backward(n2_grad, pl.ds(0, L))
    k.cot[...] = middle_grad
    k.gsrc[base : base + W, :] = mm_nn(k.att[t], middle_grad.astype(BF16)).astype(BF16)
    k.gsrc[base + W : base + 2 * W, :] = mm_nn(k.dp[0], k.normed[...]).astype(BF16)
    grads1(2)
    grads4(1)

    @pl.loop(1, s.half)
    def _(i):
        ag_wait_relay("q", q_at, i)

    ag_wait_relay("q", q_at, 0)

    def backward_bands(bands):
        tiles = [(h, i) for h in range(H) for i in range(len(bands))]
        allowed = [my_column == id_row(band) for band in bands]
        scores = {(h, i): mm_tn(k.kv[b, head(h), :], k.qd[bands[i], head(h), :]) for h, i in tiles}
        dots = {
            (h, i): mm_tn(k.kv[b, value_head(h), :], k.qd[bands[i], value_head(h), :]) for h, i in tiles
        }
        key_outs = [k.dk[head(h), :] for h in range(H)]
        value_outs = [k.dv[head(h), :] for h in range(H)]
        probs, grads = score_grads(allowed, scores, dots, [k.st[band] for band in bands])
        for h, i in tiles:
            key_outs[h] += mm_nt(k.qd[bands[i], head(h), :], grads[h, i])
            value_outs[h] += mm_nt(k.qd[bands[i], value_head(h), :], probs[h, i].astype(BF16))
        for h in range(H):
            k.dk[head(h), :] = key_outs[h]
            k.dv[head(h), :] = value_outs[h]

    def backward_loop(start, stop):
        @pl.loop(start, stop)
        def _(i):
            @pl.when(i > 0)
            def _():
                ag_relay("da0", da_at(0), i)
                ag_relay("da1", da_at(1), i)
                ag_relay("st", st_at, i)

            ag_wait_relay("da0", da_at(0), i)
            ag_wait_relay("da1", da_at(1), i)
            ag_wait_relay("st", st_at, i)
            backward_bands([band_same(i), band_sib(i)])

    backward_loop(0, s.half // 2)
    grads2(2)
    grads5(0)
    backward_loop(s.half // 2, s.half)
    k.dp[1] = k.dk[...].astype(BF16)
    k.dp[2] = k.dv[...].astype(BF16)
    for h in range(2):
        k.ngp[half(h), :] = mm_tn(
            k.dp[:, :, half(h)].reshape(3 * W, T), k.qkv[...].reshape(3 * W, D)
        ).astype(BF16)
        rs_start("zng", h, k.ngp, k.ngr)
    base = s.bases[3]
    k.gsrc[base : base + 2 * W, :] = mm_nn(k.dp[1:3].reshape(2 * W, L), k.normed[...]).astype(BF16)
    grads1(3)
    grads5(1)
    grads3(2)
    grads2(3)
    for h in range(2):
        k.ngg[piece(h, t), :] = rs_sum("zng", h, k.ngp, k.ngr).astype(BF16)
        gather_start("zngg", h, k.ngg)
        if h == 0:
            grads6(0)
            grads4(2)
    grads3(3)
    grads6(1)
    grads5(2)
    grads4(3)
    grads7(0)
    grads6(2)
    grads5(3)
    for h in range(2):
        gather_wait("zngg", h, k.ngg)
    n1_grad = k.ngg[...].astype(F32)
    unit1 = k.u1[...]
    gain1_grad = jnp.sum(n1_grad * unit1, axis=0, keepdims=True)
    bias1_grad = jnp.sum(n1_grad, axis=0, keepdims=True)
    hidden_grad = k.cot[...] + norm_backward(n1_grad, unit1, k.r1[...], row_of(k.gain1))
    k.patches[...] = hidden_grad
    hidden_copy = pltpu.make_async_copy(k.patches, o_hidden, k.stores.at[5])
    hidden_copy.start()
    coarse = hidden_grad.astype(BF16)
    fine = (hidden_grad - coarse.astype(F32)).astype(BF16)
    tail = [
        mm_nn(lead_hot, coarse) + mm_nn(lead_hot, fine),
        gain1_grad,
        bias1_grad,
        gain2_grad,
        bias2_grad,
        jnp.zeros((s.tail - s.leads - 4, D), F32),
    ]
    k.vb[near[1]] = jnp.concatenate(tail, axis=0).astype(BF16)
    swap_start("vb", near)
    grads7(1)
    grads6(3)
    grads7(2)
    swap_wait("ent", every)
    k.va_sum[...] = swap_sum("va")
    k.va_sum[24:32, 0:128] = jnp.sum(k.ent[...], axis=0)
    va_copy = pltpu.make_async_copy(k.va_sum, o_va, k.stores.at[6])
    va_copy.start()
    grads7(3)
    k.vb_sum[...] = swap_sum("vb")
    vb_copy = pltpu.make_async_copy(k.vb_sum, o_vb, k.stores.at[7])
    vb_copy.start()

    for j in range(1, nt):
        z_copy("zmask", j, k.mask.at[t], k.mask.at[t]).wait_send()
        z_copy("zgate", j, k.gatec.at[t], k.gatec.at[t]).wait_send()
        z_copy("zow", j, ow_half(t, core), ow_half(t, core)).wait_send()
        ow_relay(j, t, core).wait_send()
        for h in range(2):
            z_copy("zatt", j, att_half(t, h), att_half(t, h), h).wait_send()
            z_copy("zda", j, k.dasrc.at[h, z_peer(j)], k.datok.at[h, t], h).wait_send()
    rs_finish("zff", k.ffp, k.ffr)
    gather_finish("zblk", k.blow)
    rs_finish("zn2", k.n2p, k.n2r)
    gather_finish("zn2g", k.n2g)
    rs_finish("zng", k.ngp, k.ngr)
    gather_finish("zngg", k.ngg)
    for name, at in (("kv", kv_at), ("q", q_at), ("da0", da_at(0)), ("da1", da_at(1)), ("st", st_at)):
        ag_finish(name, at)
    swap_finish("cnt", every)
    swap_finish("ent", every)
    for i in range(4):
        grads_store(i).wait()
    for copy in (block_copy, hidden_copy, va_copy, vb_copy):
        copy.wait()


def last_kernel(
    s, cuts, block, hidden, grads, va, vb,
    o_block, o_hidden, o_qkv, o_out, o_up, o_down, o_pen, o_lead, o_g1, o_b1, o_g2, o_b2, o_gate,
    low, wide, low_block, wide_block, keep, load_sem, store_sem,
):
    outs = {"down": o_down, "up": o_up, "out": o_out, "q": o_qkv.at[0], "k": o_qkv.at[1], "v": o_qkv.at[2]}
    loads = [
        pltpu.make_async_copy(block, low_block, load_sem.at[0]),
        pltpu.make_async_copy(hidden, keep, load_sem.at[1]),
    ]
    stores = [
        pltpu.make_async_copy(wide_block, o_block, store_sem.at[0]),
        pltpu.make_async_copy(keep, o_hidden, store_sem.at[1]),
    ]
    for i, (row, name, start, size) in enumerate(cuts):
        rows = pl.ds(row, size)
        loads.append(pltpu.make_async_copy(grads.at[rows], low.at[rows], load_sem.at[i + 2]))
        stores.append(
            pltpu.make_async_copy(wide.at[rows], outs[name].at[pl.ds(start, size)], store_sem.at[i + 2])
        )
    for copy in loads:
        copy.start()
    loads[0].wait()
    wide_block[...] = low_block[...].astype(F32)
    stores[0].start()
    loads[1].wait()
    stores[1].start()
    for i, (row, name, start, size) in enumerate(cuts):
        loads[i + 2].wait()
        rows = pl.ds(row, size)
        wide[rows, :] = low[rows, :].astype(F32)
        stores[i + 2].start()
    small = va[...]
    for e in range(3):
        o_gate[e] = small[8 * e : 8 * e + 4]
    o_pen[...] = small[24:25, 0:1]
    tail = vb[...]
    o_lead[...] = tail[0 : s.leads]
    o_g1[...] = tail[s.leads].reshape(s.D)
    o_b1[...] = tail[s.leads + 1].reshape(s.D)
    o_g2[...] = tail[s.leads + 2].reshape(s.D)
    o_b2[...] = tail[s.leads + 3].reshape(s.D)
    for copy in stores:
        copy.wait()


def local(
    nb,
    nt,
    patches,
    window_ids,
    lead_index,
    lead_table,
    attention_gain,
    attention_bias,
    query_key_value,
    out_weight,
    feedforward_gain,
    feedforward_bias,
    up_weight,
    down_weight,
    gate_head,
    pixel_mask,
    cotangent,
):
    L, D = patches.shape
    leads = lead_table.shape[0]
    W = out_weight.shape[0]
    F = up_weight.shape[1]
    s = dims_of(nb, nt, L, D, W, F, leads, L * nb * pixel_mask.shape[0] * nt)
    scratch = scratch_of(s)
    vm = pl.BlockSpec(memory_space=pltpu.VMEM)
    block, hidden, grads, va, vb = pl.pallas_call(
        partial(main_kernel, s, tuple(scratch)),
        out_shape=(
            jax.ShapeDtypeStruct((L, D), BF16),
            jax.ShapeDtypeStruct((L, D), F32),
            jax.ShapeDtypeStruct((s.rows, D), BF16),
            jax.ShapeDtypeStruct((32, D), F32),
            jax.ShapeDtypeStruct((s.tail, D), F32),
        ),
        in_specs=[pl.BlockSpec(memory_space=pltpu.HBM)] * 15,
        out_specs=(pl.BlockSpec(memory_space=pl.ANY),) * 5,
        scratch_shapes=list(scratch.values()),
        compiler_params=pltpu.CompilerParams(
            collective_id=0,
            has_side_effects=True,
            vmem_limit_bytes=VMEM_LIMIT,
        ),
        cost_estimate=pl.CostEstimate(
            flops=2 * s.rows * D * L * 3 + 14 * L * nb * L * W, bytes_accessed=16 * 2**20, transcendentals=0
        ),
        name="block_step",
    )(
        patches,
        window_ids,
        lead_index,
        lead_table,
        attention_gain,
        attention_bias,
        jnp.transpose(query_key_value, (0, 2, 1)),
        out_weight,
        feedforward_gain,
        feedforward_bias,
        up_weight,
        down_weight,
        gate_head,
        pixel_mask,
        cotangent,
    )
    vec = jax.ShapeDtypeStruct((D,), F32)
    cuts = []
    row = 0
    for name, size in (("down", F), ("up", D), ("out", W), ("q", W), ("k", W), ("v", W)):
        for start in range(0, size, 256):
            cuts.append((row + start, name, start, min(256, size - start)))
        row += size
    hbm = pl.BlockSpec(memory_space=pl.ANY)
    wide, high, qkv_grad, out_grad, up_grad, down_grad, pen, lead, g1, b1, g2, b2, gates = pl.pallas_call(
        partial(last_kernel, s, cuts),
        out_shape=(
            jax.ShapeDtypeStruct((L, D), F32),
            jax.ShapeDtypeStruct((L, D), F32),
            jax.ShapeDtypeStruct((3, W, D), F32),
            jax.ShapeDtypeStruct((W, D), F32),
            jax.ShapeDtypeStruct((D, F), F32),
            jax.ShapeDtypeStruct((F, D), F32),
            jax.ShapeDtypeStruct((1, 1), F32),
            jax.ShapeDtypeStruct((leads, D), F32),
            vec,
            vec,
            vec,
            vec,
            jax.ShapeDtypeStruct(gate_head.shape, F32),
        ),
        in_specs=[hbm] * 3 + [vm] * 2,
        out_specs=(hbm,) * 6 + (vm,) * 7,
        scratch_shapes=[
            pltpu.VMEM((s.rows, D), BF16),
            pltpu.VMEM((s.rows, D), F32),
            pltpu.VMEM((L, D), BF16),
            pltpu.VMEM((L, D), F32),
            pltpu.VMEM((L, D), F32),
            pltpu.SemaphoreType.DMA((len(cuts) + 2,)),
            pltpu.SemaphoreType.DMA((len(cuts) + 2,)),
        ],
        compiler_params=pltpu.CompilerParams(vmem_limit_bytes=VMEM_LIMIT),
        name="write_out",
    )(block, hidden, grads, va, vb)
    return (
        wide,
        pen.reshape(()),
        high,
        lead,
        g1,
        b1,
        jnp.transpose(qkv_grad, (0, 2, 1)),
        out_grad,
        g2,
        b2,
        up_grad,
        down_grad,
        gates,
    )


def solution(mesh):
    in_specs = (
        P("blk", None),
        P(),
        P("blk"),
        P(),
        P(),
        P(),
        P(None, None, "tp"),
        P("tp", None),
        P(),
        P(),
        P(None, "tp"),
        P("tp", None),
        P(None, "tp", None),
        P("tp", "blk"),
        P("blk", None),
    )
    out_specs = (
        P("blk", None),
        P(),
        P("blk", None),
        P(),
        P(),
        P(),
        P(None, None, "tp"),
        P("tp", None),
        P(),
        P(),
        P(None, "tp"),
        P("tp", None),
        P(None, "tp", None),
    )
    return jax.shard_map(
        partial(local, mesh.shape["blk"], mesh.shape["tp"]),
        mesh=mesh,
        in_specs=in_specs,
        out_specs=out_specs,
        check_vma=False,
    )
```

time: 127 us -> 122 us (0.961); the launches traced: 126 us -> 120 us
  Pallas kernels: 126 us -> 119 us
    pallas_call x1, Pallas kernels: 120 us -> 113 us  [local(): pl.pallas_call(partial(main_kernel, s, tuple(scratch)), out_shape=(jax.Sh...]
where the time goes in v4:
time: 122 us; the launch traced here: 120 us
  Pallas kernels  119 us (98%)
    pallas_call x1, Pallas kernels, local(): pl.pallas_call(partial(main_kernel, s, tuple(scratch)), out_shape=(jax.Sh...  113 us
    pallas_call x1, Pallas kernels, local(): pl.pallas_call(partial(last_kernel, s, cuts), out_shape=(jax.ShapeDtypeSt...  6.23 us

profile of v4, /device:TPU:1, one launch (start us, length us, event | category | flops | bytes accessed | tf_op | source)
XLA Modules:
  0.0 119.9 jit_solution(13607314635117763998)
XLA Ops:
  0.7 112.9 %block_step.1 = (bf16[256,768]{1,0:T(8,128)(2,1)}, f32[256,768]{1,0:T(8,128)}, bf16[2304,768]{1,0:T(8,128)(2,1)}, f32[32,768]{1,0:T(8,128)}, f32[32,768]{1,0:T(8,128)}) custom-call(f32[256,768]{1,0:T(8,128)} %refs_0_.1, s32[2048]{0:T(1024)} %refs_1_.1, s32[256]{0:T(256)} %refs_2_.1, bf16[16,768]{1,0:T(8,128)(2,1)} %refs_3_.1, f32[768]{0:T(1024)} %refs_4_.1, ...), custom_call_target="tpu_custom_call" | custom-call | flops 4127195136 | bytes 16777216 | tf_op jit(solution)/shard_map/block_step/pallas_call | solution.py:985
  113.6 6.2 %write_out.1 = (f32[256,768]{1,0:T(8,128)}, f32[256,768]{1,0:T(8,128)}, f32[3,192,768]{2,1,0:T(8,128)}, f32[192,768]{1,0:T(8,128)}, f32[768,768]{1,0:T(8,128)}, ...) custom-call(bf16[256,768]{1,0:T(8,128)(2,1)} %get-tuple-element.31.b, ...), custom_call_target="tpu_custom_call" | custom-call | tf_op jit(solution)/shard_map/write_out/pallas_call | solution.py:1031

commit v5 on v4

--- a/solution.py
+++ b/solution.py
@@ -69,7 +69,7 @@
     s.half = nb // 2
     s.groups = nb // GROUP
     s.pixels = pixels
-    s.sizes = (hidden, width, local_width * 2, local_width * 2)
+    s.sizes = (hidden, width, local_width * 2 + 128, local_width * 2)
     s.bases = tuple(sum(s.sizes[:i]) for i in range(4))
     s.rows = sum(s.sizes)
     s.tail = (leads + 4 + 15) // 16 * 16
@@ -134,10 +134,9 @@
         "ngp": v((L, D), BF16),
         "ngr": v((2, nt - 1, R, D), BF16),
         "ngg": v((L, D), BF16),
-        "va": v((GROUP, 32, D), BF16),
         "vb": v((GROUP, s.tail, D), BF16),
         "ent": v((nb, 8, 128), F32),
-        "va_sum": v((32, D), F32),
+        "ent_sum": v((8, 128), F32),
         "vb_sum": v((s.tail, D), F32),
         "gsrc": v((s.rows, D), BF16),
         "gout": v((s.rows, D), BF16),
@@ -145,20 +144,19 @@
     dma = pltpu.SemaphoreType.DMA
     out["loads"] = dma((15,))
     out["stores"] = dma((8,))
-    for name in ("zmask", "zgate", "zow", "zowr", "zatt", "zff", "zblk", "zn2", "zn2g", "zda", "zng", "zngg"):
+    for name in ("zmask", "zgate", "zow", "zowy", "zowr", "zatt", "zff", "zblk", "zn2", "zn2g", "zda", "zng", "zngg"):
         out[name + "_s"] = dma((2 * (nt - 1),))
         out[name + "_r"] = dma((2 * (nt - 1),))
     for name in ("kv", "q", "da0", "da1", "st"):
         for part in ("_s", "_r", "_rs", "_rr"):
             out[name + part] = dma((s.half,))
-    for name, count in (("cnt", nb), ("ent", nb), ("va", GROUP), ("vb", GROUP)):
+    for name, count in (("cnt", nb), ("ent", nb), ("vb", GROUP)):
         out[name + "_s"] = dma((count - 1,))
         out[name + "_r"] = dma((count - 1,))
     if s.groups > 1:
-        for name, rows in (("va2", 32), ("vb2", s.tail)):
-            out[name] = v((s.groups, rows, D), BF16)
-            out[name + "_s"] = dma((s.groups - 1,))
-            out[name + "_r"] = dma((s.groups - 1,))
+        out["vb2"] = v((s.groups, s.tail, D), BF16)
+        out["vb2_s"] = dma((s.groups - 1,))
+        out["vb2_r"] = dma((s.groups - 1,))
     for i, rows in enumerate(s.sizes):
         hr = rows // 2
         qr = hr // 4
@@ -193,7 +191,7 @@
         o_block,
         o_hidden,
         o_grads,
-        o_va,
+        o_ent,
         o_vb,
     ) = refs[:20]
     k = SimpleNamespace(**dict(zip(names, refs[20:])))
@@ -401,29 +399,36 @@
         dev = ((lax.rem(group + j, s.groups) * 4 + quarter) * 2 + core, t)
         return remote(ref.at[group], ref.at[group], sem["sup%d_s" % i].at[j - 1], sem["sup%d_r" % i].at[j - 1], dev)
 
-    def grads1(i):
-        c1_copy(i).start()
-
-    def grads2(i):
+    def q_peer(j):
+        return lax.rem(quarter + j, 4)
+
+    def direct_copy(i, j):
+        src = sem["core%d" % i].at[q_rows(i, q_peer(j))]
+        return g_copy(i, j, src, sem["quart%d" % i].at[j - 1], q_peer(j))
+
+    def direct2(i):
         c1_copy(i).wait()
         hs = sem["core%d" % i]
         hs[...] = (k.gsrc[g_half(i, core), :].astype(F32) + hs[...].astype(F32)).astype(BF16)
-        for copy in rs_copies(i):
-            copy.start()
-
-    def grads3(i):
-        for copy in rs_copies(i):
-            copy.wait()
-        hs = sem["core%d" % i]
-        rows = q_rows(i, second)
-        hs[rows, :] = (hs[rows, :].astype(F32) + sem["quart%d" % i][1].astype(F32)).astype(BF16)
-        rs_copy_b(i).start()
-
-    def grads4(i):
-        rs_copy_b(i).wait()
-        land = sem["quart%d" % i]
+        for j in range(1, 4):
+            direct_copy(i, j).start()
+
+    def direct3(i):
         acc = sem["core%d" % i][q_rows(i, quarter), :].astype(F32)
-        acc = acc + land[0].astype(F32) + land[2].astype(F32)
+        for j in range(1, 4):
+            direct_copy(i, j).wait()
+            acc = acc + sem["quart%d" % i][j - 1].astype(F32)
+        k.gout[g_rows(i, quarter), :] = across_groups(i, acc)
+        for j in range(1, 4):
+            out_copy(i, 3 + j, quarter, q_peer(j)).start()
+
+    def direct6(i):
+        for j in range(1, 4):
+            out_copy(i, 3 + j, quarter, q_peer(j)).wait_send()
+            out_copy(i, 3 + j, lax.rem(quarter + 4 - j, 4), q_peer(j)).wait_recv()
+        c2_copy(i, core).start()
+
+    def across_groups(i, acc):
         if s.groups > 1:
             ref = sem["sup%d" % i]
             ref[group] = acc.astype(BF16)
@@ -434,7 +439,32 @@
             acc = ref[0].astype(F32)
             for g in range(1, s.groups):
                 acc = acc + ref[g].astype(F32)
-        k.gout[g_rows(i, quarter), :] = acc.astype(BF16)
+        return acc.astype(BF16)
+
+    def grads1(i):
+        c1_copy(i).start()
+
+    def grads2(i):
+        c1_copy(i).wait()
+        hs = sem["core%d" % i]
+        hs[...] = (k.gsrc[g_half(i, core), :].astype(F32) + hs[...].astype(F32)).astype(BF16)
+        for copy in rs_copies(i):
+            copy.start()
+
+    def grads3(i):
+        for copy in rs_copies(i):
+            copy.wait()
+        hs = sem["core%d" % i]
+        rows = q_rows(i, second)
+        hs[rows, :] = (hs[rows, :].astype(F32) + sem["quart%d" % i][1].astype(F32)).astype(BF16)
+        rs_copy_b(i).start()
+
+    def grads4(i):
+        rs_copy_b(i).wait()
+        land = sem["quart%d" % i]
+        acc = sem["core%d" % i][q_rows(i, quarter), :].astype(F32)
+        acc = acc + land[0].astype(F32) + land[2].astype(F32)
+        k.gout[g_rows(i, quarter), :] = across_groups(i, acc)
         out_copy(i, 4, quarter, second).start()
 
     def grads5(i):
@@ -509,13 +539,17 @@
     compact = [k.head[e].astype(F32) for e in range(3)] + [jnp.zeros((4, D), F32)]
     k.gatec[t] = jnp.concatenate(compact, axis=0).astype(BF16)
     k.mask[t] = jnp.concatenate([k.pix[...].astype(F32), jnp.zeros((4, L), F32)], axis=0)
-    hw = W // 2
-
-    def ow_half(tt, c):
-        return k.ow.at[tt, pl.ds(pl.multiple_of(c * hw, hw), hw)]
-
-    def ow_relay(j, tt, c):
-        return remote(ow_half(tt, c), ow_half(tt, c), k.zowr_s.at[j - 1], k.zowr_r.at[j - 1], (sib, t))
+    part = W // 4
+    upper = quarter // 2
+
+    def ow_part(tt, c, u):
+        return k.ow.at[tt, pl.ds(pl.multiple_of((c + 2 * u) * part, part), part)]
+
+    def ow_copy(name, j, at, dev, second_set=0):
+        i = second_set * (nt - 1) + j - 1
+        return remote(at, at, sem[name + "_s"].at[i], sem[name + "_r"].at[i], (dev, t))
+
+    high_dev = (first_pair + high_peer) * 2 + core
 
     qkv_load.wait()
 
@@ -533,7 +567,7 @@
     ag_start("kv", kv_at)
     for j in range(1, nt):
         z_copy("zmask", j, k.mask.at[t], k.mask.at[t]).start()
-        z_copy("zow", j, ow_half(t, core), ow_half(t, core)).start()
+        z_copy("zow", j, ow_part(t, core, upper), ow_part(t, core, upper)).start()
         z_copy("zgate", j, k.gatec.at[t], k.gatec.at[t]).start()
     for copy in late_loads:
         copy.start()
@@ -584,6 +618,24 @@
             k.l[h : h + 1, :] = sums[h]
             k.acc[head(h), :] = outs[h]
 
+    def ow_pass_on():
+        for j in range(1, nt):
+            at = ow_part(z_from(j), core, upper)
+            z_copy("zow", j, at, at).wait_recv()
+            ow_copy("zowy", j, at, high_dev).start()
+            ow_copy("zowr", j, at, sib).start()
+
+    def ow_pass_second():
+        for j in range(1, nt):
+            at = ow_part(z_from(j), core, 1 - upper)
+            ow_copy("zowy", j, at, high_dev).wait_recv()
+            ow_copy("zowr", j, at, sib, 1).start()
+
+    def ow_arrived():
+        for j in range(1, nt):
+            ow_copy("zowr", j, ow_part(z_from(j), 1 - core, upper), sib).wait_recv()
+            ow_copy("zowr", j, ow_part(z_from(j), 1 - core, 1 - upper), sib, 1).wait_recv()
+
     ag_wait_relay("kv", kv_at, 0)
     forward_bands([b, sib])
     for j in range(1, nt):
@@ -591,11 +643,19 @@
     k.cnt[b] = jnp.broadcast_to(total(jnp.sum(k.mask[...], axis=0)), (8, 128))
     swap_start("cnt", every)
 
+    def forward_loop(start, stop):
+        @pl.loop(start, stop)
+        def _(i):
+            ag_wait_relay("kv", kv_at, i)
+            forward_bands([band_same(i), band_sib(i)])
+
     @pl.loop(1, s.half)
     def _(i):
         ag_relay("kv", kv_at, i)
-        ag_wait_relay("kv", kv_at, i)
-        forward_bands([band_same(i), band_sib(i)])
+
+    forward_loop(1, s.half // 2)
+    ow_pass_on()
+    forward_loop(s.half // 2, s.half)
 
     for h in range(H):
         att = k.acc[head(h), :] / k.l[h : h + 1, :]
@@ -620,14 +680,10 @@
         return k.st.at[band]
 
     ag_start("q", q_at)
-    for j in range(1, nt):
-        src = z_from(j)
-        z_copy("zow", j, ow_half(src, core), ow_half(src, core)).wait_recv()
-        ow_relay(j, src, core).start()
+    ow_pass_second()
     for copy in late_loads:
         copy.wait()
-    for j in range(1, nt):
-        ow_relay(j, z_from(j), 1 - core).wait_recv()
+    ow_arrived()
 
     for h in range(2):
         for j in range(1, nt):
@@ -695,21 +751,21 @@
         rs_start("zn2", h, k.n2p, k.n2r)
     block_copy = pltpu.make_async_copy(k.blow, o_block, k.stores.at[4])
     block_copy.start()
-    own_lg = k.lg[pl.ds(pl.multiple_of(t * 32, 32), 32), :]
-    k.va[near[1]] = mm_nn(own_lg, k.blow[...]).astype(BF16)
-    k.ent[b] = jnp.broadcast_to(entropy_sum / pixel_count, (8, 128))
-    swap_start("va", near)
-    swap_start("ent", every)
     k.gsrc[0:F, :] = mm_tn(k.actlow[...], k.oglow[...]).astype(BF16)
     grads1(0)
     k.gsrc[F : F + D, :] = mm_tn(k.n2low[...], k.ug[...]).astype(BF16)
     grads1(1)
+    own_lg = k.lg[pl.ds(pl.multiple_of(t * 32, 32), 32), :]
+    base = s.bases[2] + 2 * W
+    k.gsrc[base : base + 32, :] = mm_nn(own_lg, k.blow[...]).astype(BF16)
+    k.gsrc[base + 32 : base + 128, :] = jnp.zeros((96, D), BF16)
+    k.ent[b] = jnp.broadcast_to(entropy_sum / pixel_count, (8, 128))
+    swap_start("ent", every)
 
     def middle_backward(n2_grad, rows):
         return k.cot[rows, :] + norm_backward(n2_grad, k.u2[rows, :], k.r2[rows, :], row_of(k.gain2))
 
-    grads2(0)
-    for h in range(2):
+    def attended_exchange(h):
         rows = piece(h, t)
         n2_low = rs_sum("zn2", h, k.n2p, k.n2r).astype(BF16)
         k.n2g[rows, :] = n2_low
@@ -719,12 +775,8 @@
         for j in range(1, nt):
             z_copy("zda", j, k.dasrc.at[h, z_peer(j)], k.datok.at[h, t], h).start()
         k.datok[h, t] = k.dasrc[h, t]
-        if h == 0:
-            grads2(1)
-            grads3(0)
-    for h in range(2):
-        gather_start("zn2g", h, k.n2g)
-    for h in range(2):
+
+    def attended_arrived(h):
         for j in range(1, nt):
             z_copy("zda", j, k.dasrc.at[h, z_peer(j)], k.datok.at[h, z_from(j)], h).wait_recv()
         att_grad = jnp.transpose(k.datok[h].reshape(T, W).astype(F32)).astype(BF16)
@@ -735,8 +787,17 @@
             k.st[b, H + i : H + i + 1, half(h)] = jnp.sum(
                 weighted[i * HEAD_DIM : (i + 1) * HEAD_DIM], axis=0, keepdims=True
             )
+
+    grads2(0)
+    attended_exchange(0)
+    grads2(1)
+    attended_exchange(1)
+    attended_arrived(0)
+    attended_arrived(1)
     ag_start("st", st_at)
-    grads3(1)
+    for h in range(2):
+        gather_start("zn2g", h, k.n2g)
+    grads3(0)
     k.dq[...] = jnp.zeros((W, L), F32)
     k.dk[...] = jnp.zeros((W, L), F32)
     k.dv[...] = jnp.zeros((W, L), F32)
@@ -769,21 +830,7 @@
         for h in range(H):
             k.dq[head(h), :] = outs[h]
 
-    grads4(0)
-    k.dp[0] = (k.dq[...] * SCALE).astype(BF16)
-    base = s.bases[2]
-    for h in range(2):
-        gather_wait("zn2g", h, k.n2g)
-    n2_grad = k.n2g[...].astype(F32)
-    gain2_grad = jnp.sum(n2_grad * k.u2[...], axis=0, keepdims=True)
-    bias2_grad = jnp.sum(n2_grad, axis=0, keepdims=True)
-    middle_grad = middle_backward(n2_grad, pl.ds(0, L))
-    k.cot[...] = middle_grad
-    k.gsrc[base : base + W, :] = mm_nn(k.att[t], middle_grad.astype(BF16)).astype(BF16)
-    k.gsrc[base + W : base + 2 * W, :] = mm_nn(k.dp[0], k.normed[...]).astype(BF16)
-    grads1(2)
-    grads4(1)
-
+    grads3(1)
     @pl.loop(1, s.half)
     def _(i):
         ag_wait_relay("q", q_at, i)
@@ -810,21 +857,25 @@
     def backward_loop(start, stop):
         @pl.loop(start, stop)
         def _(i):
-            @pl.when(i > 0)
-            def _():
-                ag_relay("da0", da_at(0), i)
-                ag_relay("da1", da_at(1), i)
-                ag_relay("st", st_at, i)
-
             ag_wait_relay("da0", da_at(0), i)
             ag_wait_relay("da1", da_at(1), i)
             ag_wait_relay("st", st_at, i)
             backward_bands([band_same(i), band_sib(i)])
 
-    backward_loop(0, s.half // 2)
-    grads2(2)
+    backward_loop(0, 1)
+    grads4(0)
+
+    @pl.loop(1, s.half)
+    def _(i):
+        ag_relay("da0", da_at(0), i)
+        ag_relay("da1", da_at(1), i)
+        ag_relay("st", st_at, i)
+
+    backward_loop(1, s.half // 2)
+    grads4(1)
+    backward_loop(s.half // 2, s.half)
     grads5(0)
-    backward_loop(s.half // 2, s.half)
+    k.dp[0] = (k.dq[...] * SCALE).astype(BF16)
     k.dp[1] = k.dk[...].astype(BF16)
     k.dp[2] = k.dv[...].astype(BF16)
     for h in range(2):
@@ -832,27 +883,42 @@
             k.dp[:, :, half(h)].reshape(3 * W, T), k.qkv[...].reshape(3 * W, D)
         ).astype(BF16)
         rs_start("zng", h, k.ngp, k.ngr)
+    base = s.bases[2]
+    for h in range(2):
+        gather_wait("zn2g", h, k.n2g)
+    n2_grad = k.n2g[...].astype(F32)
+    gain2_grad = jnp.sum(n2_grad * k.u2[...], axis=0, keepdims=True)
+    bias2_grad = jnp.sum(n2_grad, axis=0, keepdims=True)
+    middle_grad = middle_backward(n2_grad, pl.ds(0, L))
+    k.cot[...] = middle_grad
+    k.gsrc[base : base + W, :] = mm_nn(k.att[t], middle_grad.astype(BF16)).astype(BF16)
+    k.gsrc[base + W : base + 2 * W, :] = mm_nn(k.dp[0], k.normed[...]).astype(BF16)
+    grads1(2)
+
     base = s.bases[3]
     k.gsrc[base : base + 2 * W, :] = mm_nn(k.dp[1:3].reshape(2 * W, L), k.normed[...]).astype(BF16)
     grads1(3)
     grads5(1)
-    grads3(2)
-    grads2(3)
-    for h in range(2):
-        k.ngg[piece(h, t), :] = rs_sum("zng", h, k.ngp, k.ngr).astype(BF16)
-        gather_start("zngg", h, k.ngg)
-        if h == 0:
-            grads6(0)
-            grads4(2)
-    grads3(3)
+    k.ngg[piece(0, t), :] = rs_sum("zng", 0, k.ngp, k.ngr).astype(BF16)
+    gather_start("zngg", 0, k.ngg)
+    direct2(2)
+    direct2(3)
+    grads6(0)
+    k.ngg[piece(1, t), :] = rs_sum("zng", 1, k.ngp, k.ngr).astype(BF16)
+    gather_start("zngg", 1, k.ngg)
     grads6(1)
-    grads5(2)
-    grads4(3)
+    direct3(2)
+    direct3(3)
     grads7(0)
-    grads6(2)
-    grads5(3)
-    for h in range(2):
-        gather_wait("zngg", h, k.ngg)
+    grads7(1)
+    swap_wait("ent", every)
+    k.ent_sum[...] = jnp.sum(k.ent[...], axis=0)
+    ent_copy = pltpu.make_async_copy(k.ent_sum, o_ent, k.stores.at[6])
+    ent_copy.start()
+    gather_wait("zngg", 0, k.ngg)
+    direct6(2)
+    direct6(3)
+    gather_wait("zngg", 1, k.ngg)
     n1_grad = k.ngg[...].astype(F32)
     unit1 = k.u1[...]
     gain1_grad = jnp.sum(n1_grad * unit1, axis=0, keepdims=True)
@@ -873,14 +939,7 @@
     ]
     k.vb[near[1]] = jnp.concatenate(tail, axis=0).astype(BF16)
     swap_start("vb", near)
-    grads7(1)
-    grads6(3)
     grads7(2)
-    swap_wait("ent", every)
-    k.va_sum[...] = swap_sum("va")
-    k.va_sum[24:32, 0:128] = jnp.sum(k.ent[...], axis=0)
-    va_copy = pltpu.make_async_copy(k.va_sum, o_va, k.stores.at[6])
-    va_copy.start()
     grads7(3)
     k.vb_sum[...] = swap_sum("vb")
     vb_copy = pltpu.make_async_copy(k.vb_sum, o_vb, k.stores.at[7])
@@ -889,8 +948,11 @@
     for j in range(1, nt):
         z_copy("zmask", j, k.mask.at[t], k.mask.at[t]).wait_send()
         z_copy("zgate", j, k.gatec.at[t], k.gatec.at[t]).wait_send()
-        z_copy("zow", j, ow_half(t, core), ow_half(t, core)).wait_send()
-        ow_relay(j, t, core).wait_send()
+        z_copy("zow", j, ow_part(t, core, upper), ow_part(t, core, upper)).wait_send()
+        at = ow_part(z_from(j), core, upper)
+        ow_copy("zowy", j, at, high_dev).wait_send()
+        ow_copy("zowr", j, at, sib).wait_send()
+        ow_copy("zowr", j, at, sib, 1).wait_send()
         for h in range(2):
             z_copy("zatt", j, att_half(t, h), att_half(t, h), h).wait_send()
             z_copy("zda", j, k.dasrc.at[h, z_peer(j)], k.datok.at[h, t], h).wait_send()
@@ -906,12 +968,12 @@
     swap_finish("ent", every)
     for i in range(4):
         grads_store(i).wait()
-    for copy in (block_copy, hidden_copy, va_copy, vb_copy):
+    for copy in (block_copy, hidden_copy, ent_copy, vb_copy):
         copy.wait()
 
 
 def last_kernel(
-    s, cuts, block, hidden, grads, va, vb,
+    s, cuts, block, hidden, grads, ent, vb,
     o_block, o_hidden, o_qkv, o_out, o_up, o_down, o_pen, o_lead, o_g1, o_b1, o_g2, o_b2, o_gate,
     low, wide, low_block, wide_block, keep, load_sem, store_sem,
 ):
@@ -930,7 +992,9 @@
         stores.append(
             pltpu.make_async_copy(wide.at[rows], outs[name].at[pl.ds(start, size)], store_sem.at[i + 2])
         )
-    for copy in loads:
+    gate_rows = pl.ds(s.bases[2] + 2 * s.W, 32)
+    gate_load = pltpu.make_async_copy(grads.at[gate_rows], low.at[gate_rows], load_sem.at[len(cuts) + 2])
+    for copy in loads + [gate_load]:
         copy.start()
     loads[0].wait()
     wide_block[...] = low_block[...].astype(F32)
@@ -942,10 +1006,11 @@
         rows = pl.ds(row, size)
         wide[rows, :] = low[rows, :].astype(F32)
         stores[i + 2].start()
-    small = va[...]
+    gate_load.wait()
+    small = low[gate_rows, :].astype(F32)
     for e in range(3):
         o_gate[e] = small[8 * e : 8 * e + 4]
-    o_pen[...] = small[24:25, 0:1]
+    o_pen[...] = ent[0:1, 0:1]
     tail = vb[...]
     o_lead[...] = tail[0 : s.leads]
     o_g1[...] = tail[s.leads].reshape(s.D)
@@ -982,13 +1047,13 @@
     s = dims_of(nb, nt, L, D, W, F, leads, L * nb * pixel_mask.shape[0] * nt)
     scratch = scratch_of(s)
     vm = pl.BlockSpec(memory_space=pltpu.VMEM)
-    block, hidden, grads, va, vb = pl.pallas_call(
+    block, hidden, grads, ent, vb = pl.pallas_call(
         partial(main_kernel, s, tuple(scratch)),
         out_shape=(
             jax.ShapeDtypeStruct((L, D), BF16),
             jax.ShapeDtypeStruct((L, D), F32),
             jax.ShapeDtypeStruct((s.rows, D), BF16),
-            jax.ShapeDtypeStruct((32, D), F32),
+            jax.ShapeDtypeStruct((8, 128), F32),
             jax.ShapeDtypeStruct((s.tail, D), F32),
         ),
         in_specs=[pl.BlockSpec(memory_space=pltpu.HBM)] * 15,
@@ -1022,11 +1087,18 @@
     )
     vec = jax.ShapeDtypeStruct((D,), F32)
     cuts = []
-    row = 0
-    for name, size in (("down", F), ("up", D), ("out", W), ("q", W), ("k", W), ("v", W)):
+    first = s.bases[2]
+    places = (
+        ("down", 0, F),
+        ("up", F, D),
+        ("out", first, W),
+        ("q", first + W, W),
+        ("k", s.bases[3], W),
+        ("v", s.bases[3] + W, W),
+    )
+    for name, row, size in places:
         for start in range(0, size, 256):
             cuts.append((row + start, name, start, min(256, size - start)))
-        row += size
     hbm = pl.BlockSpec(memory_space=pl.ANY)
     wide, high, qkv_grad, out_grad, up_grad, down_grad, pen, lead, g1, b1, g2, b2, gates = pl.pallas_call(
         partial(last_kernel, s, cuts),
@@ -1053,12 +1125,12 @@
             pltpu.VMEM((L, D), BF16),
             pltpu.VMEM((L, D), F32),
             pltpu.VMEM((L, D), F32),
-            pltpu.SemaphoreType.DMA((len(cuts) + 2,)),
+            pltpu.SemaphoreType.DMA((len(cuts) + 3,)),
             pltpu.SemaphoreType.DMA((len(cuts) + 2,)),
         ],
         compiler_params=pltpu.CompilerParams(vmem_limit_bytes=VMEM_LIMIT),
         name="write_out",
-    )(block, hidden, grads, va, vb)
+    )(block, hidden, grads, ent, vb)
     return (
         wide,
         pen.reshape(()),

time: 122 us -> 116 us (0.951); the launches traced: 120 us -> 116 us
  Pallas kernels: 119 us -> 115 us
    pallas_call x1, Pallas kernels: 113 us -> 109 us  [local(): pl.pallas_call(partial(main_kernel, s, tuple(scratch)), out_shape=(jax.Sh...]
where the time goes in v5:
time: 116 us
  Pallas kernels  115 us (99%)
    pallas_call x1, Pallas kernels, local(): pl.pallas_call(partial(main_kernel, s, tuple(scratch)), out_shape=(jax.Sh...  109 us
    pallas_call x1, Pallas kernels, local(): pl.pallas_call(partial(last_kernel, s, cuts), out_shape=(jax.ShapeDtypeSt...  6.19 us

profile of v5, /device:TPU:1, one launch (start us, length us, event | category | flops | bytes accessed | tf_op | source)
XLA Modules:
  0.0 115.6 jit_solution(9710591637647616720)
XLA Ops:
  0.7 108.6 %block_step.1 = (bf16[256,768]{1,0:T(8,128)(2,1)}, f32[256,768]{1,0:T(8,128)}, bf16[2432,768]{1,0:T(8,128)(2,1)}, f32[8,128]{1,0:T(8,128)}, f32[32,768]{1,0:T(8,128)}) custom-call(f32[256,768]{1,0:T(8,128)} %refs_0_.1, s32[2048]{0:T(1024)} %refs_1_.1, s32[256]{0:T(256)} %refs_2_.1, bf16[16,768]{1,0:T(8,128)(2,1)} %refs_3_.1, f32[768]{0:T(1024)} %refs_4_.1, ...), custom_call_target="tpu_custom_call" | custom-call | flops 4278190080 | bytes 16777216 | tf_op jit(solution)/shard_map/block_step/pallas_call | solution.py:1050
  109.2 6.2 %write_out.1 = (f32[256,768]{1,0:T(8,128)}, f32[256,768]{1,0:T(8,128)}, f32[3,192,768]{2,1,0:T(8,128)}, f32[192,768]{1,0:T(8,128)}, f32[768,768]{1,0:T(8,128)}, ...) custom-call(bf16[256,768]{1,0:T(8,128)(2,1)} %get-tuple-element.31.b, ...), custom_call_target="tpu_custom_call" | custom-call | tf_op jit(solution)/shard_map/write_out/pallas_call | solution.py:1103

commit v6 on v5

--- a/solution.py
+++ b/solution.py
@@ -69,7 +69,7 @@
     s.half = nb // 2
     s.groups = nb // GROUP
     s.pixels = pixels
-    s.sizes = (hidden, width, local_width * 2 + 128, local_width * 2)
+    s.sizes = (hidden, width + 128, local_width * 2, local_width * 2)
     s.bases = tuple(sum(s.sizes[:i]) for i in range(4))
     s.rows = sum(s.sizes)
     s.tail = (leads + 4 + 15) // 16 * 16
@@ -144,19 +144,25 @@
     dma = pltpu.SemaphoreType.DMA
     out["loads"] = dma((15,))
     out["stores"] = dma((8,))
-    for name in ("zmask", "zgate", "zow", "zowy", "zowr", "zatt", "zff", "zblk", "zn2", "zn2g", "zda", "zng", "zngg"):
-        out[name + "_s"] = dma((2 * (nt - 1),))
-        out[name + "_r"] = dma((2 * (nt - 1),))
+    for name in ("zmask", "zgate", "zow", "zowy", "zowr", "zowq"):
+        out[name + "_s"] = dma((1,))
+        out[name + "_r"] = dma((1,))
+    for name in ("zatt", "zff", "zblk", "zn2", "zn2g", "zda", "zng", "zngg"):
+        out[name + "_s"] = dma((2,))
+        out[name + "_r"] = dma((2,))
     for name in ("kv", "q", "da0", "da1", "st"):
-        for part in ("_s", "_r", "_rs", "_rr"):
-            out[name + part] = dma((s.half,))
-    for name, count in (("cnt", nb), ("ent", nb), ("vb", GROUP)):
-        out[name + "_s"] = dma((count - 1,))
-        out[name + "_r"] = dma((count - 1,))
+        count = s.half if name == "kv" else 1
+        out[name + "_s"] = dma((1,))
+        out[name + "_r"] = dma((count,))
+        out[name + "_rs"] = dma((1,))
+        out[name + "_rr"] = dma((count,))
+    for name in ("cnt", "ent", "vb"):
+        out[name + "_s"] = dma((1,))
+        out[name + "_r"] = dma((1,))
     if s.groups > 1:
         out["vb2"] = v((s.groups, s.tail, D), BF16)
-        out["vb2_s"] = dma((s.groups - 1,))
-        out["vb2_r"] = dma((s.groups - 1,))
+        out["vb2_s"] = dma((1,))
+        out["vb2_r"] = dma((1,))
     for i, rows in enumerate(s.sizes):
         hr = rows // 2
         qr = hr // 4
@@ -164,10 +170,10 @@
         out["quart%d" % i] = v((3, qr, D), BF16)
         if s.groups > 1:
             out["sup%d" % i] = v((s.groups, qr, D), BF16)
-            out["sup%d_s" % i] = dma((s.groups - 1,))
-            out["sup%d_r" % i] = dma((s.groups - 1,))
-        out["gs%d" % i] = dma((8,))
-        out["gr%d" % i] = dma((8,))
+            out["sup%d_s" % i] = dma((1,))
+            out["sup%d_r" % i] = dma((1,))
+        out["gs%d" % i] = dma((6 if i < 2 else 4,))
+        out["gr%d" % i] = dma((6 if i < 2 else 4,))
     return out
 
 
@@ -215,8 +221,10 @@
         )
 
     def z_copy(name, j, src, dst, h=0):
-        i = h * (nt - 1) + j - 1
-        return remote(src, dst, sem[name + "_s"].at[i], sem[name + "_r"].at[i], (b, z_peer(j)))
+        return remote(src, dst, sem[name + "_s"].at[h], sem[name + "_r"].at[h], (b, z_peer(j)))
+
+    def z_all(name, ref, h=0):
+        return z_copy(name, 1, ref, ref, h)
 
     def half(h):
         return pl.ds(h * T, T)
@@ -225,10 +233,12 @@
         return pl.ds(pl.multiple_of(h * T + tt * R, R), R)
 
     def ag_copy(name, at, i, dst_band):
-        return remote(at(b), at(b), sem[name + "_s"].at[i], sem[name + "_r"].at[i], (dst_band, t))
+        slot = i if name == "kv" else 0
+        return remote(at(b), at(b), sem[name + "_s"].at[0], sem[name + "_r"].at[slot], (dst_band, t))
 
     def relay_copy(name, at, i, band):
-        return remote(at(band), at(band), sem[name + "_rs"].at[i], sem[name + "_rr"].at[i], (sib, t))
+        slot = i if name == "kv" else 0
+        return remote(at(band), at(band), sem[name + "_rs"].at[0], sem[name + "_rr"].at[slot], (sib, t))
 
     def band_same(i):
         return lax.rem(b + nb - 2 * i, nb)
@@ -243,58 +253,56 @@
 
         relay_copy(name, at, 0, b).start()
 
+    def ag_wait(name, at, i):
+        band = band_same(i)
+        remote(at(band), at(band), sem[name + "_s"].at[0], sem[name + "_r"].at[i], (sib, t)).wait_recv()
+
     def ag_relay(name, at, i):
-        band = band_same(i)
-        remote(at(band), at(band), sem[name + "_s"].at[i], sem[name + "_r"].at[i], (sib, t)).wait_recv()
-        relay_copy(name, at, i, band).start()
+        relay_copy(name, at, i, band_same(i)).start()
 
     def ag_wait_relay(name, at, i):
         relay_copy(name, at, i, band_sib(i)).wait_recv()
 
-    def ag_finish(name, at):
+    def ag_pass_on(name, at, all_at):
+        ref = all_at(s.half - 1)
+        remote(ref, ref, sem[name + "_s"].at[0], sem[name + "_r"].at[0], (sib, t)).wait_recv()
+
         @pl.loop(1, s.half)
         def _(i):
-            ag_copy(name, at, i, sib).wait_send()
-
-        @pl.loop(0, s.half)
-        def _(i):
-            relay_copy(name, at, i, b).wait_send()
+            ag_relay(name, at, i)
+
+    def ag_arrived(name, all_at):
+        ref = all_at(s.half)
+        remote(ref, ref, sem[name + "_rs"].at[0], sem[name + "_rr"].at[0], (sib, t)).wait_recv()
+
+    def ag_finish(name, all_at):
+        ref = all_at(s.half - 1)
+        remote(ref, ref, sem[name + "_s"].at[0], sem[name + "_r"].at[0], (sib, t)).wait_send()
+        ref = all_at(s.half)
+        remote(ref, ref, sem[name + "_rs"].at[0], sem[name + "_rr"].at[0], (sib, t)).wait_send()
 
     every = (nb, b, lambda i: i)
     near = (GROUP, lax.rem(b, GROUP), lambda i: b // GROUP * GROUP + i)
     far = (s.groups, b // GROUP, lambda i: i * GROUP + lax.rem(b, GROUP))
 
-    def swap_copy(name, members, i, slot, to):
-        ref = sem[name]
-        return remote(
-            ref.at[slot],
-            ref.at[slot],
-            sem[name + "_s"].at[i - 1],
-            sem[name + "_r"].at[i - 1],
-            (members[2](to), t),
-        )
+    def swap_copy(name, members, ref, to):
+        return remote(ref, ref, sem[name + "_s"].at[0], sem[name + "_r"].at[0], (members[2](to), t))
 
     def swap_start(name, members):
         count, me, _ = members
 
         @pl.loop(1, count)
         def _(i):
-            swap_copy(name, members, i, me, lax.rem(me + i, count)).start()
+            swap_copy(name, members, sem[name].at[me], lax.rem(me + i, count)).start()
+
+    def swap_all(name, members):
+        return swap_copy(name, members, sem[name].at[pl.ds(0, members[0] - 1)], 0)
 
     def swap_wait(name, members):
-        count, me, _ = members
-
-        @pl.loop(1, count)
-        def _(i):
-            peer = lax.rem(me + count - i, count)
-            swap_copy(name, members, i, peer, peer).wait_recv()
+        swap_all(name, members).wait_recv()
 
     def swap_finish(name, members):
-        count, me, _ = members
-
-        @pl.loop(1, count)
-        def _(i):
-            swap_copy(name, members, i, me, lax.rem(me + i, count)).wait_send()
+        swap_all(name, members).wait_send()
 
     def slots_sum(ref, count):
         return lax.fori_loop(
@@ -318,30 +326,29 @@
             z_copy(name, j, part.at[piece(h, z_peer(j))], recv.at[h, j - 1], h).start()
 
     def rs_sum(name, h, part, recv):
+        z_all(name, recv.at[h], h).wait_recv()
         acc = part[piece(h, t), :].astype(F32)
         for j in range(1, nt):
-            z_copy(name, j, part.at[piece(h, z_from(j))], recv.at[h, j - 1], h).wait_recv()
             acc = acc + recv[h, j - 1].astype(F32)
         return acc
 
-    def rs_finish(name, part, recv):
+    def rs_finish(name, recv):
         for h in range(2):
-            for j in range(1, nt):
-                z_copy(name, j, part.at[piece(h, z_peer(j))], recv.at[h, j - 1], h).wait_send()
+            z_all(name, recv.at[h], h).wait_send()
 
     def gather_start(name, h, ref):
         for j in range(1, nt):
             z_copy(name, j, ref.at[piece(h, t)], ref.at[piece(h, t)], h).start()
 
+    def gather_all(name, h, ref):
+        return z_all(name, ref.at[pl.ds(h * T, (nt - 1) * R)], h)
+
     def gather_wait(name, h, ref):
-        for j in range(1, nt):
-            rows = piece(h, z_from(j))
-            z_copy(name, j, ref.at[rows], ref.at[rows], h).wait_recv()
+        gather_all(name, h, ref).wait_recv()
 
     def gather_finish(name, ref):
         for h in range(2):
-            for j in range(1, nt):
-                z_copy(name, j, ref.at[piece(h, t)], ref.at[piece(h, t)], h).wait_send()
+            gather_all(name, h, ref).wait_send()
 
     quarter = lax.rem(pair, 4)
     first_pair = pair - quarter
@@ -380,11 +387,19 @@
         land = sem["quart%d" % i]
         return (
             g_copy(i, 1, hs.at[q_rows(i, first)], land.at[0], first),
-            g_copy(i, 2, hs.at[q_rows(i, across)], land.at[1], first),
+            g_copy(i, 1, hs.at[q_rows(i, across)], land.at[1], first),
         )
 
+    def land_all(i, slot, count):
+        ref = sem["quart%d" % i].at[pl.ds(0, count)]
+        return g_copy(i, slot, ref, ref, first)
+
+    def out_all(i, slot, count):
+        ref = k.gout.at[pl.ds(s.bases[i], count * (s.sizes[i] // 8))]
+        return g_copy(i, slot, ref, ref, first)
+
     def rs_copy_b(i):
-        return g_copy(i, 3, sem["core%d" % i].at[q_rows(i, second)], sem["quart%d" % i].at[2], second)
+        return g_copy(i, 2, sem["core%d" % i].at[q_rows(i, second)], sem["quart%d" % i].at[2], second)
 
     def out_copy(i, slot, q, to):
         rows = g_rows(i, q)
@@ -392,50 +407,20 @@
 
     def c2_copy(i, c):
         rows = g_half(i, c)
-        return sib_copy(i, 7, k.gout.at[rows], k.gout.at[rows])
-
-    def sup_copy(i, j):
-        ref = sem["sup%d" % i]
-        dev = ((lax.rem(group + j, s.groups) * 4 + quarter) * 2 + core, t)
-        return remote(ref.at[group], ref.at[group], sem["sup%d_s" % i].at[j - 1], sem["sup%d_r" % i].at[j - 1], dev)
-
-    def q_peer(j):
-        return lax.rem(quarter + j, 4)
-
-    def direct_copy(i, j):
-        src = sem["core%d" % i].at[q_rows(i, q_peer(j))]
-        return g_copy(i, j, src, sem["quart%d" % i].at[j - 1], q_peer(j))
-
-    def direct2(i):
-        c1_copy(i).wait()
-        hs = sem["core%d" % i]
-        hs[...] = (k.gsrc[g_half(i, core), :].astype(F32) + hs[...].astype(F32)).astype(BF16)
-        for j in range(1, 4):
-            direct_copy(i, j).start()
-
-    def direct3(i):
-        acc = sem["core%d" % i][q_rows(i, quarter), :].astype(F32)
-        for j in range(1, 4):
-            direct_copy(i, j).wait()
-            acc = acc + sem["quart%d" % i][j - 1].astype(F32)
-        k.gout[g_rows(i, quarter), :] = across_groups(i, acc)
-        for j in range(1, 4):
-            out_copy(i, 3 + j, quarter, q_peer(j)).start()
-
-    def direct6(i):
-        for j in range(1, 4):
-            out_copy(i, 3 + j, quarter, q_peer(j)).wait_send()
-            out_copy(i, 3 + j, lax.rem(quarter + 4 - j, 4), q_peer(j)).wait_recv()
-        c2_copy(i, core).start()
+        return sib_copy(i, 3, k.gout.at[rows], k.gout.at[rows])
 
     def across_groups(i, acc):
         if s.groups > 1:
             ref = sem["sup%d" % i]
             ref[group] = acc.astype(BF16)
+
+            def copy(j, at):
+                dev = ((lax.rem(group + j, s.groups) * 4 + quarter) * 2 + core, t)
+                return remote(at, at, sem["sup%d_s" % i].at[0], sem["sup%d_r" % i].at[0], dev)
+
             for j in range(1, s.groups):
-                sup_copy(i, j).start()
-            for j in range(1, s.groups):
-                sup_copy(i, j).wait()
+                copy(j, ref.at[group]).start()
+            copy(1, ref.at[pl.ds(0, s.groups - 1)]).wait()
             acc = ref[0].astype(F32)
             for g in range(1, s.groups):
                 acc = acc + ref[g].astype(F32)
@@ -444,16 +429,18 @@
     def grads1(i):
         c1_copy(i).start()
 
-    def grads2(i):
+    def pair_sum(i):
         c1_copy(i).wait()
         hs = sem["core%d" % i]
         hs[...] = (k.gsrc[g_half(i, core), :].astype(F32) + hs[...].astype(F32)).astype(BF16)
+
+    def grads2(i):
+        pair_sum(i)
         for copy in rs_copies(i):
             copy.start()
 
     def grads3(i):
-        for copy in rs_copies(i):
-            copy.wait()
+        land_all(i, 1, 2).wait()
         hs = sem["core%d" % i]
         rows = q_rows(i, second)
         hs[rows, :] = (hs[rows, :].astype(F32) + sem["quart%d" % i][1].astype(F32)).astype(BF16)
@@ -471,13 +458,32 @@
         out_copy(i, 4, quarter, second).wait_send()
         out_copy(i, 4, second, second).wait_recv()
         out_copy(i, 5, quarter, first).start()
-        out_copy(i, 6, second, first).start()
+        out_copy(i, 5, second, first).start()
 
     def grads6(i):
-        out_copy(i, 5, quarter, first).wait_send()
-        out_copy(i, 6, second, first).wait_send()
-        out_copy(i, 5, first, first).wait_recv()
-        out_copy(i, 6, across, first).wait_recv()
+        out_all(i, 5, 2).wait()
+        c2_copy(i, core).start()
+
+    def q_peer(j):
+        return lax.rem(quarter + j, 4)
+
+    def direct2(i):
+        pair_sum(i)
+        for j in range(1, 4):
+            src = sem["core%d" % i].at[q_rows(i, q_peer(j))]
+            g_copy(i, 1, src, sem["quart%d" % i].at[j - 1], q_peer(j)).start()
+
+    def direct3(i):
+        land_all(i, 1, 3).wait()
+        acc = sem["core%d" % i][q_rows(i, quarter), :].astype(F32)
+        for j in range(3):
+            acc = acc + sem["quart%d" % i][j].astype(F32)
+        k.gout[g_rows(i, quarter), :] = across_groups(i, acc)
+        for j in range(1, 4):
+            out_copy(i, 2, quarter, q_peer(j)).start()
+
+    def direct6(i):
+        out_all(i, 2, 3).wait()
         c2_copy(i, core).start()
 
     def grads_store(i):
@@ -545,10 +551,10 @@
     def ow_part(tt, c, u):
         return k.ow.at[tt, pl.ds(pl.multiple_of((c + 2 * u) * part, part), part)]
 
-    def ow_copy(name, j, at, dev, second_set=0):
-        i = second_set * (nt - 1) + j - 1
-        return remote(at, at, sem[name + "_s"].at[i], sem[name + "_r"].at[i], (dev, t))
-
+    def ow_copy(name, at, dev):
+        return remote(at, at, sem[name + "_s"].at[0], sem[name + "_r"].at[0], (dev, t))
+
+    ow_all = k.ow.at[pl.ds(0, nt - 1), pl.ds(0, part)]
     high_dev = (first_pair + high_peer) * 2 + core
 
     qkv_load.wait()
@@ -619,43 +625,41 @@
             k.acc[head(h), :] = outs[h]
 
     def ow_pass_on():
+        z_all("zow", ow_all).wait_recv()
         for j in range(1, nt):
             at = ow_part(z_from(j), core, upper)
-            z_copy("zow", j, at, at).wait_recv()
-            ow_copy("zowy", j, at, high_dev).start()
-            ow_copy("zowr", j, at, sib).start()
+            ow_copy("zowy", at, high_dev).start()
+            ow_copy("zowr", at, sib).start()
 
     def ow_pass_second():
+        ow_copy("zowy", ow_all, high_dev).wait_recv()
         for j in range(1, nt):
-            at = ow_part(z_from(j), core, 1 - upper)
-            ow_copy("zowy", j, at, high_dev).wait_recv()
-            ow_copy("zowr", j, at, sib, 1).start()
-
-    def ow_arrived():
-        for j in range(1, nt):
-            ow_copy("zowr", j, ow_part(z_from(j), 1 - core, upper), sib).wait_recv()
-            ow_copy("zowr", j, ow_part(z_from(j), 1 - core, 1 - upper), sib, 1).wait_recv()
+            ow_copy("zowq", ow_part(z_from(j), core, 1 - upper), sib).start()
 
     ag_wait_relay("kv", kv_at, 0)
     forward_bands([b, sib])
-    for j in range(1, nt):
-        z_copy("zmask", j, k.mask.at[t], k.mask.at[z_from(j)]).wait_recv()
+    z_all("zmask", k.mask.at[pl.ds(0, nt - 1)]).wait_recv()
     k.cnt[b] = jnp.broadcast_to(total(jnp.sum(k.mask[...], axis=0)), (8, 128))
     swap_start("cnt", every)
 
-    def forward_loop(start, stop):
-        @pl.loop(start, stop)
-        def _(i):
-            ag_wait_relay("kv", kv_at, i)
-            forward_bands([band_same(i), band_sib(i)])
-
     @pl.loop(1, s.half)
     def _(i):
+        ag_wait("kv", kv_at, i)
         ag_relay("kv", kv_at, i)
 
-    forward_loop(1, s.half // 2)
+    @pl.loop(0, s.half // 2 - 1)
+    def _(i):
+        forward_bands([band_same(2 * i + 1), band_same(2 * i + 2)])
+
+    ag_wait_relay("kv", kv_at, 1)
+    forward_bands([band_same(s.half - 1), band_sib(1)])
     ow_pass_on()
-    forward_loop(s.half // 2, s.half)
+
+    @pl.loop(1, s.half // 2)
+    def _(i):
+        ag_wait_relay("kv", kv_at, 2 * i)
+        ag_wait_relay("kv", kv_at, 2 * i + 1)
+        forward_bands([band_sib(2 * i), band_sib(2 * i + 1)])
 
     for h in range(H):
         att = k.acc[head(h), :] / k.l[h : h + 1, :]
@@ -679,15 +683,24 @@
     def st_at(band):
         return k.st.at[band]
 
+    def q_all(count):
+        return k.qd.at[pl.ds(0, count), pl.ds(0, W)]
+
+    def da_all(h):
+        return lambda count: k.qd.at[pl.ds(0, count), pl.ds(W, W), half(h)]
+
+    def st_all(count):
+        return k.st.at[pl.ds(0, count)]
+
     ag_start("q", q_at)
     ow_pass_second()
     for copy in late_loads:
         copy.wait()
-    ow_arrived()
+    ow_copy("zowr", ow_all, sib).wait_recv()
+    ow_copy("zowq", ow_all, sib).wait_recv()
 
     for h in range(2):
-        for j in range(1, nt):
-            z_copy("zatt", j, att_half(z_from(j), h), att_half(z_from(j), h), h).wait_recv()
+        z_all("zatt", k.att.at[pl.ds(0, nt - 1), :, half(h)], h).wait_recv()
         rows = half(h)
         middle = k.mid[rows, :] + mm_tn(
             k.att[:, :, half(h)].reshape(nt * W, T), k.ow[...].reshape(nt * W, D)
@@ -706,8 +719,7 @@
     k.upw[...] = 0.5 * (1.0 + lax.erf(upward * INV_SQRT2)) + upward * (
         jnp.exp(-0.5 * upward * upward) * INV_SQRT_2PI
     )
-    for j in range(1, nt):
-        z_copy("zgate", j, k.gatec.at[t], k.gatec.at[z_from(j)]).wait_recv()
+    z_all("zgate", k.gatec.at[pl.ds(0, nt - 1)]).wait_recv()
     for tt in range(nt):
         x = k.gatec[tt].astype(F32)
         pad = jnp.zeros((4, D), F32)
@@ -722,9 +734,7 @@
         k.blow[piece(h, t), :] = block_piece.astype(BF16)
         gather_start("zblk", h, k.blow)
 
-    @pl.loop(1, s.half)
-    def _(i):
-        ag_relay("q", q_at, i)
+    ag_pass_on("q", q_at, q_all)
 
     entropy_sum = jnp.zeros((1, 1), F32)
     for h in range(2):
@@ -754,11 +764,11 @@
     k.gsrc[0:F, :] = mm_tn(k.actlow[...], k.oglow[...]).astype(BF16)
     grads1(0)
     k.gsrc[F : F + D, :] = mm_tn(k.n2low[...], k.ug[...]).astype(BF16)
-    grads1(1)
     own_lg = k.lg[pl.ds(pl.multiple_of(t * 32, 32), 32), :]
-    base = s.bases[2] + 2 * W
+    base = s.bases[1] + D
     k.gsrc[base : base + 32, :] = mm_nn(own_lg, k.blow[...]).astype(BF16)
     k.gsrc[base + 32 : base + 128, :] = jnp.zeros((96, D), BF16)
+    grads1(1)
     k.ent[b] = jnp.broadcast_to(entropy_sum / pixel_count, (8, 128))
     swap_start("ent", every)
 
@@ -777,8 +787,7 @@
         k.datok[h, t] = k.dasrc[h, t]
 
     def attended_arrived(h):
-        for j in range(1, nt):
-            z_copy("zda", j, k.dasrc.at[h, z_peer(j)], k.datok.at[h, z_from(j)], h).wait_recv()
+        z_all("zda", k.datok.at[h, pl.ds(0, nt - 1)], h).wait_recv()
         att_grad = jnp.transpose(k.datok[h].reshape(T, W).astype(F32)).astype(BF16)
         k.qd[b, W : 2 * W, half(h)] = att_grad
         ag_start("da%d" % h, da_at(h))
@@ -798,6 +807,7 @@
     for h in range(2):
         gather_start("zn2g", h, k.n2g)
     grads3(0)
+    grads3(1)
     k.dq[...] = jnp.zeros((W, L), F32)
     k.dk[...] = jnp.zeros((W, L), F32)
     k.dv[...] = jnp.zeros((W, L), F32)
@@ -830,12 +840,9 @@
         for h in range(H):
             k.dq[head(h), :] = outs[h]
 
-    grads3(1)
-    @pl.loop(1, s.half)
-    def _(i):
-        ag_wait_relay("q", q_at, i)
-
-    ag_wait_relay("q", q_at, 0)
+    grads4(0)
+    grads4(1)
+    ag_arrived("q", q_all)
 
     def backward_bands(bands):
         tiles = [(h, i) for h in range(H) for i in range(len(bands))]
@@ -854,27 +861,23 @@
             k.dk[head(h), :] = key_outs[h]
             k.dv[head(h), :] = value_outs[h]
 
+    for name, at, all_at in (
+        ("da0", da_at(0), da_all(0)),
+        ("da1", da_at(1), da_all(1)),
+        ("st", st_at, st_all),
+    ):
+        ag_pass_on(name, at, all_at)
+        ag_arrived(name, all_at)
+
     def backward_loop(start, stop):
         @pl.loop(start, stop)
         def _(i):
-            ag_wait_relay("da0", da_at(0), i)
-            ag_wait_relay("da1", da_at(1), i)
-            ag_wait_relay("st", st_at, i)
             backward_bands([band_same(i), band_sib(i)])
 
-    backward_loop(0, 1)
-    grads4(0)
-
-    @pl.loop(1, s.half)
-    def _(i):
-        ag_relay("da0", da_at(0), i)
-        ag_relay("da1", da_at(1), i)
-        ag_relay("st", st_at, i)
-
-    backward_loop(1, s.half // 2)
-    grads4(1)
+    backward_loop(0, s.half // 2)
+    grads5(0)
     backward_loop(s.half // 2, s.half)
-    grads5(0)
+    grads5(1)
     k.dp[0] = (k.dq[...] * SCALE).astype(BF16)
     k.dp[1] = k.dk[...].astype(BF16)
     k.dp[2] = k.dv[...].astype(BF16)
@@ -898,7 +901,6 @@
     base = s.bases[3]
     k.gsrc[base : base + 2 * W, :] = mm_nn(k.dp[1:3].reshape(2 * W, L), k.normed[...]).astype(BF16)
     grads1(3)
-    grads5(1)
     k.ngg[piece(0, t), :] = rs_sum("zng", 0, k.ngp, k.ngr).astype(BF16)
     gather_start("zngg", 0, k.ngg)
     direct2(2)
@@ -945,25 +947,25 @@
     vb_copy = pltpu.make_async_copy(k.vb_sum, o_vb, k.stores.at[7])
     vb_copy.start()
 
-    for j in range(1, nt):
-        z_copy("zmask", j, k.mask.at[t], k.mask.at[t]).wait_send()
-        z_copy("zgate", j, k.gatec.at[t], k.gatec.at[t]).wait_send()
-        z_copy("zow", j, ow_part(t, core, upper), ow_part(t, core, upper)).wait_send()
-        at = ow_part(z_from(j), core, upper)
-        ow_copy("zowy", j, at, high_dev).wait_send()
-        ow_copy("zowr", j, at, sib).wait_send()
-        ow_copy("zowr", j, at, sib, 1).wait_send()
-        for h in range(2):
-            z_copy("zatt", j, att_half(t, h), att_half(t, h), h).wait_send()
-            z_copy("zda", j, k.dasrc.at[h, z_peer(j)], k.datok.at[h, t], h).wait_send()
-    rs_finish("zff", k.ffp, k.ffr)
+    z_all("zmask", k.mask.at[pl.ds(0, nt - 1)]).wait_send()
+    z_all("zgate", k.gatec.at[pl.ds(0, nt - 1)]).wait_send()
+    z_all("zow", ow_all).wait_send()
+    for name in ("zowy", "zowr", "zowq"):
+        ow_copy(name, ow_all, sib).wait_send()
+    for h in range(2):
+        z_all("zatt", k.att.at[pl.ds(0, nt - 1), :, half(h)], h).wait_send()
+        z_all("zda", k.datok.at[h, pl.ds(0, nt - 1)], h).wait_send()
+    rs_finish("zff", k.ffr)
     gather_finish("zblk", k.blow)
-    rs_finish("zn2", k.n2p, k.n2r)
+    rs_finish("zn2", k.n2r)
     gather_finish("zn2g", k.n2g)
-    rs_finish("zng", k.ngp, k.ngr)
+    rs_finish("zng", k.ngr)
     gather_finish("zngg", k.ngg)
-    for name, at in (("kv", kv_at), ("q", q_at), ("da0", da_at(0)), ("da1", da_at(1)), ("st", st_at)):
-        ag_finish(name, at)
+    ag_finish("kv", lambda count: k.kv.at[pl.ds(0, count)])
+    ag_finish("q", q_all)
+    ag_finish("da0", da_all(0))
+    ag_finish("da1", da_all(1))
+    ag_finish("st", st_all)
     swap_finish("cnt", every)
     swap_finish("ent", every)
     for i in range(4):
@@ -992,7 +994,7 @@
         stores.append(
             pltpu.make_async_copy(wide.at[rows], outs[name].at[pl.ds(start, size)], store_sem.at[i + 2])
         )
-    gate_rows = pl.ds(s.bases[2] + 2 * s.W, 32)
+    gate_rows = pl.ds(s.bases[1] + s.D, 32)
     gate_load = pltpu.make_async_copy(grads.at[gate_rows], low.at[gate_rows], load_sem.at[len(cuts) + 2])
     for copy in loads + [gate_load]:
         copy.start()

time: 116 us -> 114 us (0.983)
  Pallas kernels: 115 us -> 113 us
    pallas_call x1, Pallas kernels: 109 us -> 107 us  [local(): pl.pallas_call(partial(main_kernel, s, tuple(scratch)), out_shape=(jax.Sh...]
where the time goes in v6:
time: 114 us
  Pallas kernels  113 us (99%)
    pallas_call x1, Pallas kernels, local(): pl.pallas_call(partial(main_kernel, s, tuple(scratch)), out_shape=(jax.Sh...  107 us
    pallas_call x1, Pallas kernels, local(): pl.pallas_call(partial(last_kernel, s, cuts), out_shape=(jax.ShapeDtypeSt...  6.19 us

profile of v6, /device:TPU:1, one launch (start us, length us, event | category | flops | bytes accessed | tf_op | source)
XLA Modules:
  0.0 114.2 jit_solution(2882395421995859323)
XLA Ops:
  0.7 107.2 %block_step.1 = (bf16[256,768]{1,0:T(8,128)(2,1)}, f32[256,768]{1,0:T(8,128)}, bf16[2432,768]{1,0:T(8,128)(2,1)}, f32[8,128]{1,0:T(8,128)}, f32[32,768]{1,0:T(8,128)}) custom-call(f32[256,768]{1,0:T(8,128)} %refs_0_.1, s32[2048]{0:T(1024)} %refs_1_.1, s32[256]{0:T(256)} %refs_2_.1, bf16[16,768]{1,0:T(8,128)(2,1)} %refs_3_.1, f32[768]{0:T(1024)} %refs_4_.1, ...), custom_call_target="tpu_custom_call" | custom-call | flops 4278190080 | bytes 16777216 | tf_op jit(solution)/shard_map/block_step/pallas_call | solution.py:1052
  107.8 6.2 %write_out.1 = (f32[256,768]{1,0:T(8,128)}, f32[256,768]{1,0:T(8,128)}, f32[3,192,768]{2,1,0:T(8,128)}, f32[192,768]{1,0:T(8,128)}, f32[768,768]{1,0:T(8,128)}, ...) custom-call(bf16[256,768]{1,0:T(8,128)(2,1)} %get-tuple-element.31.b, ...), custom_call_target="tpu_custom_call" | custom-call | tf_op jit(solution)/shard_map/write_out/pallas_call | solution.py:1105

commit v7 on v6

--- a/solution.py
+++ b/solution.py
@@ -72,7 +72,7 @@
     s.sizes = (hidden, width + 128, local_width * 2, local_width * 2)
     s.bases = tuple(sum(s.sizes[:i]) for i in range(4))
     s.rows = sum(s.sizes)
-    s.tail = (leads + 4 + 15) // 16 * 16
+    s.packed = (4 * width // 128 + 15) // 16 * 16
     return s
 
 
@@ -134,16 +134,18 @@
         "ngp": v((L, D), BF16),
         "ngr": v((2, nt - 1, R, D), BF16),
         "ngg": v((L, D), BF16),
-        "vb": v((GROUP, s.tail, D), BF16),
+        "vb": v((GROUP, s.leads, D), BF16),
+        "vc": v((GROUP, s.packed, 128), BF16),
         "ent": v((nb, 8, 128), F32),
         "ent_sum": v((8, 128), F32),
-        "vb_sum": v((s.tail, D), F32),
+        "vb_sum": v((s.leads, D), F32),
+        "vc_sum": v((s.packed, 128), F32),
         "gsrc": v((s.rows, D), BF16),
         "gout": v((s.rows, D), BF16),
     }
     dma = pltpu.SemaphoreType.DMA
     out["loads"] = dma((15,))
-    out["stores"] = dma((8,))
+    out["stores"] = dma((9,))
     for name in ("zmask", "zgate", "zow", "zowy", "zowr", "zowq"):
         out[name + "_s"] = dma((1,))
         out[name + "_r"] = dma((1,))
@@ -151,18 +153,20 @@
         out[name + "_s"] = dma((2,))
         out[name + "_r"] = dma((2,))
     for name in ("kv", "q", "da0", "da1", "st"):
-        count = s.half if name == "kv" else 1
+        count = s.half if name == "kv" else 2
         out[name + "_s"] = dma((1,))
         out[name + "_r"] = dma((count,))
         out[name + "_rs"] = dma((1,))
         out[name + "_rr"] = dma((count,))
-    for name in ("cnt", "ent", "vb"):
+    for name in ("cnt", "ent", "vb", "vc"):
         out[name + "_s"] = dma((1,))
         out[name + "_r"] = dma((1,))
     if s.groups > 1:
-        out["vb2"] = v((s.groups, s.tail, D), BF16)
-        out["vb2_s"] = dma((1,))
-        out["vb2_r"] = dma((1,))
+        out["vb2"] = v((s.groups, s.leads, D), BF16)
+        out["vc2"] = v((s.groups, s.packed, 128), BF16)
+        for name in ("vb2", "vc2"):
+            out[name + "_s"] = dma((1,))
+            out[name + "_r"] = dma((1,))
     for i, rows in enumerate(s.sizes):
         hr = rows // 2
         qr = hr // 4
@@ -199,8 +203,9 @@
         o_grads,
         o_ent,
         o_vb,
-    ) = refs[:20]
-    k = SimpleNamespace(**dict(zip(names, refs[20:])))
+        o_vc,
+    ) = refs[:21]
+    k = SimpleNamespace(**dict(zip(names, refs[21:])))
     sem = vars(k)
     L, D, W, F, H, T, R, nb, nt = s.L, s.D, s.W, s.F, s.H, s.T, s.R, s.nb, s.nt
     b = lax.axis_index("blk")
@@ -237,7 +242,7 @@
         return remote(at(b), at(b), sem[name + "_s"].at[0], sem[name + "_r"].at[slot], (dst_band, t))
 
     def relay_copy(name, at, i, band):
-        slot = i if name == "kv" else 0
+        slot = i if name == "kv" or isinstance(i, int) else 1
         return remote(at(band), at(band), sem[name + "_rs"].at[0], sem[name + "_rr"].at[slot], (sib, t))
 
     def band_same(i):
@@ -272,8 +277,8 @@
             ag_relay(name, at, i)
 
     def ag_arrived(name, all_at):
-        ref = all_at(s.half)
-        remote(ref, ref, sem[name + "_rs"].at[0], sem[name + "_rr"].at[0], (sib, t)).wait_recv()
+        ref = all_at(s.half - 1)
+        remote(ref, ref, sem[name + "_rs"].at[0], sem[name + "_rr"].at[1], (sib, t)).wait_recv()
 
     def ag_finish(name, all_at):
         ref = all_at(s.half - 1)
@@ -842,6 +847,7 @@
 
     grads4(0)
     grads4(1)
+    ag_wait_relay("q", q_at, 0)
     ag_arrived("q", q_all)
 
     def backward_bands(bands):
@@ -861,12 +867,17 @@
             k.dk[head(h), :] = key_outs[h]
             k.dv[head(h), :] = value_outs[h]
 
-    for name, at, all_at in (
+    da_kinds = (
         ("da0", da_at(0), da_all(0)),
         ("da1", da_at(1), da_all(1)),
         ("st", st_at, st_all),
-    ):
+    )
+    for name, at, _ in da_kinds:
+        ag_wait_relay(name, at, 0)
+    backward_bands([b, sib])
+    for name, at, all_at in da_kinds:
         ag_pass_on(name, at, all_at)
+    for name, at, all_at in da_kinds:
         ag_arrived(name, all_at)
 
     def backward_loop(start, stop):
@@ -874,10 +885,10 @@
         def _(i):
             backward_bands([band_same(i), band_sib(i)])
 
-    backward_loop(0, s.half // 2)
+    backward_loop(1, s.half // 2)
     grads5(0)
-    backward_loop(s.half // 2, s.half)
-    grads5(1)
+    backward_loop(s.half // 2, s.half - s.half // 4)
+    backward_loop(s.half - s.half // 4, s.half)
     k.dp[0] = (k.dq[...] * SCALE).astype(BF16)
     k.dp[1] = k.dk[...].astype(BF16)
     k.dp[2] = k.dv[...].astype(BF16)
@@ -886,6 +897,7 @@
             k.dp[:, :, half(h)].reshape(3 * W, T), k.qkv[...].reshape(3 * W, D)
         ).astype(BF16)
         rs_start("zng", h, k.ngp, k.ngr)
+    grads5(1)
     base = s.bases[2]
     for h in range(2):
         gather_wait("zn2g", h, k.n2g)
@@ -901,14 +913,14 @@
     base = s.bases[3]
     k.gsrc[base : base + 2 * W, :] = mm_nn(k.dp[1:3].reshape(2 * W, L), k.normed[...]).astype(BF16)
     grads1(3)
+    grads6(0)
+    direct2(2)
     k.ngg[piece(0, t), :] = rs_sum("zng", 0, k.ngp, k.ngr).astype(BF16)
     gather_start("zngg", 0, k.ngg)
-    direct2(2)
     direct2(3)
-    grads6(0)
+    grads6(1)
     k.ngg[piece(1, t), :] = rs_sum("zng", 1, k.ngp, k.ngr).astype(BF16)
     gather_start("zngg", 1, k.ngg)
-    grads6(1)
     direct3(2)
     direct3(3)
     grads7(0)
@@ -931,21 +943,25 @@
     hidden_copy.start()
     coarse = hidden_grad.astype(BF16)
     fine = (hidden_grad - coarse.astype(F32)).astype(BF16)
-    tail = [
-        mm_nn(lead_hot, coarse) + mm_nn(lead_hot, fine),
-        gain1_grad,
-        bias1_grad,
-        gain2_grad,
-        bias2_grad,
-        jnp.zeros((s.tail - s.leads - 4, D), F32),
+    k.vb[near[1]] = (mm_nn(lead_hot, coarse) + mm_nn(lead_hot, fine)).astype(BF16)
+    swap_start("vb", near)
+    lanes = D // 128
+    packed = [
+        x[:, 128 * i : 128 * (i + 1)]
+        for x in (gain1_grad, bias1_grad, gain2_grad, bias2_grad)
+        for i in range(lanes)
     ]
-    k.vb[near[1]] = jnp.concatenate(tail, axis=0).astype(BF16)
-    swap_start("vb", near)
+    packed.append(jnp.zeros((s.packed - 4 * lanes, 128), F32))
+    k.vc[near[1]] = jnp.concatenate(packed, axis=0).astype(BF16)
+    swap_start("vc", near)
     grads7(2)
     grads7(3)
     k.vb_sum[...] = swap_sum("vb")
+    k.vc_sum[...] = swap_sum("vc")
     vb_copy = pltpu.make_async_copy(k.vb_sum, o_vb, k.stores.at[7])
+    vc_copy = pltpu.make_async_copy(k.vc_sum, o_vc, k.stores.at[8])
     vb_copy.start()
+    vc_copy.start()
 
     z_all("zmask", k.mask.at[pl.ds(0, nt - 1)]).wait_send()
     z_all("zgate", k.gatec.at[pl.ds(0, nt - 1)]).wait_send()
@@ -970,12 +986,12 @@
     swap_finish("ent", every)
     for i in range(4):
         grads_store(i).wait()
-    for copy in (block_copy, hidden_copy, ent_copy, vb_copy):
+    for copy in (block_copy, hidden_copy, ent_copy, vb_copy, vc_copy):
         copy.wait()
 
 
 def last_kernel(
-    s, cuts, block, hidden, grads, ent, vb,
+    s, cuts, block, hidden, grads, ent, vb, vc,
     o_block, o_hidden, o_qkv, o_out, o_up, o_down, o_pen, o_lead, o_g1, o_b1, o_g2, o_b2, o_gate,
     low, wide, low_block, wide_block, keep, load_sem, store_sem,
 ):
@@ -1013,12 +1029,12 @@
     for e in range(3):
         o_gate[e] = small[8 * e : 8 * e + 4]
     o_pen[...] = ent[0:1, 0:1]
-    tail = vb[...]
-    o_lead[...] = tail[0 : s.leads]
-    o_g1[...] = tail[s.leads].reshape(s.D)
-    o_b1[...] = tail[s.leads + 1].reshape(s.D)
-    o_g2[...] = tail[s.leads + 2].reshape(s.D)
-    o_b2[...] = tail[s.leads + 3].reshape(s.D)
+    o_lead[...] = vb[...]
+    lanes = s.D // 128
+    for i, out in enumerate((o_g1, o_b1, o_g2, o_b2)):
+        for j in range(lanes):
+            row = i * lanes + j
+            out[128 * j : 128 * (j + 1)] = vc[row : row + 1, :].reshape(128)
     for copy in stores:
         copy.wait()
 
@@ -1049,17 +1065,18 @@
     s = dims_of(nb, nt, L, D, W, F, leads, L * nb * pixel_mask.shape[0] * nt)
     scratch = scratch_of(s)
     vm = pl.BlockSpec(memory_space=pltpu.VMEM)
-    block, hidden, grads, ent, vb = pl.pallas_call(
+    block, hidden, grads, ent, vb, vc = pl.pallas_call(
         partial(main_kernel, s, tuple(scratch)),
         out_shape=(
             jax.ShapeDtypeStruct((L, D), BF16),
             jax.ShapeDtypeStruct((L, D), F32),
             jax.ShapeDtypeStruct((s.rows, D), BF16),
             jax.ShapeDtypeStruct((8, 128), F32),
-            jax.ShapeDtypeStruct((s.tail, D), F32),
+            jax.ShapeDtypeStruct((leads, D), F32),
+            jax.ShapeDtypeStruct((s.packed, 128), F32),
         ),
         in_specs=[pl.BlockSpec(memory_space=pltpu.HBM)] * 15,
-        out_specs=(pl.BlockSpec(memory_space=pl.ANY),) * 5,
+        out_specs=(pl.BlockSpec(memory_space=pl.ANY),) * 6,
         scratch_shapes=list(scratch.values()),
         compiler_params=pltpu.CompilerParams(
             collective_id=0,
@@ -1119,7 +1136,7 @@
             vec,
             jax.ShapeDtypeStruct(gate_head.shape, F32),
         ),
-        in_specs=[hbm] * 3 + [vm] * 2,
+        in_specs=[hbm] * 3 + [vm] * 3,
         out_specs=(hbm,) * 6 + (vm,) * 7,
         scratch_shapes=[
             pltpu.VMEM((s.rows, D), BF16),
@@ -1132,7 +1149,7 @@
         ],
         compiler_params=pltpu.CompilerParams(vmem_limit_bytes=VMEM_LIMIT),
         name="write_out",
-    )(block, hidden, grads, ent, vb)
+    )(block, hidden, grads, ent, vb, vc)
     return (
         wide,
         pen.reshape(()),

time: 114 us -> 110 us (0.965)
  Pallas kernels: 113 us -> 108 us
    pallas_call x1, Pallas kernels: 107 us -> 102 us  [local(): pl.pallas_call(partial(main_kernel, s, tuple(scratch)), out_shape=(jax.Sh...]
where the time goes in v7:
time: 110 us; the launch traced here: 109 us
  Pallas kernels  108 us (98%)
    pallas_call x1, Pallas kernels, local(): pl.pallas_call(partial(main_kernel, s, tuple(scratch)), out_shape=(jax.Sh...  102 us
    pallas_call x1, Pallas kernels, local(): pl.pallas_call(partial(last_kernel, s, cuts), out_shape=(jax.ShapeDtypeSt...  6.1 us

profile of v7, /device:TPU:1, one launch (start us, length us, event | category | flops | bytes accessed | tf_op | source)
XLA Modules:
  0.0 109.2 jit_solution(5726200725432224229)
XLA Ops:
  0.7 102.3 %block_step.1 = (bf16[256,768]{1,0:T(8,128)(2,1)}, f32[256,768]{1,0:T(8,128)}, bf16[2432,768]{1,0:T(8,128)(2,1)}, f32[8,128]{1,0:T(8,128)}, f32[16,768]{1,0:T(8,128)}, /*index=5*/f32[32,128]{1,0:T(8,128)}) custom-call(f32[256,768]{1,0:T(8,128)} %refs_0_.1, s32[2048]{0:T(1024)} %refs_1_.1, s32[256]{0:T(256)} %refs_2_.1, bf16[16,768]{1,0:T(8,128)(2,1)} %refs_3_.1, ...), custom_call_target="tpu_custom_call" | custom-call | flops 4278190080 | bytes 16777216 | tf_op jit(solution)/shard_map/block_step/pallas_call | solution.py:1068
  102.9 6.1 %write_out.1 = (f32[256,768]{1,0:T(8,128)}, f32[256,768]{1,0:T(8,128)}, f32[3,192,768]{2,1,0:T(8,128)}, f32[192,768]{1,0:T(8,128)}, f32[768,768]{1,0:T(8,128)}, ...) custom-call(bf16[256,768]{1,0:T(8,128)(2,1)} %get-tuple-element.32.b, ...), custom_call_target="tpu_custom_call" | custom-call | tf_op jit(solution)/shard_map/write_out/pallas_call | solution.py:1122

commit v8 on v7

--- a/solution.py
+++ b/solution.py
@@ -652,13 +652,14 @@
         ag_wait("kv", kv_at, i)
         ag_relay("kv", kv_at, i)
 
+    ow_pass_on()
+
     @pl.loop(0, s.half // 2 - 1)
     def _(i):
         forward_bands([band_same(2 * i + 1), band_same(2 * i + 2)])
 
     ag_wait_relay("kv", kv_at, 1)
     forward_bands([band_same(s.half - 1), band_sib(1)])
-    ow_pass_on()
 
     @pl.loop(1, s.half // 2)
     def _(i):
@@ -761,13 +762,14 @@
         out_grad = k.cot[rows, :] + mm_tn(k.lg[:, half(h)], k.gate[...])
         k.cot[rows, :] = out_grad
         k.oglow[rows, :] = out_grad.astype(BF16)
+        if h == 1:
+            k.gsrc[0:F, :] = mm_tn(k.actlow[...], k.oglow[...]).astype(BF16)
+            grads1(0)
         k.ug[rows, :] = (mm_nt(k.oglow[rows, :], k.down[...]) * k.upw[rows, :]).astype(BF16)
         k.n2p[rows, :] = mm_nt(k.ug[rows, :], k.up[...]).astype(BF16)
         rs_start("zn2", h, k.n2p, k.n2r)
     block_copy = pltpu.make_async_copy(k.blow, o_block, k.stores.at[4])
     block_copy.start()
-    k.gsrc[0:F, :] = mm_tn(k.actlow[...], k.oglow[...]).astype(BF16)
-    grads1(0)
     k.gsrc[F : F + D, :] = mm_tn(k.n2low[...], k.ug[...]).astype(BF16)
     own_lg = k.lg[pl.ds(pl.multiple_of(t * 32, 32), 32), :]
     base = s.bases[1] + D
@@ -872,14 +874,14 @@
         ("da1", da_at(1), da_all(1)),
         ("st", st_at, st_all),
     )
-    for name, at, _ in da_kinds:
-        ag_wait_relay(name, at, 0)
-    backward_bands([b, sib])
     for name, at, all_at in da_kinds:
         ag_pass_on(name, at, all_at)
     for name, at, all_at in da_kinds:
         ag_arrived(name, all_at)
 
+    for name, at, _ in da_kinds:
+        ag_wait_relay(name, at, 0)
+    backward_bands([b, sib])
     def backward_loop(start, stop):
         @pl.loop(start, stop)
         def _(i):
@@ -929,22 +931,29 @@
     k.ent_sum[...] = jnp.sum(k.ent[...], axis=0)
     ent_copy = pltpu.make_async_copy(k.ent_sum, o_ent, k.stores.at[6])
     ent_copy.start()
-    gather_wait("zngg", 0, k.ngg)
-    direct6(2)
-    direct6(3)
-    gather_wait("zngg", 1, k.ngg)
-    n1_grad = k.ngg[...].astype(F32)
-    unit1 = k.u1[...]
-    gain1_grad = jnp.sum(n1_grad * unit1, axis=0, keepdims=True)
-    bias1_grad = jnp.sum(n1_grad, axis=0, keepdims=True)
-    hidden_grad = k.cot[...] + norm_backward(n1_grad, unit1, k.r1[...], row_of(k.gain1))
-    k.patches[...] = hidden_grad
+    gain1_grad = jnp.zeros((1, D), F32)
+    bias1_grad = jnp.zeros((1, D), F32)
+    lead_grad = jnp.zeros((s.leads, D), F32)
+    for h in range(2):
+        rows = half(h)
+        gather_wait("zngg", h, k.ngg)
+        n1_grad = k.ngg[rows, :].astype(F32)
+        unit1 = k.u1[rows, :]
+        gain1_grad += jnp.sum(n1_grad * unit1, axis=0, keepdims=True)
+        bias1_grad += jnp.sum(n1_grad, axis=0, keepdims=True)
+        hidden_grad = k.cot[rows, :] + norm_backward(n1_grad, unit1, k.r1[rows, :], row_of(k.gain1))
+        k.patches[rows, :] = hidden_grad
+        coarse = hidden_grad.astype(BF16)
+        fine = (hidden_grad - coarse.astype(F32)).astype(BF16)
+        hot = lead_hot[:, h * T : (h + 1) * T]
+        lead_grad += mm_nn(hot, coarse) + mm_nn(hot, fine)
+        if h == 0:
+            direct6(2)
+            direct6(3)
+    k.vb[near[1]] = lead_grad.astype(BF16)
+    swap_start("vb", near)
     hidden_copy = pltpu.make_async_copy(k.patches, o_hidden, k.stores.at[5])
     hidden_copy.start()
-    coarse = hidden_grad.astype(BF16)
-    fine = (hidden_grad - coarse.astype(F32)).astype(BF16)
-    k.vb[near[1]] = (mm_nn(lead_hot, coarse) + mm_nn(lead_hot, fine)).astype(BF16)
-    swap_start("vb", near)
     lanes = D // 128
     packed = [
         x[:, 128 * i : 128 * (i + 1)]

time: 110 us -> 109 us (level)
  no operation moved by 1% of the time
where the time goes in v8:
time: 109 us; the launch traced here: 108 us
  Pallas kernels  107 us (98%)
    pallas_call x1, Pallas kernels, local(): pl.pallas_call(partial(main_kernel, s, tuple(scratch)), out_shape=(jax.Sh...  101 us
    pallas_call x1, Pallas kernels, local(): pl.pallas_call(partial(last_kernel, s, cuts), out_shape=(jax.ShapeDtypeSt...  6.1 us

profile of v8, /device:TPU:1, one launch (start us, length us, event | category | flops | bytes accessed | tf_op | source)
XLA Modules:
  0.0 108.1 jit_solution(3216701280173194126)
XLA Ops:
  0.7 101.2 %block_step.1 = (bf16[256,768]{1,0:T(8,128)(2,1)}, f32[256,768]{1,0:T(8,128)}, bf16[2432,768]{1,0:T(8,128)(2,1)}, f32[8,128]{1,0:T(8,128)}, f32[16,768]{1,0:T(8,128)}, /*index=5*/f32[32,128]{1,0:T(8,128)}) custom-call(f32[256,768]{1,0:T(8,128)} %refs_0_.1, s32[2048]{0:T(1024)} %refs_1_.1, s32[256]{0:T(256)} %refs_2_.1, bf16[16,768]{1,0:T(8,128)(2,1)} %refs_3_.1, ...), custom_call_target="tpu_custom_call" | custom-call | flops 4278190080 | bytes 16777216 | tf_op jit(solution)/shard_map/block_step/pallas_call | solution.py:1077
  101.8 6.1 %write_out.1 = (f32[256,768]{1,0:T(8,128)}, f32[256,768]{1,0:T(8,128)}, f32[3,192,768]{2,1,0:T(8,128)}, f32[192,768]{1,0:T(8,128)}, f32[768,768]{1,0:T(8,128)}, ...) custom-call(bf16[256,768]{1,0:T(8,128)(2,1)} %get-tuple-element.32.b, ...), custom_call_target="tpu_custom_call" | custom-call | tf_op jit(solution)/shard_map/write_out/pallas_call | solution.py:1131

commit v9 on v8

--- a/solution.py
+++ b/solution.py
@@ -1125,8 +1125,8 @@
         ("v", s.bases[3] + W, W),
     )
     for name, row, size in places:
-        for start in range(0, size, 256):
-            cuts.append((row + start, name, start, min(256, size - start)))
+        for start in range(0, size, 384):
+            cuts.append((row + start, name, start, min(384, size - start)))
     hbm = pl.BlockSpec(memory_space=pl.ANY)
     wide, high, qkv_grad, out_grad, up_grad, down_grad, pen, lead, g1, b1, g2, b2, gates = pl.pallas_call(
         partial(last_kernel, s, cuts),

time: 109 us -> 109 us (level)
  no operation moved by 1% of the time
where the time goes in v9:
time: 109 us; the launch traced here: 108 us
  Pallas kernels  107 us (98%)
    pallas_call x1, Pallas kernels, local(): pl.pallas_call(partial(main_kernel, s, tuple(scratch)), out_shape=(jax.Sh...  101 us
    pallas_call x1, Pallas kernels, local(): pl.pallas_call(partial(last_kernel, s, cuts), out_shape=(jax.ShapeDtypeSt...  6.07 us

profile of v9, /device:TPU:1, one launch (start us, length us, event | category | flops | bytes accessed | tf_op | source)
XLA Modules:
  0.0 108.1 jit_solution(13929447628930737361)
XLA Ops:
  0.7 101.2 %block_step.1 = (bf16[256,768]{1,0:T(8,128)(2,1)}, f32[256,768]{1,0:T(8,128)}, bf16[2432,768]{1,0:T(8,128)(2,1)}, f32[8,128]{1,0:T(8,128)}, f32[16,768]{1,0:T(8,128)}, /*index=5*/f32[32,128]{1,0:T(8,128)}) custom-call(f32[256,768]{1,0:T(8,128)} %refs_0_.1, s32[2048]{0:T(1024)} %refs_1_.1, s32[256]{0:T(256)} %refs_2_.1, bf16[16,768]{1,0:T(8,128)(2,1)} %refs_3_.1, ...), custom_call_target="tpu_custom_call" | custom-call | flops 4278190080 | bytes 16777216 | tf_op jit(solution)/shard_map/block_step/pallas_call | solution.py:1077
  101.8 6.1 %write_out.1 = (f32[256,768]{1,0:T(8,128)}, f32[256,768]{1,0:T(8,128)}, f32[3,192,768]{2,1,0:T(8,128)}, f32[192,768]{1,0:T(8,128)}, f32[768,768]{1,0:T(8,128)}, ...) custom-call(bf16[256,768]{1,0:T(8,128)(2,1)} %get-tuple-element.32.b, ...), custom_call_target="tpu_custom_call" | custom-call | tf_op jit(solution)/shard_map/write_out/pallas_call | solution.py:1131
